TPU v7x, 256 devices: a whole 4x4x8 slice. The times are simulated.
256 devices in a mesh: group: 2 (over core), row: 4 (over z_hi), col: 32 (over z_lo, y, x).
Axes of the slice: x: 4, y: 4, z: 8 (z_hi: 4, z_lo: 2; z = z_hi * 2 + z_lo), core: 2. Of those that a mesh axis runs over, the one named last changes fastest.
Arguments:
- teacher_tokens: bfloat16 [2048, 4, 8, 1536], P(('group', 'col'), None, None, 'row'), may hold values from -6 to 6
- view_index: int32 [2048, 4], P(('group', 'col')), may hold values from 0 to 31
- aug_embed: bfloat16 [32, 1536], P(None, 'row'), may hold values from -3 to 3
- norm_gain: bfloat16 [1536], replicated, may hold values from 0.099609375 to 1.8984375
- layer_scale: bfloat16 [1536], P('row'), may hold values from 0.29882812 to 1.5
- gate_weight: bfloat16 [1536, 4096], P('col', 'row'), may hold values from -0.15625 to 0.15625
- up_weight: bfloat16 [1536, 4096], P('col', 'row'), may hold values from -0.15625 to 0.15625
- down_weight: bfloat16 [4096, 1536], P(('row', 'col')), may hold values from -0.09375 to 0.09375
- student_tokens: bfloat16 [2048, 6144], P(('group', 'col'), 'row'), may hold values from -6 to 6
- head_weight: bfloat16 [768, 1536], P(None, 'row'), may hold values from -0.21875 to 0.21875
- owner: int32 [2048, 1], P(('group', 'col')), may hold values from 0 to 31; in each aligned block of 32 rows (0 to 31, 32 to 63, ...) at most 2 rows name the same one
Outputs:
- head_grad: float32 [768, 1536], P(None, 'row')
- owner_loss: float32 [64], P(('group', 'col'))
Inputs may be any that keep to these rules, and one draw needn't show every extreme that they name: Among the 32 images of one device (aligned blocks) no owner is named more than 2 times, a bound that some block reaches.
All inputs are finite; a program needn't handle non-finite values.
Results may differ from a plain program's by a relative error of at most 0.012.
Values may be sent and summed in bfloat16 or wider, within the bound.
No kernel may reach another device: no remote copies, remote signals or barrier semaphores. Data moves between devices by JAX's collectives and lax.ppermute only.
A program may use at most 64 MiB of HBM per device.

v0:
```python
import jax
import jax.numpy as jnp
from jax import lax
from jax.sharding import PartitionSpec as P

D = 1536
SW = 768


def shards(
    teacher_tokens,
    view_index,
    aug_embed,
    norm_gain,
    layer_scale,
    gate_weight,
    up_weight,
    down_weight,
    student_tokens,
    head_weight,
    owner,
):
    images, views, patches, feature_part = teacher_tokens.shape
    kinds = aug_embed.shape[0]
    columns = lax.axis_size("col")
    groups = lax.axis_size("group")
    most = max(2, 2 * ((images + columns - 1) // columns))
    total_images = images * columns * groups
    kind_table = (
        view_index.reshape(-1)[:, None] == jnp.arange(kinds, dtype=jnp.int32)[None, :]
    ).astype(jnp.bfloat16)
    embedded = jnp.dot(kind_table, aug_embed, preferred_element_type=jnp.float32).reshape(
        images, views, 1, feature_part
    )
    shifted = (teacher_tokens.astype(jnp.float32) + embedded).astype(jnp.bfloat16)
    whole = lax.all_gather(shifted, "row", axis=3, tiled=True)
    flat = whole.reshape(-1, D).astype(jnp.float32)
    center = flat - jnp.mean(flat, axis=1, keepdims=True)
    spread = jnp.mean(center * center, axis=1, keepdims=True)
    normed = (center * lax.rsqrt(spread + 1e-06) * norm_gain.astype(jnp.float32)).astype(
        jnp.bfloat16
    )
    block = normed
    gate = jnp.dot(
        block,
        lax.all_gather(gate_weight, "col", axis=0, tiled=True),
        preferred_element_type=jnp.float32,
    )
    upward = jnp.dot(
        block,
        lax.all_gather(up_weight, "col", axis=0, tiled=True),
        preferred_element_type=jnp.float32,
    )
    hidden = (jax.nn.silu(gate) * upward).astype(jnp.bfloat16)
    block = hidden
    branch = jnp.dot(
        block,
        lax.all_gather(down_weight, "col", axis=0, tiled=True),
        preferred_element_type=jnp.float32,
    )
    branch = branch.reshape(images, views, patches, D)
    summed = lax.psum_scatter(branch, "row", scatter_dimension=3, tiled=True)
    averaged = jnp.mean(summed, axis=1)
    residual = jnp.mean(shifted.astype(jnp.float32), axis=1)
    target = (residual + layer_scale.astype(jnp.float32) * averaged).astype(jnp.bfloat16)
    owners_local = owner[:, 0]
    owner_table = (owners_local[:, None] == jnp.arange(columns, dtype=jnp.int32)[None, :]).astype(
        jnp.int32
    )
    earlier = jnp.cumsum(owner_table, axis=0) - owner_table
    ranking = jnp.sum(earlier * owner_table, axis=1)
    placed = (owner_table.T[:, None, :] == 1) & (
        ranking[None, None, :] == jnp.arange(most, dtype=jnp.int32)[None, :, None]
    )
    placed = placed.astype(jnp.bfloat16)
    packets = jnp.einsum(
        "oki,ipd->okpd", placed, target, preferred_element_type=jnp.float32
    ).astype(jnp.bfloat16)
    lessons = jnp.einsum(
        "oki,if->okf", placed, student_tokens, preferred_element_type=jnp.float32
    ).astype(jnp.bfloat16)
    filled = jnp.sum(placed.astype(jnp.float32), axis=2).astype(jnp.bfloat16)
    got_targets, got_lessons, got_filled = (
        lax.all_to_all(packets, "col", split_axis=0, concat_axis=0, tiled=True),
        lax.all_to_all(lessons, "col", split_axis=0, concat_axis=0, tiled=True),
        lax.all_to_all(filled, "col", split_axis=0, concat_axis=0, tiled=True),
    )
    lessons_full = lax.all_gather(got_lessons, "row", axis=2, tiled=True)
    pupil_rows = lessons_full.reshape(-1, SW)
    target_rows = got_targets.reshape(-1, feature_part).astype(jnp.float32)
    row_mask = jnp.repeat(got_filled.reshape(-1).astype(jnp.float32), patches)[:, None]
    head = jnp.dot(pupil_rows, head_weight, preferred_element_type=jnp.float32)
    sum_head, sum_square = lax.psum((jnp.sum(head, axis=1), jnp.sum(head * head, axis=1)), "row")
    middle = (sum_head / D)[:, None]
    spread_head = (sum_square / D)[:, None] - middle * middle
    scaler = lax.rsqrt(spread_head + 1e-05)
    pred = (head - middle) * scaler
    diff = (pred - target_rows) * row_mask
    loss_part = jnp.sum(diff * diff) / (patches * D)
    dpred = 2.0 * diff / total_images
    sum_first, sum_second, loss_total = lax.psum(
        (jnp.sum(dpred, axis=1), jnp.sum(dpred * pred, axis=1), loss_part), "row"
    )
    dz_value = (
        scaler * (dpred - (sum_first / D)[:, None] - pred * (sum_second / D)[:, None])
    ).astype(jnp.bfloat16)
    grad_part = lax.dot_general(
        pupil_rows, dz_value, (((0,), (0,)), ((), ())), preferred_element_type=jnp.float32
    )
    head_grad = lax.psum(grad_part, ("group", "col"))
    return (head_grad, jnp.reshape(loss_total, (1,)))


def solution(mesh):
    return jax.shard_map(
        shards,
        mesh=mesh,
        in_specs=(
            P(("group", "col"), None, None, "row"),
            P(("group", "col"), None),
            P(None, "row"),
            P(),
            P("row"),
            P("col", "row"),
            P("col", "row"),
            P(("row", "col"), None),
            P(("group", "col"), "row"),
            P(None, "row"),
            P(("group", "col"), None),
        ),
        out_specs=(P(None, "row"), P(("group", "col"))),
        check_vma=False,
    )
```

profile of v0, /device:TPU:1, one launch (start us, length us, event | category | flops | bytes accessed | tf_op | source)
XLA Modules:
  0.0 1341.4 jit_solution(14941791488041793263)
XLA Ops:
  9.2 2.3 convert_reduce_fusion.1
  13.6 65.0 %all-gather.5.cloned.1.call-done = bf16[32,4,8,1536]{3,2,1,0:T(8,128)(2,1)} async-done(((bf16[32,4,8,384]{3,2,1,0:T(8,128)(2,1)}), bf16[32,4,8,1536]{3,2,1,0:T(8,128)(2,1)}) %all-gather.5.cloned.1.call-update) | async-done | bytes 3145744 | tf_op jit(solution)/shard_map/all_gather | solution.py:36
  78.6 2.4 convert_reduce_fusion
  81.1 2.9 multiply_reduce_fusion
  84.2 4.5 fusion.2
  88.7 134.0 %all-gather.7.cloned.1.call-done = bf16[1536,1024]{1,0:T(8,128)(2,1)} async-done(((bf16[48,1024]{1,0:T(8,128)(2,1)}), bf16[1536,1024]{1,0:T(8,128)(2,1)}) %all-gather.7.cloned.1.call-update) | async-done | bytes 3145744 | tf_op jit(solution)/shard_map/all_gather | solution.py:46
  222.8 8.3 fusion.24
  231.0 151.7 %all-gather.11.cloned.1.call-done = bf16[1024,1536]{1,0:T(8,128)(2,1)} async-done(((bf16[32,1536]{1,0:T(8,128)(2,1)}), bf16[1024,1536]{1,0:T(8,128)(2,1)}) %all-gather.11.cloned.1.call-update) | async-done | bytes 3145744 | tf_op jit(solution)/shard_map/all_gather | solution.py:58
  382.7 159.8 %all-gather.9.cloned.1.call-done = bf16[1536,1024]{1,0:T(8,128)(2,1)} async-done(((bf16[48,1024]{1,0:T(8,128)(2,1)}), bf16[1536,1024]{1,0:T(8,128)(2,1)}) %all-gather.9.cloned.1.call-update) | async-done | bytes 3145744 | tf_op jit(solution)/shard_map/all_gather | solution.py:51
  542.5 14.3 %fusion.3 = f32[1024,1536]{1,0:T(8,128)} fusion(bf16[1024,1536]{1,0:T(8,128)(2,1)} %all-gather.11.cloned.1.call-done, f32[1024,1024]{1,0:T(8,128)} %fusion.24, bf16[1024,1536]{1,0:T(8,128)(2,1)} %fusion.2, bf16[1536,1024]{1,0:T(8,128)(2,1)} %all-gather.9.cloned.1.call-done), kind=kOutput, calls=%fused_computation.11 | convolution fusion | flops 6448742400 | bytes 19922944 | tf_op jit(solution)/shard_map/dot_general | solution.py:56
  558.6 6.8 all-to-all-start.2
  566.5 6.0 all-to-all-done.2
  572.4 3.9 all-to-all-start
  576.7 121.9 %reduce-scatter.2.cloned.1.call-done = f32[32,4,8,384]{3,2,1,0:T(8,128)} async-done(((f32[32,4,8,1536]{3,2,1,0:T(8,128)}), f32[32,4,8,384]{3,2,1,0:T(8,128)}) %reduce-scatter.2.cloned.1.call-update) | async-done | bytes 1572880 | tf_op jit(solution)/shard_map/reduce_scatter | solution.py:62
  698.5 1.6 reduce_sum.108
  701.3 7.2 all-to-all-start.1
  708.5 22.5 %all_gather.15 = bf16[32,2,6144]{2,1,0:T(2,128)(2,1)S(1)} all-gather(bf16[32,2,1536]{2,1,0:T(2,128)(2,1)S(1)} %all-to-all-done), channel_id=1, replica_groups=mesh['group'=2,'row'=4,'col'=32] {'row'}, dimensions={2}, use_global_device_ids=true | all-gather | bytes 983040 | tf_op jit(solution)/shard_map/all_gather | solution.py:88
  732.1 8.1 all-reduce.1
  740.2 1.0 bitcast_convert_fusion
  741.2 1.4 copy.25
  744.1 9.3 all-reduce
  753.3 1.7 fusion.4
  755.1 577.2 %all-reduce.4.cloned.1.call-done = f32[768,384]{1,0:T(8,128)} async-done(((f32[768,384]{1,0:T(8,128)}), f32[768,384]{1,0:T(8,128)}) %all-reduce.4.cloned.1.call-update) | async-done | bytes 1179664 | tf_op jit(solution)/shard_map/psum | solution.py:110
  1332.2 2.4 copy.33
  (54 shorter events, 10.6 us)
Async XLA Ops:
  7.2 724.4 %copy-start = (bf16[768,384]{1,0:T(8,128)(2,1)S(1)}, bf16[768,384]{1,0:T(8,128)(2,1)}, u32[]{:S(2)}) copy-start(bf16[768,384]{1,0:T(8,128)(2,1)} %param.20) | copy-start | bytes 1769476
  7.2 6.4 copy-start.3
  7.2 71.4 %all-gather.5.cloned.1.call-start = ((), (), s32[]{:S(2)}) async-start(), calls=%async_computation.4 | async-start | bytes 3932160 | tf_op jit(solution)/shard_map/all_gather | solution.py:36
  11.5 211.3 %all-gather.7.cloned.1.call-start = ((), (), s32[]{:S(2)}) async-start(), calls=%async_computation.5 | async-start | bytes 3244032 | tf_op jit(solution)/shard_map/all_gather | solution.py:46
  12.2 370.5 %all-gather.11.cloned.1.call-start = ((), (), s32[]{:S(2)}) async-start(), calls=%async_computation.7 | async-start | bytes 3244032 | tf_op jit(solution)/shard_map/all_gather | solution.py:58
  12.9 529.5 %all-gather.9.cloned.1.call-start = ((), (), s32[]{:S(2)}) async-start(), calls=%async_computation.6 | async-start | bytes 3244032 | tf_op jit(solution)/shard_map/all_gather | solution.py:51
  13.5 685.0 %reduce-scatter.2.cloned.1.call-start = ((), (), s32[]{:S(2)}) async-start(), calls=%async_computation.8 | async-start | bytes 7864320 | tf_op jit(solution)/shard_map/reduce_scatter | solution.py:62
  556.8 0.7 copy-start.2
  556.8 8.6 copy-start.1
  556.8 8.8 copy-start.4
  558.6 13.9 %all-to-all-start.2 = ((bf16[32,1,2]{2,1,0:T(2,128)(2,1)}), bf16[32,1,2]{2,1,0:T(2,128)(2,1)S(1)}, u32[]{:S(2)}, u32[]{:S(2)}) async-start(bf16[32,1,2]{2,1,0:T(2,128)(2,1)} %copy.26), calls=%async_computation.3 | async-start | bytes 32768 | tf_op jit(solution)/shard_map/all_to_all | solution.py:86
  572.4 128.8 %all-to-all-start = ((bf16[32,2,1536]{2,1,0:T(2,128)(2,1)}), bf16[32,2,1536]{2,1,0:T(2,128)(2,1)S(1)}, u32[]{:S(2)}, u32[]{:S(2)}) async-start(bf16[32,2,1536]{2,1,0:T(2,128)(2,1)} %copy.21), calls=%async_computation | async-start | bytes 393216 | tf_op jit(solution)/shard_map/all_to_all | solution.py:85
  701.3 38.9 %all-to-all-start.1 = ((bf16[32,2,8,384]{3,2,1,0:T(8,128)(2,1)}), bf16[32,2,8,384]{3,2,1,0:T(8,128)(2,1)S(1)}, u32[]{:S(2)}, u32[]{:S(2)}) async-start(bf16[32,2,8,384]{3,2,1,0:T(8,128)(2,1)} %copy.24), calls=%async_computation.2 | async-start | bytes 786432 | tf_op jit(solution)/shard_map/all_to_all | solution.py:84
  708.5 623.7 %all-reduce.4.cloned.1.call-start = ((), (), s32[]{:S(2)}) async-start(), calls=%async_computation.9 | async-start | bytes 2359296 | tf_op jit(solution)/shard_map/psum | solution.py:110
Sparse Core Ops, SparseCore 0:
  11.6 66.9 all-gather.4
  80.4 142.3 all-gather.6
  224.5 158.1 all-gather.10
  384.3 158.1 all-gather.8
  556.9 141.5 reduce-scatter.1
  755.2 576.9 all-reduce.3
where the time goes:
time: 1360 us; the launch traced here: 1340 us
  waiting for transfers between devices  1220 us (90%)
  blocking collectives  39.8 us (3%)
  matrix products  26.2 us (2%)
  starting transfers between devices  18.1 us (1%)
  other arithmetic  16.1 us (1%)
  between operations  15 us (1%)
    psum x1, waiting for transfers between devices, shards(): head_grad = lax.psum(grad_part, ('group', 'col'))  577 us
    all_gather x1, waiting for transfers between devices, shards(): lax.all_gather(up_weight, 'col', axis=0, tiled=True)  160 us
    all_gather x1, waiting for transfers between devices, shards(): lax.all_gather(down_weight, 'col', axis=0, tiled=True)  152 us
    all_gather x1, waiting for transfers between devices, shards(): lax.all_gather(gate_weight, 'col', axis=0, tiled=True)  134 us
    reduce_scatter x1, waiting for transfers between devices, shards(): summed = lax.psum_scatter(branch, 'row', scatter_dimension=3, tiled=True)  122 us
    all_gather x1, waiting for transfers between devices, shards(): whole = lax.all_gather(shifted, 'row', axis=3, tiled=True)  65 us
  transfers between devices with their start and end apart: 9, of which 7 were waited for; matrix products, arithmetic and copies ran while one was open for 2% of the time, Pallas kernels for 0%

commit v1 on v0

v1 whole, which is shorter than its diff:
```python
import jax
import jax.numpy as jnp
from jax import lax
from jax.sharding import Mesh, PartitionSpec as P

D = 1536
SW = 768
ROWS = 4
YX = ("y", "x")
COL = ("zl", "y", "x")
EVERY = ("group", "zl", "y", "x")
IMAGES = 2048


def shift(value, axis, size, by):
    return lax.ppermute(value, axis, [(i, (i + by) % size) for i in range(size)])


def middle(pieces, gate_halves, up_halves, down_halves, norm_gain, row, group):
    tokens = jnp.concatenate(pieces, axis=1).astype(jnp.float32)
    center = tokens - jnp.mean(tokens, axis=1, keepdims=True)
    spread = jnp.mean(center * center, axis=1, keepdims=True)
    normed = center * lax.rsqrt(spread + 1e-06)
    normed = jnp.stack([normed[:, 384 * j : 384 * j + 384] for j in range(4)])
    normed = jnp.take(normed, (jnp.arange(4) - row) % 4, axis=0)
    normed = jnp.concatenate([normed[j] for j in range(4)], axis=1)
    normed = (normed * norm_gain.astype(jnp.float32)).astype(jnp.bfloat16)

    def whole(halves):
        own, other = halves
        low = jnp.where(group == 0, own, other)
        high = jnp.where(group == 0, other, own)
        return jnp.concatenate([low, high], axis=0)

    gate = jnp.dot(normed, whole(gate_halves), preferred_element_type=jnp.float32)
    upward = jnp.dot(normed, whole(up_halves), preferred_element_type=jnp.float32)
    hidden = jax.nn.silu(gate) * upward
    hidden = jnp.mean(hidden.reshape(32, 4, 8, 1024), axis=1).reshape(256, 1024).astype(jnp.bfloat16)
    branch = jnp.dot(hidden, whole(down_halves), preferred_element_type=jnp.float32)
    parts = jnp.stack([branch[:, 384 * j : 384 * j + 384] for j in range(4)])
    parts = jnp.take(parts, (jnp.arange(4) + row) % 4, axis=0)
    return parts


def shards(
    teacher_tokens,
    view_index,
    aug_embed,
    norm_gain,
    layer_scale,
    gate_weight,
    up_weight,
    down_weight,
    student_tokens,
    head_weight,
    owner,
):
    group, row, zl = lax.axis_index("group"), lax.axis_index("row"), lax.axis_index("zl")
    images = teacher_tokens.shape[0]

    def fetch(block):
        other = lax.ppermute(block, ("group", "zl"), [(0, 1), (3, 2)])
        mine = jnp.where(group == zl, block, other)
        spread = jnp.broadcast_to(mine[None], (16,) + mine.shape)
        return lax.all_to_all(spread, YX, 0, 0, tiled=True)

    gate_up = fetch(jnp.stack([gate_weight, up_weight]))
    gate_own = gate_up[:, 0].reshape(768, 1024)
    up_own = gate_up[:, 1].reshape(768, 1024)
    down_own = fetch(down_weight).reshape(512, D)
    gate_other = shift(gate_own, "group", 2, 1)
    up_other = shift(up_own, "group", 2, 1)
    down_other = shift(down_own, "group", 2, 1)

    kinds = aug_embed.shape[0]
    kind_table = (
        view_index.reshape(-1)[:, None] == jnp.arange(kinds, dtype=jnp.int32)[None, :]
    ).astype(jnp.bfloat16)
    embedded = jnp.dot(kind_table, aug_embed, preferred_element_type=jnp.float32).reshape(
        images, 4, 1, 384
    )
    shifted = (teacher_tokens.astype(jnp.float32) + embedded).astype(jnp.bfloat16)
    own = shifted.reshape(1024, 384)
    before = shift(own, "row", 4, 1)
    after = shift(own, "row", 4, -1)
    far_top = shift(before[:512], "row", 4, 1)
    far_bottom = shift(after[512:], "row", 4, -1)
    far = jnp.concatenate([far_top, far_bottom], axis=0)
    residual = jnp.mean(shifted.astype(jnp.float32), axis=1).reshape(256, 384)

    pupils = [student_tokens] + [shift(student_tokens, "row", 4, -j) for j in (1, 2, 3)]
    pupils = jnp.stack(pupils).reshape(4, images, 2, SW)
    pupils = jnp.take(pupils, (jnp.arange(4) - row) % 4, axis=0)
    pupils = pupils.transpose(1, 0, 2, 3).reshape(256, SW)
    head = jnp.dot(pupils, head_weight, preferred_element_type=jnp.float32)
    sums = lax.psum(jnp.stack([jnp.sum(head, axis=1), jnp.sum(head * head, axis=1)]), "row")
    center = (sums[0] / D)[:, None]
    scaler = lax.rsqrt((sums[1] / D)[:, None] - center * center + 1e-05)
    pred = (head - center) * scaler

    parts = middle(
        (own, after, far, before),
        (gate_own, gate_other),
        (up_own, up_other),
        (down_own, down_other),
        norm_gain,
        row,
        group,
    )
    narrow = parts.astype(jnp.bfloat16)
    got = [shift(narrow[j], "row", 4, j) for j in (2, 1, 3)]
    averaged = parts[0] + got[0].astype(jnp.float32) + got[1].astype(jnp.float32) + got[2].astype(jnp.float32)
    target = (residual + layer_scale.astype(jnp.float32) * averaged).astype(jnp.bfloat16)
    diff = pred - target.astype(jnp.float32)
    dpred = 2.0 * diff / IMAGES
    totals = lax.psum(
        jnp.stack(
            [jnp.sum(dpred, axis=1), jnp.sum(dpred * pred, axis=1), jnp.sum(diff * diff, axis=1)]
        ),
        "row",
    )
    dz = (
        scaler * (dpred - (totals[0] / D)[:, None] - pred * (totals[1] / D)[:, None])
    ).astype(jnp.bfloat16)
    errors = jnp.sum(totals[2].reshape(images, 8), axis=1) / (8 * D)
    mine = owner == jnp.arange(32, dtype=jnp.int32)[None, :]
    loss = jnp.sum(jnp.where(mine, errors[:, None], 0.0), axis=0)
    loss_high = loss.astype(jnp.bfloat16)
    loss_low = (loss - loss_high.astype(jnp.float32)).astype(jnp.bfloat16)

    grad = lax.dot_general(pupils, dz, (((0,), (0,)), ((), ())), preferred_element_type=jnp.float32)
    grad = grad.reshape(2, 384, 384)
    keep = lax.dynamic_index_in_dim(grad, group, 0, keepdims=False)
    give = lax.dynamic_index_in_dim(grad, 1 - group, 0, keepdims=False)
    half = keep + shift(give.astype(jnp.bfloat16), "group", 2, 1).astype(jnp.float32)
    half = half.astype(jnp.bfloat16).reshape(32, 12, 384)
    note = jnp.stack([loss_high, loss_low], axis=1)[:, :, None]
    note = jnp.broadcast_to(note, (32, 2, 384))
    packet = jnp.concatenate([half, note], axis=1)
    packet = lax.all_to_all(packet, COL, 0, 0, tiled=True).astype(jnp.float32)
    summed = jnp.sum(packet, axis=0)
    owner_loss = (summed[12, :1] + summed[13, :1])
    part = summed[:12].astype(jnp.bfloat16)
    part = lax.all_to_all(jnp.broadcast_to(part[None], (32, 12, 384)), COL, 0, 0, tiled=True)
    part = part.reshape(384, 384)
    twin = shift(part, "group", 2, 1)
    head_grad = jnp.concatenate(
        [jnp.where(group == 0, part, twin), jnp.where(group == 0, twin, part)], axis=0
    ).astype(jnp.float32)
    return (head_grad, owner_loss)


def solution(mesh):
    fine = Mesh(mesh.devices.reshape(2, 4, 2, 4, 4), ("group", "row", "zl", "y", "x"))
    return jax.shard_map(
        shards,
        mesh=fine,
        in_specs=(
            P(EVERY, None, None, "row"),
            P(EVERY, None),
            P(None, "row"),
            P(),
            P("row"),
            P(COL, "row"),
            P(COL, "row"),
            P(("row",) + COL, None),
            P(EVERY, "row"),
            P(None, "row"),
            P(EVERY, None),
        ),
        out_specs=(P(None, "row"), P(EVERY)),
        check_vma=False,
    )
```

time: 1360 us -> 223 us (0.16); the launches traced: 1340 us -> 222 us
  waiting for transfers between devices: 1220 us -> 43.9 us
  starting transfers between devices: 18.1 us -> 68 us
    psum x1 -> x0, waiting for transfers between devices: 577 us -> none  [shards(): head_grad = lax.psum(grad_part, ('group', 'col'))]
    all_gather x4 -> x0, waiting for transfers between devices: 510 us -> none  [the longest x1 160 us: shards(): lax.all_gather(up_weight, 'col', axis=0, tiled=True)]
    reduce_scatter x1 -> x0, waiting for transfers between devices: 122 us -> none  [shards(): summed = lax.psum_scatter(branch, 'row', scatter_dimension=3, tiled=True)]
    ppermute x0 -> x17, starting transfers between devices: none -> 54.2 us  [the longest x15 51.5 us: shift(): lax.ppermute(value, axis, [(i, (i + by) % size) for i in range(size)])]
    ppermute x0 -> x17, waiting for transfers between devices: none -> 37.1 us  [the longest x15 25.1 us: shift(): lax.ppermute(value, axis, [(i, (i + by) % size) for i in range(size)])]
    all_to_all x0 -> x2, blocking collectives: none -> 27.4 us  [the longest x1 14.7 us: shards(): packet = lax.all_to_all(packet, COL, 0, 0, tiled=True).astype(jnp.float32)]
    all_gather x1 -> x0, blocking collectives: 22.5 us -> none  [shards(): lessons_full = lax.all_gather(got_lessons, 'row', axis=2, tiled=True)]
  transfers between devices with their start and end apart: 9 -> 19, of which waited for: 7 -> 6; matrix products, arithmetic and copies ran while one was open for 2% -> 19% of each run, Pallas kernels for 0% -> 0%
where the time goes in v1:
time: 223 us; the launch traced here: 222 us
  starting transfers between devices  68 us (30%)
  blocking collectives  44.8 us (20%)
  waiting for transfers between devices  43.9 us (20%)
  other arithmetic  26 us (12%)
  local copies, waits for them, and re-layouts  21.5 us (10%)
  matrix products  14.4 us (6%)
  between operations  3.64 us (2%)
    ppermute x15, starting transfers between devices, shift(): lax.ppermute(value, axis, [(i, (i + by) % size) for i in range(size)])  51.5 us
    ppermute x15, waiting for transfers between devices, shift(): lax.ppermute(value, axis, [(i, (i + by) % size) for i in range(size)])  25.1 us
    all_to_all x1, blocking collectives, shards(): packet = lax.all_to_all(packet, COL, 0, 0, tiled=True).astype(jnp.float32)  14.7 us
    all_to_all x2, starting transfers between devices, fetch(): return lax.all_to_all(spread, YX, 0, 0, tiled=True)  13.8 us
    all_to_all x1, blocking collectives, shards(): lax.all_to_all(jnp.broadcast_to(part[None], (32, 12, 384)), COL, 0, 0, ti...  12.7 us
    ppermute x2, waiting for transfers between devices, fetch(): other = lax.ppermute(block, ('group', 'zl'), [(0, 1), (3, 2)])  12 us
    psum x1, blocking collectives, shards(): lax.psum(jnp.stack([jnp.sum(head, axis=1), jnp.sum(head * head, axis=1)])...  9.8 us
    psum x1, blocking collectives, shards(): lax.psum(jnp.stack([jnp.sum(dpred, axis=1), jnp.sum(dpred * pred, axis=1)...  7.65 us
  transfers between devices with their start and end apart: 19, of which 6 were waited for; matrix products, arithmetic and copies ran while one was open for 19% of the time, Pallas kernels for 0%

profile of v1, /device:TPU:1, one launch (start us, length us, event | category | flops | bytes accessed | tf_op | source)
XLA Modules:
  0.0 222.3 jit_solution(7345289424312077747)
XLA Ops:
  7.0 3.8 %collective-permute-start.4 = (bf16[1024,384]{1,0:T(8,128)(2,1)}, bf16[1024,384]{1,0:T(8,128)(2,1)}, u32[]{:S(2)}, u32[]{:S(2)}) collective-permute-start(bf16[1024,384]{1,0:T(8,128)(2,1)} %bitcast.9), channel_id=1, source_target_pairs={{0,32},{32,64},{64,96},{96,0},{1,33},{33,65},{65,97},{97,1},{2,34}... | collective-permute-start | bytes 2359304 | tf_op jit(solution)/shard_map/ppermute | solution.py:16
  10.8 3.0 %collective-permute-start.3 = (bf16[1024,384]{1,0:T(8,128)(2,1)}, bf16[1024,384]{1,0:T(8,128)(2,1)}, u32[]{:S(2)}, u32[]{:S(2)}) collective-permute-start(bf16[1024,384]{1,0:T(8,128)(2,1)} %bitcast.9), channel_id=1, source_target_pairs={{0,96},{32,0},{64,32},{96,64},{1,97},{33,1},{65,33},{97,65},{2,98}... | collective-permute-start | bytes 2359304 | tf_op jit(solution)/shard_map/ppermute | solution.py:16
  22.0 6.9 %all-to-all-start.1 = ((bf16[16,32,1536]{2,1,0:T(8,128)(2,1)}), bf16[16,32,1536]{2,1,0:T(8,128)(2,1)S(1)}, u32[]{:S(2)}, u32[]{:S(2)}) async-start(bf16[16,32,1536]{2,1,0:T(8,128)(2,1)} %broadcast_in_dim.83), calls=%async_computation.1 | async-start | bytes 3145728 | tf_op jit(solution)/shard_map/all_to_all | solution.py:65
  30.9 11.8 %collective-permute-done = bf16[32,1536]{1,0:T(8,128)(2,1)S(1)} collective-permute-done((bf16[32,1536]{1,0:T(8,128)(2,1)S(1)}, bf16[32,1536]{1,0:T(8,128)(2,1)S(1)}, u32[]{:S(2)}, u32[]{:S(2)}) %collective-permute-start) | collective-permute-done | bytes 98336 | tf_op jit(solution)/shard_map/ppermute | solution.py:16
  50.2 3.0 %collective-permute-start.6 = (bf16[512,384]{1,0:T(8,128)(2,1)}, bf16[512,384]{1,0:T(8,128)(2,1)}, u32[]{:S(2)}, u32[]{:S(2)}) collective-permute-start(bf16[512,384]{1,0:T(8,128)(2,1)} %slice.122), channel_id=1, source_target_pairs={{0,96},{32,0},{64,32},{96,64},{1,97},{33,1},{65,33},{97,65},{2,98}... | collective-permute-start | bytes 1179656 | tf_op jit(solution)/shard_map/ppermute | solution.py:16
  53.2 12.0 %collective-permute-done.7 = bf16[2,48,1024]{2,1,0:T(8,128)(2,1)} collective-permute-done((bf16[2,48,1024]{2,1,0:T(8,128)(2,1)}, bf16[2,48,1024]{2,1,0:T(8,128)(2,1)}, u32[]{:S(2)}, u32[]{:S(2)}) %collective-permute-start.7) | collective-permute-done | bytes 196640 | tf_op jit(solution)/shard_map/ppermute | solution.py:62
  68.2 6.9 %all-to-all-start = ((bf16[16,2,48,1024]{3,2,1,0:T(8,128)(2,1)}), bf16[16,2,48,1024]{3,2,1,0:T(8,128)(2,1)}, u32[]{:S(2)}, u32[]{:S(2)}) async-start(bf16[16,2,48,1024]{3,2,1,0:T(8,128)(2,1)} %broadcast_in_dim.82), calls=%async_computation | async-start | bytes 6291456 | tf_op jit(solution)/shard_map/all_to_all | solution.py:65
  75.2 9.8 %psum.14 = f32[2,256]{1,0:T(2,128)S(1)} all-reduce(f32[2,256]{1,0:T(2,128)S(1)} %pad_maximum_fusion.7), channel_id=1, replica_groups=mesh['group'=2,'row'=4,'zl'=2,'y'=4,'x'=4] {'row'}, use_global_device_ids=true, to_apply=%region_2.3 | all-reduce | flops 512 | bytes 4096 | tf_op jit(solution)/shard_map/psum | solution.py:96
  85.0 3.3 %convert_reduce_fusion = (f32[1024]{0:T(1024)S(1)}, bf16[1024,1536]{1,0:T(8,128)(2,1)S(1)}) fusion(bf16[1024,384]{1,0:T(8,128)(2,1)} %collective-permute-done.4, bf16[512,384]{1,0:T(8,128)(2,1)} %collective-permute-done.6, bf16[512,384]{1,0:T(8,128)(2,1)} %collective-permute-done.5, bf16[1024,384]{1,0:T(8,128)(2,1)} %collective-permute-done.3, ...), kind=kLoop, calls=%fused_computation.4 | loop fusion | flops 18873344 | bytes 6295552 | tf_op jit(solution)/shard_map/reduce_sum | solution.py:21
  90.5 5.9 %collective-permute-start.11 = (bf16[512,1536]{1,0:T(8,128)(2,1)S(1)}, bf16[512,1536]{1,0:T(8,128)(2,1)}, u32[]{:S(2)}, u32[]{:S(2)}) collective-permute-start(bf16[512,1536]{1,0:T(8,128)(2,1)S(1)} %bitcast.103), channel_id=1, source_target_pairs={{0,128},{128,0},{1,129},{129,1},{2,130},{130,2},{3,131},{131,3},{4... | collective-permute-start | bytes 4718600 | tf_op jit(solution)/shard_map/ppermute | solution.py:16
  99.3 6.4 %gather_fusion.1 = f32[4,1024,384]{2,1,0:T(8,128)} fusion(f32[4,1024,384]{2,1,0:T(8,128)} %pad_maximum_fusion, s32[1024]{0:T(1024)S(1)} %pad_clamp_fusion.1), kind=kCustom, calls=%fused_computation.1 | custom fusion | bytes 12582928 | tf_op jit(solution)/shard_map/jit(_take)/gather | solution.py:25
  105.7 6.8 %all-to-all-done = bf16[16,2,48,1024]{3,2,1,0:T(8,128)(2,1)} async-done(((bf16[16,2,48,1024]{3,2,1,0:T(8,128)(2,1)}), bf16[16,2,48,1024]{3,2,1,0:T(8,128)(2,1)}, u32[]{:S(2)}, u32[]{:S(2)}) %all-to-all-start) | async-done | bytes 3145760 | tf_op jit(solution)/shard_map/all_to_all | solution.py:65
  114.9 6.8 %collective-permute-start.8 = (bf16[768,1024]{1,0:T(8,128)(2,1)S(1)}, bf16[768,1024]{1,0:T(8,128)(2,1)S(1)}, u32[]{:S(2)}, u32[]{:S(2)}) collective-permute-start(bf16[768,1024]{1,0:T(8,128)(2,1)S(1)} %bitcast.105), channel_id=1, source_target_pairs={{0,128},{128,0},{1,129},{129,1},{2,130},{130,2},{3,131},{131,3},{4... | collective-permute-start | bytes 4718600 | tf_op jit(solution)/shard_map/ppermute | solution.py:16
  123.9 3.3 %broadcast_select_fusion.2 = (bf16[512,1536]{1,0:T(8,128)(2,1)}, bf16[512,1536]{1,0:T(8,128)(2,1)}) fusion(bf16[512,1536]{1,0:T(8,128)(2,1)} %collective-permute-done.11, pred[]{:T(512)S(6)} %eq.24, bf16[16,32,1536]{2,1,0:T(8,128)(2,1)S(1)} %all-to-all-done.1), kind=kLoop, calls=%fused_computation.38 | loop fusion | flops 1572864 | bytes 6291457 | tf_op jit(solution)/shard_map/jit(_where)/select_n | solution.py:31
  127.5 3.4 %fusion.4 = f32[1024,1024]{1,0:T(8,128)S(1)} fusion(bf16[768,1024]{1,0:T(8,128)(2,1)S(1)} %get-tuple-element.27, bf16[768,1024]{1,0:T(8,128)(2,1)S(1)} %get-tuple-element.26, f32[1024,384]{1,0:T(8,128)S(1)} %get-tuple-element.15, f32[1024,384]{1,0:T(8,128)S(1)} %get-tuple-element.16, f32[1024,384]{1,0:T(8,128)S(1)} %get-tuple-element.17, ...), kind=kOutput, calls=%fused_computation.13 | convolution fusion | flops 3235381248 | bytes 13637632 | tf_op jit(solution)/shard_map/dot_general | solution.py:35
  131.3 5.7 %multiply_multiply_fusion = f32[1024,1024]{1,0:T(8,128)} fusion(f32[1024,1024]{1,0:T(8,128)S(1)} %fusion.4, bf16[768,1024]{1,0:T(8,128)(2,1)S(1)} %get-tuple-element.23, bf16[768,1024]{1,0:T(8,128)(2,1)S(1)} %get-tuple-element.22, f32[1024,384]{1,0:T(8,128)S(1)} %get-tuple-element.15, f32[1024,384]{1,0:T(8,128)S(1)} %get-tuple-element.16, ...), kind=kOutput, calls=%fused_computation.11 | convolution fusion | flops 3240624128 | bytes 17831936 | tf_op jit(solution)/shard_map/dot_general | solution.py:36
  137.1 3.8 %reduce_sum.115 = f32[32,8,1024]{2,1,0:T(8,128)} reduce(f32[32,4,8,1024]{3,2,1,0:T(8,128)} %bitcast.106, f32[]{:T(128)} %constant.111.clone.1), dimensions={1}, to_apply=%region_6.7 | reduce | flops 786432 | bytes 5242884 | tf_op jit(solution)/shard_map/reduce_sum | solution.py:38
  150.5 3.4 %collective-permute-start.13 = (bf16[256,384]{1,0:T(8,128)(2,1)S(1)}, bf16[256,384]{1,0:T(8,128)(2,1)S(1)}, u32[]{:S(2)}, u32[]{:S(2)}) collective-permute-start(bf16[256,384]{1,0:T(8,128)(2,1)S(1)} %get-tuple-element.36), channel_id=1, source_target_pairs={{0,32},{32,64},{64,96},{96,0},{1,33},{33,65},{65,97},{97,1},{2,34}... | collective-permute-start | bytes 589832 | tf_op jit(solution)/shard_map/ppermute | solution.py:16
  154.1 4.0 %collective-permute-done.12 = bf16[256,384]{1,0:T(8,128)(2,1)S(1)} collective-permute-done((bf16[256,384]{1,0:T(8,128)(2,1)S(1)}, bf16[256,384]{1,0:T(8,128)(2,1)S(1)}, u32[]{:S(2)}, u32[]{:S(2)}) %collective-permute-start.12) | collective-permute-done | bytes 196640 | tf_op jit(solution)/shard_map/ppermute | solution.py:16
  158.2 8.5 %collective-permute-done.13 = bf16[256,384]{1,0:T(8,128)(2,1)S(1)} collective-permute-done((bf16[256,384]{1,0:T(8,128)(2,1)S(1)}, bf16[256,384]{1,0:T(8,128)(2,1)S(1)}, u32[]{:S(2)}, u32[]{:S(2)}) %collective-permute-start.13) | collective-permute-done | bytes 196640 | tf_op jit(solution)/shard_map/ppermute | solution.py:16
  167.1 7.7 %psum.15 = f32[3,256]{1,0:T(4,128)S(1)} all-reduce(f32[3,256]{1,0:T(4,128)S(1)} %pad_maximum_fusion.6), channel_id=1, replica_groups=mesh['group'=2,'row'=4,'zl'=2,'y'=4,'x'=4] {'row'}, use_global_device_ids=true, to_apply=%region_10.11 | all-reduce | flops 768 | bytes 6144 | tf_op jit(solution)/shard_map/psum | solution.py:116
  175.4 10.8 %collective-permute-start.15 = (bf16[384,384]{1,0:T(8,128)(2,1)S(1)}, bf16[384,384]{1,0:T(8,128)(2,1)S(1)}, u32[]{:S(2)}, u32[]{:S(2)}) collective-permute-start(bf16[384,384]{1,0:T(8,128)(2,1)S(1)} %fusion.28), channel_id=1, source_target_pairs={{0,128},{128,0},{1,129},{129,1},{2,130},{130,2},{3,131},{131,3},{4... | collective-permute-start | bytes 884744 | tf_op jit(solution)/shard_map/ppermute | solution.py:16
  187.8 14.7 %all_to_all.20 = bf16[32,14,384]{2,1,0:T(8,128)(2,1)S(1)} all-to-all(bf16[32,14,384]{2,1,0:T(8,128)(2,1)S(1)} %pad_maximum_fusion.4), channel_id=1, replica_groups=mesh['group'=2,'row'=4,'zl'=2,'y'=4,'x'=4] {'zl','y','x'}, dimensions={0} | all-to-all | bytes 688128 | tf_op jit(solution)/shard_map/all_to_all | solution.py:140
  202.6 12.7 %all_to_all.21 = bf16[32,12,384]{2,1,0:T(8,128)(2,1)S(1)} all-to-all(bf16[32,12,384]{2,1,0:T(8,128)(2,1)S(1)} %broadcast_in_dim.88), channel_id=1, replica_groups=mesh['group'=2,'row'=4,'zl'=2,'y'=4,'x'=4] {'zl','y','x'}, dimensions={0} | all-to-all | bytes 589824 | tf_op jit(solution)/shard_map/all_to_all | solution.py:144
  (136 shorter events, 53.9 us)
Async XLA Ops:
  0.6 45.1 %copy-start = (bf16[768,384]{1,0:T(8,128)(2,1)S(1)}, bf16[768,384]{1,0:T(8,128)(2,1)}, u32[]{:S(2)}) copy-start(bf16[768,384]{1,0:T(8,128)(2,1)} %param.20) | copy-start | bytes 1769476
  0.6 20.0 %copy-start.8 = (bf16[32,1536]{1,0:T(8,128)(2,1)S(1)}, bf16[32,1536]{1,0:T(8,128)(2,1)}, u32[]{:S(2)}) copy-start(bf16[32,1536]{1,0:T(8,128)(2,1)} %param.18) | copy-start | bytes 294916
  0.7 17.7 %collective-permute-start.10 = (bf16[32,1536]{1,0:T(8,128)(2,1)}, bf16[32,1536]{1,0:T(8,128)(2,1)S(1)}, u32[]{:S(2)}, u32[]{:S(2)}) collective-permute-start(bf16[32,1536]{1,0:T(8,128)(2,1)} %param.18), channel_id=1, source_target_pairs={{0,16},{144,128},{1,17},{145,129},{2,18},{146,130},{3,19},{147,131... | collective-permute-start | bytes 294920 | tf_op jit(solution)/shard_map/ppermute | solution.py:62
  7.0 39.7 %collective-permute-start.4 = (bf16[1024,384]{1,0:T(8,128)(2,1)}, bf16[1024,384]{1,0:T(8,128)(2,1)}, u32[]{:S(2)}, u32[]{:S(2)}) collective-permute-start(bf16[1024,384]{1,0:T(8,128)(2,1)} %bitcast.9), channel_id=1, source_target_pairs={{0,32},{32,64},{64,96},{96,0},{1,33},{33,65},{65,97},{97,1},{2,34}... | collective-permute-start | bytes 2359304 | tf_op jit(solution)/shard_map/ppermute | solution.py:16
  10.8 37.6 %collective-permute-start.3 = (bf16[1024,384]{1,0:T(8,128)(2,1)}, bf16[1024,384]{1,0:T(8,128)(2,1)}, u32[]{:S(2)}, u32[]{:S(2)}) collective-permute-start(bf16[1024,384]{1,0:T(8,128)(2,1)} %bitcast.9), channel_id=1, source_target_pairs={{0,96},{32,0},{64,32},{96,64},{1,97},{33,1},{65,33},{97,65},{2,98}... | collective-permute-start | bytes 2359304 | tf_op jit(solution)/shard_map/ppermute | solution.py:16
  13.8 28.9 %collective-permute-start = (bf16[32,1536]{1,0:T(8,128)(2,1)S(1)}, bf16[32,1536]{1,0:T(8,128)(2,1)S(1)}, u32[]{:S(2)}, u32[]{:S(2)}) collective-permute-start(bf16[32,1536]{1,0:T(8,128)(2,1)S(1)} %copy-done.7), channel_id=1, source_target_pairs={{0,96},{32,0},{64,32},{96,64},{1,97},{33,1},{65,33},{97,65},{2,98}... | collective-permute-start | bytes 294920 | tf_op jit(solution)/shard_map/ppermute | solution.py:16
  16.2 27.9 %collective-permute-start.1 = (bf16[32,1536]{1,0:T(8,128)(2,1)S(1)}, bf16[32,1536]{1,0:T(8,128)(2,1)S(1)}, u32[]{:S(2)}, u32[]{:S(2)}) collective-permute-start(bf16[32,1536]{1,0:T(8,128)(2,1)S(1)} %copy-done.7), channel_id=1, source_target_pairs={{0,64},{32,96},{64,0},{96,32},{1,65},{33,97},{65,1},{97,33},{2,66}... | collective-permute-start | bytes 294920 | tf_op jit(solution)/shard_map/ppermute | solution.py:16
  18.3 25.8 %collective-permute-start.2 = (bf16[32,1536]{1,0:T(8,128)(2,1)S(1)}, bf16[32,1536]{1,0:T(8,128)(2,1)S(1)}, u32[]{:S(2)}, u32[]{:S(2)}) collective-permute-start(bf16[32,1536]{1,0:T(8,128)(2,1)S(1)} %copy-done.7), channel_id=1, source_target_pairs={{0,32},{32,64},{64,96},{96,0},{1,33},{33,65},{65,97},{97,1},{2,34}... | collective-permute-start | bytes 294920 | tf_op jit(solution)/shard_map/ppermute | solution.py:16
  22.0 44.2 %all-to-all-start.1 = ((bf16[16,32,1536]{2,1,0:T(8,128)(2,1)}), bf16[16,32,1536]{2,1,0:T(8,128)(2,1)S(1)}, u32[]{:S(2)}, u32[]{:S(2)}) async-start(bf16[16,32,1536]{2,1,0:T(8,128)(2,1)} %broadcast_in_dim.83), calls=%async_computation.1 | async-start | bytes 3145728 | tf_op jit(solution)/shard_map/all_to_all | solution.py:65
  42.7 22.5 %collective-permute-start.7 = (bf16[2,48,1024]{2,1,0:T(8,128)(2,1)}, bf16[2,48,1024]{2,1,0:T(8,128)(2,1)}, u32[]{:S(2)}, u32[]{:S(2)}) collective-permute-start(bf16[2,48,1024]{2,1,0:T(8,128)(2,1)} %pad_maximum_fusion.5), channel_id=1, source_target_pairs={{0,16},{144,128},{1,17},{145,129},{2,18},{146,130},{3,19},{147,131... | collective-permute-start | bytes 589832 | tf_op jit(solution)/shard_map/ppermute | solution.py:62
  47.8 37.3 %collective-permute-start.5 = (bf16[512,384]{1,0:T(8,128)(2,1)S(1)}, bf16[512,384]{1,0:T(8,128)(2,1)}, u32[]{:S(2)}, u32[]{:S(2)}) collective-permute-start(bf16[512,384]{1,0:T(8,128)(2,1)S(1)} %slice.121), channel_id=1, source_target_pairs={{0,32},{32,64},{64,96},{96,0},{1,33},{33,65},{65,97},{97,1},{2,34}... | collective-permute-start | bytes 1179656 | tf_op jit(solution)/shard_map/ppermute | solution.py:16
  50.2 34.8 %collective-permute-start.6 = (bf16[512,384]{1,0:T(8,128)(2,1)}, bf16[512,384]{1,0:T(8,128)(2,1)}, u32[]{:S(2)}, u32[]{:S(2)}) collective-permute-start(bf16[512,384]{1,0:T(8,128)(2,1)} %slice.122), channel_id=1, source_target_pairs={{0,96},{32,0},{64,32},{96,64},{1,97},{33,1},{65,33},{97,65},{2,98}... | collective-permute-start | bytes 1179656 | tf_op jit(solution)/shard_map/ppermute | solution.py:16
  68.2 44.2 %all-to-all-start = ((bf16[16,2,48,1024]{3,2,1,0:T(8,128)(2,1)}), bf16[16,2,48,1024]{3,2,1,0:T(8,128)(2,1)}, u32[]{:S(2)}, u32[]{:S(2)}) async-start(bf16[16,2,48,1024]{3,2,1,0:T(8,128)(2,1)} %broadcast_in_dim.82), calls=%async_computation | async-start | bytes 6291456 | tf_op jit(solution)/shard_map/all_to_all | solution.py:65
  90.5 33.4 %collective-permute-start.11 = (bf16[512,1536]{1,0:T(8,128)(2,1)S(1)}, bf16[512,1536]{1,0:T(8,128)(2,1)}, u32[]{:S(2)}, u32[]{:S(2)}) collective-permute-start(bf16[512,1536]{1,0:T(8,128)(2,1)S(1)} %bitcast.103), channel_id=1, source_target_pairs={{0,128},{128,0},{1,129},{129,1},{2,130},{130,2},{3,131},{131,3},{4... | collective-permute-start | bytes 4718600 | tf_op jit(solution)/shard_map/ppermute | solution.py:16
  105.7 16.0 %copy-start.13 = (pred[4]{0:T(512)(128)(4,1)S(1)}, pred[4]{0:T(512)(128)(4,1)}, u32[]{:S(2)}) copy-start(pred[4]{0:T(512)(128)(4,1)} %copy-done.12) | copy-start | bytes 16
  114.9 12.4 %collective-permute-start.8 = (bf16[768,1024]{1,0:T(8,128)(2,1)S(1)}, bf16[768,1024]{1,0:T(8,128)(2,1)S(1)}, u32[]{:S(2)}, u32[]{:S(2)}) collective-permute-start(bf16[768,1024]{1,0:T(8,128)(2,1)S(1)} %bitcast.105), channel_id=1, source_target_pairs={{0,128},{128,0},{1,129},{129,1},{2,130},{130,2},{3,131},{131,3},{4... | collective-permute-start | bytes 4718600 | tf_op jit(solution)/shard_map/ppermute | solution.py:16
  122.6 8.4 %collective-permute-start.9 = (bf16[768,1024]{1,0:T(8,128)(2,1)S(1)}, bf16[768,1024]{1,0:T(8,128)(2,1)S(1)}, u32[]{:S(2)}, u32[]{:S(2)}) collective-permute-start(bf16[768,1024]{1,0:T(8,128)(2,1)S(1)} %bitcast.104), channel_id=1, source_target_pairs={{0,128},{128,0},{1,129},{129,1},{2,130},{130,2},{3,131},{131,3},{4... | collective-permute-start | bytes 4718600 | tf_op jit(solution)/shard_map/ppermute | solution.py:16
  145.9 20.8 %copy-start.4 = (f32[32,8,384]{2,1,0:T(8,128)S(1)}, f32[32,8,384]{2,1,0:T(8,128)}, u32[]{:S(2)}) copy-start(f32[32,8,384]{2,1,0:T(8,128)} %get-tuple-element.8) | copy-start | bytes 1179652
  147.7 10.5 %collective-permute-start.12 = (bf16[256,384]{1,0:T(8,128)(2,1)S(1)}, bf16[256,384]{1,0:T(8,128)(2,1)S(1)}, u32[]{:S(2)}, u32[]{:S(2)}) collective-permute-start(bf16[256,384]{1,0:T(8,128)(2,1)S(1)} %get-tuple-element.34), channel_id=1, source_target_pairs={{0,64},{32,96},{64,0},{96,32},{1,65},{33,97},{65,1},{97,33},{2,66}... | collective-permute-start | bytes 589832 | tf_op jit(solution)/shard_map/ppermute | solution.py:16
  150.5 16.1 %collective-permute-start.13 = (bf16[256,384]{1,0:T(8,128)(2,1)S(1)}, bf16[256,384]{1,0:T(8,128)(2,1)S(1)}, u32[]{:S(2)}, u32[]{:S(2)}) collective-permute-start(bf16[256,384]{1,0:T(8,128)(2,1)S(1)} %get-tuple-element.36), channel_id=1, source_target_pairs={{0,32},{32,64},{64,96},{96,0},{1,33},{33,65},{65,97},{97,1},{2,34}... | collective-permute-start | bytes 589832 | tf_op jit(solution)/shard_map/ppermute | solution.py:16
  154.0 12.7 %collective-permute-start.14 = (bf16[256,384]{1,0:T(8,128)(2,1)S(1)}, bf16[256,384]{1,0:T(8,128)(2,1)S(1)}, u32[]{:S(2)}, u32[]{:S(2)}) collective-permute-start(bf16[256,384]{1,0:T(8,128)(2,1)S(1)} %get-tuple-element.35), channel_id=1, source_target_pairs={{0,96},{32,0},{64,32},{96,64},{1,97},{33,1},{65,33},{97,65},{2,98}... | collective-permute-start | bytes 589832 | tf_op jit(solution)/shard_map/ppermute | solution.py:16
  167.1 19.3 %copy-start.16 = (s32[32,1]{0,1:T(1,128)S(1)}, s32[32,1]{0,1:T(1,128)}, u32[]{:S(2)}) copy-start(s32[32,1]{0,1:T(1,128)} %param.21) | copy-start | bytes 388
  175.4 12.0 %collective-permute-start.15 = (bf16[384,384]{1,0:T(8,128)(2,1)S(1)}, bf16[384,384]{1,0:T(8,128)(2,1)S(1)}, u32[]{:S(2)}, u32[]{:S(2)}) collective-permute-start(bf16[384,384]{1,0:T(8,128)(2,1)S(1)} %fusion.28), channel_id=1, source_target_pairs={{0,128},{128,0},{1,129},{129,1},{2,130},{130,2},{3,131},{131,3},{4... | collective-permute-start | bytes 884744 | tf_op jit(solution)/shard_map/ppermute | solution.py:16
  215.3 4.6 %collective-permute-start.16 = (bf16[384,384]{1,0:T(8,128)(2,1)S(1)}, bf16[384,384]{1,0:T(8,128)(2,1)S(1)}, u32[]{:S(2)}, u32[]{:S(2)}) collective-permute-start(bf16[384,384]{1,0:T(8,128)(2,1)S(1)} %reshape.240), channel_id=1, source_target_pairs={{0,128},{128,0},{1,129},{129,1},{2,130},{130,2},{3,131},{131,3},{4... | collective-permute-start | bytes 884744 | tf_op jit(solution)/shard_map/ppermute | solution.py:16
  (12 other events, 92.7 us)

commit v2 on v1

v2 whole, which is shorter than its diff:
```python
import jax
import jax.numpy as jnp
from jax import lax
from jax.experimental import pallas as pl
from jax.experimental.pallas import tpu as pltpu
from jax.sharding import Mesh, PartitionSpec as P

D = 1536
SW = 768
PART = 384
YX = ("y", "x")
COL = ("zl", "y", "x")
EVERY = ("group", "zl", "y", "x")
IMAGES = 2048
MIB = 1024 * 1024


def shift(value, axis, size, by):
    return lax.ppermute(value, axis, [(i, (i + by) % size) for i in range(size)])


def norm_kernel(place, own, after, before, far_top, far_bottom, gain, out):
    row, group = place[0], place[1]
    far = jnp.where(pl.program_id(0) < 2, far_top[...], far_bottom[...])
    pieces = [own[0], after[0], far, before[0]]
    pieces = [piece.astype(jnp.float32) for piece in pieces]
    total = sum(jnp.sum(piece, axis=1, keepdims=True) for piece in pieces)
    mean = total * (1.0 / D)
    pieces = [piece - mean for piece in pieces]
    square = sum(jnp.sum(piece * piece, axis=1, keepdims=True) for piece in pieces)
    scale = lax.rsqrt(square * (1.0 / D) + 1e-06)
    for j, piece in enumerate(pieces):
        block = lax.rem(row + j, 4)
        source = pl.multiple_of(block * PART, PART)
        target = pl.multiple_of(lax.rem(block + 2 * group, 4) * PART, PART)
        value = piece * scale * gain[:, pl.ds(source, PART)]
        out[:, pl.ds(target, PART)] = value.astype(jnp.bfloat16)


def norm(place, own, after, before, far_top, far_bottom, gain):
    piece = pl.BlockSpec((1, 256, PART), lambda b: (b // 2, b % 2, 0))
    return pl.pallas_call(
        norm_kernel,
        grid=(4,),
        in_specs=[
            pl.BlockSpec(memory_space=pltpu.SMEM),
            piece,
            piece,
            piece,
            pl.BlockSpec((256, PART), lambda b: (jnp.minimum(b, 1), 0)),
            pl.BlockSpec((256, PART), lambda b: (jnp.maximum(b - 2, 0), 0)),
            pl.BlockSpec((1, D), lambda b: (0, 0)),
        ],
        out_specs=pl.BlockSpec((256, D), lambda b: (b, 0)),
        out_shape=jax.ShapeDtypeStruct((1024, D), jnp.bfloat16),
        compiler_params=pltpu.CompilerParams(vmem_limit_bytes=24 * MIB),
        cost_estimate=pl.CostEstimate(
            flops=16 * 1024 * D, bytes_accessed=4 * 1024 * D, transcendentals=0
        ),
    )(place, own, after, before, far_top, far_bottom, gain)


def hidden_kernel(place, normed, own, other, out, weights, sems):
    group = place[1]

    def copy(side, kind, n):
        source = own if side == 0 else other
        start = pl.multiple_of(kind * 1024 + n * 256, 256)
        return pltpu.make_async_copy(
            source.at[:, pl.ds(start, 256)], weights.at[n, kind, side], sems.at[n, kind, side]
        )

    for n in range(4):
        for kind in (0, 1):
            for side in (0, 1):
                copy(side, kind, n).start()

    def step(n, carry):
        values = []
        for kind in (0, 1):
            for side in (0, 1):
                copy(side, kind, n).wait()
            values.append(
                jnp.dot(
                    normed[:, :768], weights[n, kind, 0], preferred_element_type=jnp.float32
                )
                + jnp.dot(
                    normed[:, 768:], weights[n, kind, 1], preferred_element_type=jnp.float32
                )
            )
        gate, upward = values
        hidden = gate * upward / (1.0 + jnp.exp(-gate))
        hidden = jnp.sum(hidden.reshape(32, 4, 8, 256), axis=1).reshape(256, 256) * 0.25
        target = pl.multiple_of(lax.rem(n + 2 * group, 4) * 256, 256)
        out[:, pl.ds(target, 256)] = hidden.astype(jnp.bfloat16)
        return carry

    lax.fori_loop(0, 4, step, 0)


def hidden_mean(place, normed, own, other):
    return pl.pallas_call(
        hidden_kernel,
        in_specs=[
            pl.BlockSpec(memory_space=pltpu.SMEM),
            pl.BlockSpec(memory_space=pltpu.VMEM),
            pl.BlockSpec(memory_space=pl.ANY),
            pl.BlockSpec(memory_space=pl.ANY),
        ],
        out_specs=pl.BlockSpec(memory_space=pltpu.VMEM),
        out_shape=jax.ShapeDtypeStruct((256, 1024), jnp.bfloat16),
        scratch_shapes=[
            pltpu.VMEM((4, 2, 2, 768, 256), jnp.bfloat16),
            pltpu.SemaphoreType.DMA((4, 2, 2)),
        ],
        compiler_params=pltpu.CompilerParams(vmem_limit_bytes=32 * MIB),
        cost_estimate=pl.CostEstimate(
            flops=2 * 1024 * D * 2048, bytes_accessed=10 * MIB, transcendentals=1024 * 1024
        ),
    )(place, normed, own, other)


def branch_kernel(place, hidden, own, other, out0, out1, out2, out3, weights, sems):
    row = place[0]
    outs = (out0, out1, out2, out3)

    def copy(side, j):
        source = own if side == 0 else other
        start = pl.multiple_of(lax.rem(row + j, 4) * PART, PART)
        return pltpu.make_async_copy(
            source.at[:, pl.ds(start, PART)], weights.at[j, side], sems.at[j, side]
        )

    for j in (2, 1, 3, 0):
        for side in (0, 1):
            copy(side, j).start()
    for j in (2, 1, 3, 0):
        for side in (0, 1):
            copy(side, j).wait()
        value = jnp.dot(
            hidden[:, :512], weights[j, 0], preferred_element_type=jnp.float32
        ) + jnp.dot(hidden[:, 512:], weights[j, 1], preferred_element_type=jnp.float32)
        outs[j][...] = value.astype(outs[j].dtype)


def branch(place, hidden, own, other):
    narrow = jax.ShapeDtypeStruct((256, PART), jnp.bfloat16)
    return pl.pallas_call(
        branch_kernel,
        in_specs=[
            pl.BlockSpec(memory_space=pltpu.SMEM),
            pl.BlockSpec(memory_space=pltpu.VMEM),
            pl.BlockSpec(memory_space=pl.ANY),
            pl.BlockSpec(memory_space=pl.ANY),
        ],
        out_specs=[pl.BlockSpec(memory_space=pltpu.VMEM)] * 4,
        out_shape=[jax.ShapeDtypeStruct((256, PART), jnp.float32), narrow, narrow, narrow],
        scratch_shapes=[
            pltpu.VMEM((4, 2, 512, PART), jnp.bfloat16),
            pltpu.SemaphoreType.DMA((4, 2)),
        ],
        compiler_params=pltpu.CompilerParams(vmem_limit_bytes=16 * MIB),
        cost_estimate=pl.CostEstimate(
            flops=2 * 256 * D * 1024, bytes_accessed=5 * MIB, transcendentals=0
        ),
    )(place, hidden, own, other)


def shards(
    teacher_tokens,
    view_index,
    aug_embed,
    norm_gain,
    layer_scale,
    gate_weight,
    up_weight,
    down_weight,
    student_tokens,
    head_weight,
    owner,
):
    group, row, zl = lax.axis_index("group"), lax.axis_index("row"), lax.axis_index("zl")
    images = teacher_tokens.shape[0]
    place = jnp.stack([row, group]).astype(jnp.int32)

    def select(block):
        other = lax.ppermute(block, ("group", "zl"), [(0, 1), (3, 2)])
        return jnp.where(group == zl, block, other)

    def fetch(mine):
        spread = jnp.broadcast_to(mine[None], (16,) + mine.shape)
        return lax.all_to_all(spread, YX, 0, 0, tiled=True).reshape(-1, mine.shape[-1])

    gate_up = select(jnp.concatenate([gate_weight, up_weight], axis=1))
    down = select(down_weight)
    gate_up_own = fetch(gate_up)
    gate_up_other = shift(gate_up_own, "group", 2, 1)
    down, gate_up_own = lax.optimization_barrier((down, gate_up_own))
    down_own = fetch(down)
    down_other = shift(down_own, "group", 2, 1)

    kinds = aug_embed.shape[0]
    kind_table = (
        view_index.reshape(-1)[:, None] == jnp.arange(kinds, dtype=jnp.int32)[None, :]
    ).astype(jnp.bfloat16)
    embedded = jnp.dot(kind_table, aug_embed, preferred_element_type=jnp.float32).reshape(
        images, 4, 1, PART
    )
    shifted = (teacher_tokens.astype(jnp.float32) + embedded).astype(jnp.bfloat16)
    residual = jnp.mean(shifted.astype(jnp.float32), axis=1).reshape(256, PART)
    student = [student_tokens[:, PART * c : PART * c + PART] for c in range(4)]
    own = jnp.concatenate(
        [
            shifted.reshape(2, 512, PART),
            jnp.stack([jnp.concatenate(student[:2]), jnp.concatenate(student[2:])]),
        ],
        axis=1,
    )
    before = shift(own, "row", 4, 1)
    after = shift(own, "row", 4, -1)
    far_top = shift(before[0], "row", 4, 1)
    far_bottom = shift(after[1], "row", 4, -1)

    gain = norm_gain.astype(jnp.float32).reshape(1, D)
    normed = norm(place, own, after, before, far_top, far_bottom, gain)
    hidden = hidden_mean(place, normed, gate_up_own, gate_up_other)
    part, *away = branch(place, hidden, down_own, down_other)
    got = [shift(away[j - 1], "row", 4, j) for j in (2, 1, 3)]

    def pupil(halves):
        return jnp.stack(
            [jnp.concatenate([half[512:544], half[544:576]], axis=1) for half in halves]
        )

    pupils = [pupil(own), pupil(after), pupil((far_top, far_bottom)), pupil(before)]
    pupils = jnp.stack(pupils + pupils)
    pupils = lax.dynamic_slice_in_dim(pupils, 4 - row, 4, axis=0)
    pupils = pupils.reshape(8, images, SW).transpose(1, 0, 2).reshape(256, SW)
    head = jnp.dot(pupils, head_weight, preferred_element_type=jnp.float32)

    averaged = part + sum(piece.astype(jnp.float32) for piece in got)
    target = (residual + layer_scale.astype(jnp.float32) * averaged).astype(jnp.bfloat16)
    target = target.astype(jnp.float32)
    sums = jnp.stack(
        [
            jnp.sum(head, axis=1),
            jnp.sum(head * head, axis=1),
            jnp.sum(target, axis=1),
            jnp.sum(head * target, axis=1),
            jnp.sum(target * target, axis=1),
        ]
    )
    sums = jnp.sum(lax.all_gather(sums, "row"), axis=0)
    center = sums[0] / D
    spread = sums[1] / D - center * center
    scaler = lax.rsqrt(spread + 1e-05)
    pred_square = scaler * scaler * (sums[1] - D * center * center)
    pred_target = scaler * (sums[3] - center * sums[2])
    diff_square = pred_square - 2.0 * pred_target + sums[4]
    mean_first = -2.0 / IMAGES * sums[2] / D
    mean_second = 2.0 / IMAGES * (pred_square - pred_target) / D
    pred = (head - center[:, None]) * scaler[:, None]
    dpred = 2.0 / IMAGES * (pred - target)
    dz = (
        scaler[:, None] * (dpred - mean_first[:, None] - pred * mean_second[:, None])
    ).astype(jnp.bfloat16)
    errors = jnp.sum(diff_square.reshape(images, 8), axis=1) / (8 * D)
    mine = owner == jnp.arange(32, dtype=jnp.int32)[None, :]
    loss = jnp.sum(jnp.where(mine, errors[:, None], 0.0), axis=0)
    loss_high = loss.astype(jnp.bfloat16)
    loss_low = (loss - loss_high.astype(jnp.float32)).astype(jnp.bfloat16)

    grad = lax.dot_general(pupils, dz, (((0,), (0,)), ((), ())), preferred_element_type=jnp.float32)
    grad = grad.reshape(2, PART, PART)
    keep = lax.dynamic_index_in_dim(grad, group, 0, keepdims=False)
    give = lax.dynamic_index_in_dim(grad, 1 - group, 0, keepdims=False)
    half = keep + shift(give.astype(jnp.bfloat16), "group", 2, 1).astype(jnp.float32)
    half = half.astype(jnp.bfloat16).reshape(32, 12, PART)
    note = jnp.stack([loss_high, loss_low], axis=1)[:, :, None]
    note = jnp.broadcast_to(note, (32, 2, PART))
    packet = jnp.concatenate([half, note], axis=1)
    packet = lax.all_to_all(packet, COL, 0, 0, tiled=True).astype(jnp.float32)
    summed = jnp.sum(packet, axis=0)
    owner_loss = summed[12, :1] + summed[13, :1]
    piece = summed[:12].astype(jnp.bfloat16)
    piece = lax.all_to_all(jnp.broadcast_to(piece[None], (32, 12, PART)), COL, 0, 0, tiled=True)
    piece = piece.reshape(PART, PART)
    twin = shift(piece, "group", 2, 1)
    head_grad = jnp.concatenate(
        [jnp.where(group == 0, piece, twin), jnp.where(group == 0, twin, piece)], axis=0
    ).astype(jnp.float32)
    return (head_grad, owner_loss)


def solution(mesh):
    fine = Mesh(mesh.devices.reshape(2, 4, 2, 4, 4), ("group", "row", "zl", "y", "x"))
    return jax.shard_map(
        shards,
        mesh=fine,
        in_specs=(
            P(EVERY, None, None, "row"),
            P(EVERY, None),
            P(None, "row"),
            P(),
            P("row"),
            P(COL, "row"),
            P(COL, "row"),
            P(("row",) + COL, None),
            P(EVERY, "row"),
            P(None, "row"),
            P(EVERY, None),
        ),
        out_specs=(P(None, "row"), P(EVERY)),
        check_vma=False,
    )
```

time: 223 us -> 218 us (0.978)
  waiting for transfers between devices: 43.9 us -> 69.6 us
  starting transfers between devices: 68 us -> 42.5 us
  Pallas kernels: 0 us -> 23.5 us
  matrix products: 14.4 us -> 1.14 us
  other arithmetic: 26 us -> 14.4 us
  blocking collectives: 44.8 us -> 42 us
    all_to_all x2, waiting for transfers between devices: 6.82 us -> 39 us  [fetch(): lax.all_to_all(spread, YX, 0, 0, tiled=True).reshape(-1, mine.shape[-1])]
    pallas_call x0 -> x3, Pallas kernels: none -> 23.5 us  [the longest x1 16 us: hidden_mean(): pl.pallas_call(hidden_kernel, in_specs=[pl.BlockSpec(memory_space=pltpu.S...]
    ppermute x15 -> x11, starting transfers between devices: 51.5 us -> 28.5 us  [shift(): lax.ppermute(value, axis, [(i, (i + by) % size) for i in range(size)])]
    psum x2 -> x0, blocking collectives: 17.5 us -> none  [the longest x1 9.8 us: shards(): lax.psum(jnp.stack([jnp.sum(head, axis=1), jnp.sum(head * head, axis=1)])...]
    all_gather x0 -> x1, blocking collectives: none -> 12.3 us  [shards(): sums = jnp.sum(lax.all_gather(sums, 'row'), axis=0)]
    dot_general x3 -> x0, matrix products: 11.9 us -> none  [the longest x1 5.74 us: middle(): jnp.dot(normed, whole(up_halves), preferred_element_type=jnp.float32)]
    reduce_sum x6 -> x4, other arithmetic: 11.6 us -> 1.49 us  [the longest x1 0.97 us: shards(): residual = jnp.mean(shifted.astype(jnp.float32), axis=1).reshape(256, PART)]
    gather x3 -> x0, local copies, waits for them, and re-layouts: 9.02 us -> none  [the longest x1 6.39 us: middle(): normed = jnp.take(normed, (jnp.arange(4) - row) % 4, axis=0)]
  transfers between devices with their start and end apart: 19 -> 15, of which waited for: 6 -> 8; matrix products, arithmetic and copies ran while one was open for 19% -> 11% of each run, Pallas kernels for 0% -> 9%
where the time goes in v2:
time: 218 us; the launch traced here: 217 us
  waiting for transfers between devices  69.6 us (32%)
  starting transfers between devices  42.5 us (19%)
  blocking collectives  42 us (19%)
  Pallas kernels  23.5 us (11%)
  local copies, waits for them, and re-layouts  20.1 us (9%)
  other arithmetic  14.4 us (7%)
  between operations  3.55 us (2%)
    all_to_all x2, waiting for transfers between devices, fetch(): lax.all_to_all(spread, YX, 0, 0, tiled=True).reshape(-1, mine.shape[-1])  39 us
    ppermute x11, starting transfers between devices, shift(): lax.ppermute(value, axis, [(i, (i + by) % size) for i in range(size)])  28.5 us
    ppermute x11, waiting for transfers between devices, shift(): lax.ppermute(value, axis, [(i, (i + by) % size) for i in range(size)])  25.1 us
    all_to_all x1, blocking collectives, shards(): packet = lax.all_to_all(packet, COL, 0, 0, tiled=True).astype(jnp.float32)  17 us
    pallas_call x1, Pallas kernels, hidden_mean(): pl.pallas_call(hidden_kernel, in_specs=[pl.BlockSpec(memory_space=pltpu.S...  16 us
    all_to_all x1, blocking collectives, shards(): lax.all_to_all(jnp.broadcast_to(piece[None], (32, 12, PART)), COL, 0, 0,...  12.7 us
    all_gather x1, blocking collectives, shards(): sums = jnp.sum(lax.all_gather(sums, 'row'), axis=0)  12.3 us
    all_to_all x2, starting transfers between devices, fetch(): lax.all_to_all(spread, YX, 0, 0, tiled=True).reshape(-1, mine.shape[-1])  11.5 us
  transfers between devices with their start and end apart: 15, of which 8 were waited for; matrix products, arithmetic and copies ran while one was open for 11% of the time, Pallas kernels for 9%

profile of v2, /device:TPU:1, one launch (start us, length us, event | category | flops | bytes accessed | tf_op | source)
XLA Modules:
  0.0 216.8 jit_solution(9690324279382928753)
XLA Ops:
  3.8 5.5 %collective-permute-done.5 = bf16[48,2048]{1,0:T(8,128)(2,1)S(1)} collective-permute-done((bf16[48,2048]{1,0:T(8,128)(2,1)S(1)}, bf16[48,2048]{1,0:T(8,128)(2,1)S(1)}, u32[]{:S(2)}, u32[]{:S(2)}) %collective-permute-start.5) | collective-permute-done | bytes 196640 | tf_op jit(solution)/shard_map/ppermute | solution.py:187
  9.3 2.1 broadcast_in_dim.16
  11.4 7.4 %all-to-all-start = ((bf16[16,48,2048]{2,1,0:T(8,128)(2,1)}), bf16[16,48,2048]{2,1,0:T(8,128)(2,1)}, u32[]{:S(2)}, u32[]{:S(2)}) async-start(bf16[16,48,2048]{2,1,0:T(8,128)(2,1)} %broadcast_in_dim.16), calls=%async_computation | async-start | bytes 6291456 | tf_op jit(solution)/shard_map/all_to_all | solution.py:192
  21.0 6.1 %collective-permute-start = (bf16[2,576,384]{2,1,0:T(8,128)(2,1)S(1)}, bf16[2,576,384]{2,1,0:T(8,128)(2,1)S(1)}, u32[]{:S(2)}, u32[]{:S(2)}) collective-permute-start(bf16[2,576,384]{2,1,0:T(8,128)(2,1)S(1)} %maximum_maximum_fusion.own), channel_id=1, source_target_pairs={{0,96},{32,0},{64,32},{96,64},{1,97},{33,1},{65,33},{97,65},{2,98}... | collective-permute-start | bytes 2654216 | tf_op jit(solution)/shard_map/ppermute | solution.py:19
  29.2 34.6 %all-to-all-done = bf16[16,48,2048]{2,1,0:T(8,128)(2,1)} async-done(((bf16[16,48,2048]{2,1,0:T(8,128)(2,1)}), bf16[16,48,2048]{2,1,0:T(8,128)(2,1)}, u32[]{:S(2)}, u32[]{:S(2)}) %all-to-all-start) | async-done | bytes 3145760 | tf_op jit(solution)/shard_map/all_to_all | solution.py:192
  63.8 2.4 %collective-permute-start.6 = (bf16[768,2048]{1,0:T(8,128)(2,1)}, bf16[768,2048]{1,0:T(8,128)(2,1)}, u32[]{:S(2)}, u32[]{:S(2)}) collective-permute-start(bf16[768,2048]{1,0:T(8,128)(2,1)} %bitcast.39.own), channel_id=1, source_target_pairs={{0,128},{128,0},{1,129},{129,1},{2,130},{130,2},{3,131},{131,3},{4... | collective-permute-start | bytes 9437192 | tf_op jit(solution)/shard_map/ppermute | solution.py:19
  67.2 7.7 %collective-permute-start.3 = (bf16[576,384]{1,0:T(8,128)(2,1)}, bf16[576,384]{1,0:T(8,128)(2,1)S(1)}, u32[]{:S(2)}, u32[]{:S(2)}) collective-permute-start(bf16[576,384]{1,0:T(8,128)(2,1)} %slice_bitcast_fusion), channel_id=1, source_target_pairs={{0,96},{32,0},{64,32},{96,64},{1,97},{33,1},{65,33},{97,65},{2,98}... | collective-permute-start | bytes 1327112 | tf_op jit(solution)/shard_map/ppermute | solution.py:19
  76.2 4.1 %all-to-all-start.1 = ((bf16[16,32,1536]{2,1,0:T(8,128)(2,1)}), bf16[16,32,1536]{2,1,0:T(8,128)(2,1)S(1)}, u32[]{:S(2)}, u32[]{:S(2)}) async-start(bf16[16,32,1536]{2,1,0:T(8,128)(2,1)} %broadcast_in_dim.17), calls=%async_computation.1 | async-start | bytes 3145728 | tf_op jit(solution)/shard_map/all_to_all | solution.py:192
  85.0 5.7 %collective-permute-done.3.far_bottom = bf16[576,384]{1,0:T(8,128)(2,1)S(1)} collective-permute-done((bf16[576,384]{1,0:T(8,128)(2,1)}, bf16[576,384]{1,0:T(8,128)(2,1)S(1)}, u32[]{:S(2)}, u32[]{:S(2)}) %collective-permute-start.3) | collective-permute-done | bytes 442400 | tf_op jit(solution)/shard_map/ppermute | solution.py:19
  91.3 7.7 %collective-permute-done.2.far_top = bf16[576,384]{1,0:T(8,128)(2,1)S(1)} collective-permute-done((bf16[576,384]{1,0:T(8,128)(2,1)S(1)}, bf16[576,384]{1,0:T(8,128)(2,1)S(1)}, u32[]{:S(2)}, u32[]{:S(2)}) %collective-permute-start.2) | collective-permute-done | bytes 442400 | tf_op jit(solution)/shard_map/ppermute | solution.py:19
  100.4 4.4 %all-to-all-done.1 = bf16[16,32,1536]{2,1,0:T(8,128)(2,1)S(1)} async-done(((bf16[16,32,1536]{2,1,0:T(8,128)(2,1)}), bf16[16,32,1536]{2,1,0:T(8,128)(2,1)S(1)}, u32[]{:S(2)}, u32[]{:S(2)}) %all-to-all-start.1) | async-done | bytes 1572896 | tf_op jit(solution)/shard_map/all_to_all | solution.py:192
  108.4 1.5 fusion.22
  113.4 1.5 fusion.23
  117.6 1.9 copy.25
  121.8 4.0 %shard_map.122.normed = bf16[1024,1536]{1,0:T(8,128)(2,1)S(1)} custom-call(s32[2]{0:T(128)S(1)} %pad_add_fusion.place, bf16[2,576,384]{2,1,0:T(8,128)(2,1)S(1)} %maximum_maximum_fusion.own, bf16[2,576,384]{2,1,0:T(8,128)(2,1)S(1)} %copy-done.2, bf16[2,576,384]{2,1,0:T(8,128)(2,1)} %collective-permute-done.1.before, bf16[576,384]{1,0:T(8,128)(2,1)S(1)} %copy-done.4, ...), custom_call_target="tpu_custom_call" | custom-call | flops 25165824 | bytes 6291456 | tf_op jit(solution)/shard_map/pallas_call | solution.py:42
  125.8 16.0 %shard_map.123.hidden = bf16[256,1024]{1,0:T(8,128)(2,1)S(1)} custom-call(s32[2]{0:T(128)S(1)} %pad_add_fusion.place, bf16[1024,1536]{1,0:T(8,128)(2,1)S(1)} %shard_map.122.normed, bf16[768,2048]{1,0:T(8,128)(2,1)} %bitcast.39.own, bf16[768,2048]{1,0:T(8,128)(2,1)} %collective-permute-done.6.other), custom_call_target="tpu_custom_call" | custom-call | flops 6442450944 | bytes 10485760 | tf_op jit(solution)/shard_map/pallas_call | solution.py:102
  141.8 3.4 %shard_map.124 = (f32[256,384]{1,0:T(8,128)S(1)}, bf16[256,384]{1,0:T(8,128)(2,1)S(1)}, bf16[256,384]{1,0:T(8,128)(2,1)S(1)}, bf16[256,384]{1,0:T(8,128)(2,1)S(1)}) custom-call(s32[2]{0:T(128)S(1)} %pad_add_fusion.place, bf16[256,1024]{1,0:T(8,128)(2,1)S(1)} %shard_map.123.hidden, bf16[512,1536]{1,0:T(8,128)(2,1)S(1)} %bitcast.125, ...), custom_call_target="tpu_custom_call" | custom-call | flops 805306368 | bytes 5242880 | tf_op jit(solution)/shard_map/pallas_call | solution.py:148
  147.7 1.9 collective-permute-start.8
  150.0 9.7 %collective-permute-done.10 = bf16[256,384]{1,0:T(8,128)(2,1)S(1)} collective-permute-done((bf16[256,384]{1,0:T(8,128)(2,1)S(1)}, bf16[256,384]{1,0:T(8,128)(2,1)S(1)}, u32[]{:S(2)}, u32[]{:S(2)}) %collective-permute-start.10) | collective-permute-done | bytes 196640 | tf_op jit(solution)/shard_map/ppermute | solution.py:19
  161.1 12.3 %all-gather.1 = f32[4,5,256]{2,1,0:T(8,128)S(1)} all-gather(f32[1,5,256]{2,1,0:T(8,128)S(1)} %bitcast.131), channel_id=2, replica_groups=mesh['group'=2,'row'=4,'zl'=2,'y'=4,'x'=4] {'row'}, dimensions={0}, use_global_device_ids=true | all-gather | bytes 25600 | tf_op jit(solution)/shard_map/all_gather | solution.py:253
  174.7 3.6 %collective-permute-start.11 = (bf16[384,384]{1,0:T(8,128)(2,1)S(1)}, bf16[384,384]{1,0:T(8,128)(2,1)S(1)}, u32[]{:S(2)}, u32[]{:S(2)}) collective-permute-start(bf16[384,384]{1,0:T(8,128)(2,1)S(1)} %fusion.12), channel_id=1, source_target_pairs={{0,128},{128,0},{1,129},{129,1},{2,130},{130,2},{3,131},{131,3},{4... | collective-permute-start | bytes 884744 | tf_op jit(solution)/shard_map/ppermute | solution.py:19
  179.9 17.0 %all_to_all.20 = bf16[32,14,384]{2,1,0:T(8,128)(2,1)S(1)} all-to-all(bf16[32,14,384]{2,1,0:T(8,128)(2,1)S(1)} %pad_maximum_fusion), channel_id=1, replica_groups=mesh['group'=2,'row'=4,'zl'=2,'y'=4,'x'=4] {'zl','y','x'}, dimensions={0} | all-to-all | bytes 688128 | tf_op jit(solution)/shard_map/all_to_all | solution.py:282
  197.1 12.7 %all_to_all.21 = bf16[32,12,384]{2,1,0:T(8,128)(2,1)S(1)} all-to-all(bf16[32,12,384]{2,1,0:T(8,128)(2,1)S(1)} %broadcast_in_dim.25), channel_id=1, replica_groups=mesh['group'=2,'row'=4,'zl'=2,'y'=4,'x'=4] {'zl','y','x'}, dimensions={0} | all-to-all | bytes 589824 | tf_op jit(solution)/shard_map/all_to_all | solution.py:286
  209.9 2.8 %collective-permute-start.12 = (bf16[384,384]{1,0:T(8,128)(2,1)S(1)}, bf16[384,384]{1,0:T(8,128)(2,1)S(1)}, u32[]{:S(2)}, u32[]{:S(2)}) collective-permute-start(bf16[384,384]{1,0:T(8,128)(2,1)S(1)} %reshape.146), channel_id=1, source_target_pairs={{0,128},{128,0},{1,129},{129,1},{2,130},{130,2},{3,131},{131,3},{4... | collective-permute-start | bytes 884744 | tf_op jit(solution)/shard_map/ppermute | solution.py:19
  (127 shorter events, 37.3 us)
Async XLA Ops:
  0.6 149.0 %copy-start = (bf16[768,384]{1,0:T(8,128)(2,1)S(1)}, bf16[768,384]{1,0:T(8,128)(2,1)}, u32[]{:S(2)}) copy-start(bf16[768,384]{1,0:T(8,128)(2,1)} %param.20) | copy-start | bytes 1769476
  2.5 6.8 %collective-permute-start.5 = (bf16[48,2048]{1,0:T(8,128)(2,1)S(1)}, bf16[48,2048]{1,0:T(8,128)(2,1)S(1)}, u32[]{:S(2)}, u32[]{:S(2)}) collective-permute-start(bf16[48,2048]{1,0:T(8,128)(2,1)S(1)} %constant_dynamic-update-slice_fusion), channel_id=1, source_target_pairs={{0,16},{144,128},{1,17},{145,129},{2,18},{146,130},{3,19},{147,131... | collective-permute-start | bytes 589832 | tf_op jit(solution)/shard_map/ppermute | solution.py:187
  11.4 52.4 %all-to-all-start = ((bf16[16,48,2048]{2,1,0:T(8,128)(2,1)}), bf16[16,48,2048]{2,1,0:T(8,128)(2,1)}, u32[]{:S(2)}, u32[]{:S(2)}) async-start(bf16[16,48,2048]{2,1,0:T(8,128)(2,1)} %broadcast_in_dim.16), calls=%async_computation | async-start | bytes 6291456 | tf_op jit(solution)/shard_map/all_to_all | solution.py:192
  19.9 8.5 %copy-start.18 = (bf16[384]{0:T(512)(128)(2,1)S(1)}, bf16[384]{0:T(512)(128)(2,1)}, u32[]{:S(2)}) copy-start(bf16[384]{0:T(512)(128)(2,1)} %param.15) | copy-start | bytes 2308
  21.0 45.3 %collective-permute-start = (bf16[2,576,384]{2,1,0:T(8,128)(2,1)S(1)}, bf16[2,576,384]{2,1,0:T(8,128)(2,1)S(1)}, u32[]{:S(2)}, u32[]{:S(2)}) collective-permute-start(bf16[2,576,384]{2,1,0:T(8,128)(2,1)S(1)} %maximum_maximum_fusion.own), channel_id=1, source_target_pairs={{0,96},{32,0},{64,32},{96,64},{1,97},{33,1},{65,33},{97,65},{2,98}... | collective-permute-start | bytes 2654216 | tf_op jit(solution)/shard_map/ppermute | solution.py:19
  27.1 53.2 %collective-permute-start.1 = (bf16[2,576,384]{2,1,0:T(8,128)(2,1)S(1)}, bf16[2,576,384]{2,1,0:T(8,128)(2,1)}, u32[]{:S(2)}, u32[]{:S(2)}) collective-permute-start(bf16[2,576,384]{2,1,0:T(8,128)(2,1)S(1)} %maximum_maximum_fusion.own), channel_id=1, source_target_pairs={{0,32},{32,64},{64,96},{96,0},{1,33},{33,65},{65,97},{97,1},{2,34}... | collective-permute-start | bytes 2654216 | tf_op jit(solution)/shard_map/ppermute | solution.py:19
  27.1 39.1 %collective-permute-start.4 = (bf16[32,1536]{1,0:T(8,128)(2,1)S(1)}, bf16[32,1536]{1,0:T(8,128)(2,1)S(1)}, u32[]{:S(2)}, u32[]{:S(2)}) collective-permute-start(bf16[32,1536]{1,0:T(8,128)(2,1)S(1)} %copy-done.14), channel_id=1, source_target_pairs={{0,16},{144,128},{1,17},{145,129},{2,18},{146,130},{3,19},{147,131... | collective-permute-start | bytes 294920 | tf_op jit(solution)/shard_map/ppermute | solution.py:187
  28.5 47.7 %copy-start.10 = (bf16[1,32,768]{2,1,0:T(8,128)(2,1)}, bf16[1,32,768]{2,1,0:T(8,128)(2,1)S(1)}, u32[]{:S(2)}) copy-start(bf16[1,32,768]{2,1,0:T(8,128)(2,1)S(1)} %maximum_bitcast_fusion.5) | copy-start | bytes 147460
  63.8 62.0 %collective-permute-start.6 = (bf16[768,2048]{1,0:T(8,128)(2,1)}, bf16[768,2048]{1,0:T(8,128)(2,1)}, u32[]{:S(2)}, u32[]{:S(2)}) collective-permute-start(bf16[768,2048]{1,0:T(8,128)(2,1)} %bitcast.39.own), channel_id=1, source_target_pairs={{0,128},{128,0},{1,129},{129,1},{2,130},{130,2},{3,131},{131,3},{4... | collective-permute-start | bytes 9437192 | tf_op jit(solution)/shard_map/ppermute | solution.py:19
  66.3 9.9 %copy-start.1 = (bf16[2,576,384]{2,1,0:T(8,128)(2,1)}, bf16[2,576,384]{2,1,0:T(8,128)(2,1)S(1)}, u32[]{:S(2)}) copy-start(bf16[2,576,384]{2,1,0:T(8,128)(2,1)S(1)} %collective-permute-done.after) | copy-start | bytes 2654212
  67.2 23.5 %collective-permute-start.3 = (bf16[576,384]{1,0:T(8,128)(2,1)}, bf16[576,384]{1,0:T(8,128)(2,1)S(1)}, u32[]{:S(2)}, u32[]{:S(2)}) collective-permute-start(bf16[576,384]{1,0:T(8,128)(2,1)} %slice_bitcast_fusion), channel_id=1, source_target_pairs={{0,96},{32,0},{64,32},{96,64},{1,97},{33,1},{65,33},{97,65},{2,98}... | collective-permute-start | bytes 1327112 | tf_op jit(solution)/shard_map/ppermute | solution.py:19
  76.2 28.6 %all-to-all-start.1 = ((bf16[16,32,1536]{2,1,0:T(8,128)(2,1)}), bf16[16,32,1536]{2,1,0:T(8,128)(2,1)S(1)}, u32[]{:S(2)}, u32[]{:S(2)}) async-start(bf16[16,32,1536]{2,1,0:T(8,128)(2,1)} %broadcast_in_dim.17), calls=%async_computation.1 | async-start | bytes 3145728 | tf_op jit(solution)/shard_map/all_to_all | solution.py:192
  81.4 17.6 %collective-permute-start.2 = (bf16[576,384]{1,0:T(8,128)(2,1)S(1)}, bf16[576,384]{1,0:T(8,128)(2,1)S(1)}, u32[]{:S(2)}, u32[]{:S(2)}) collective-permute-start(bf16[576,384]{1,0:T(8,128)(2,1)S(1)} %slice_bitcast_fusion.1), channel_id=1, source_target_pairs={{0,32},{32,64},{64,96},{96,0},{1,33},{33,65},{65,97},{97,1},{2,34}... | collective-permute-start | bytes 1327112 | tf_op jit(solution)/shard_map/ppermute | solution.py:19
  82.3 16.7 %copy-start.11 = (bf16[1,32,768]{2,1,0:T(8,128)(2,1)}, bf16[1,32,768]{2,1,0:T(8,128)(2,1)S(1)}, u32[]{:S(2)}) copy-start(bf16[1,32,768]{2,1,0:T(8,128)(2,1)S(1)} %maximum_bitcast_fusion.9) | copy-start | bytes 147460
  83.1 15.9 %copy-start.12 = (bf16[1,32,768]{2,1,0:T(8,128)(2,1)}, bf16[1,32,768]{2,1,0:T(8,128)(2,1)S(1)}, u32[]{:S(2)}) copy-start(bf16[1,32,768]{2,1,0:T(8,128)(2,1)S(1)} %maximum_bitcast_fusion.8) | copy-start | bytes 147460
  104.8 37.0 %collective-permute-start.7 = (bf16[512,1536]{1,0:T(8,128)(2,1)S(1)}, bf16[512,1536]{1,0:T(8,128)(2,1)}, u32[]{:S(2)}, u32[]{:S(2)}) collective-permute-start(bf16[512,1536]{1,0:T(8,128)(2,1)S(1)} %bitcast.124), channel_id=1, source_target_pairs={{0,128},{128,0},{1,129},{129,1},{2,130},{130,2},{3,131},{131,3},{4... | collective-permute-start | bytes 4718600 | tf_op jit(solution)/shard_map/ppermute | solution.py:19
  145.3 15.4 %copy-start.8 = (f32[32,8,384]{2,1,0:T(8,128)S(1)}, f32[32,8,384]{2,1,0:T(8,128)}, u32[]{:S(2)}) copy-start(f32[32,8,384]{2,1,0:T(8,128)} %get-tuple-element.25) | copy-start | bytes 1179652
  145.3 14.4 %collective-permute-start.10 = (bf16[256,384]{1,0:T(8,128)(2,1)S(1)}, bf16[256,384]{1,0:T(8,128)(2,1)S(1)}, u32[]{:S(2)}, u32[]{:S(2)}) collective-permute-start(bf16[256,384]{1,0:T(8,128)(2,1)S(1)} %get-tuple-element.13), channel_id=1, source_target_pairs={{0,96},{32,0},{64,32},{96,64},{1,97},{33,1},{65,33},{97,65},{2,98}... | collective-permute-start | bytes 589832 | tf_op jit(solution)/shard_map/ppermute | solution.py:19
  146.5 13.2 %collective-permute-start.9 = (bf16[256,384]{1,0:T(8,128)(2,1)S(1)}, bf16[256,384]{1,0:T(8,128)(2,1)S(1)}, u32[]{:S(2)}, u32[]{:S(2)}) collective-permute-start(bf16[256,384]{1,0:T(8,128)(2,1)S(1)} %get-tuple-element.12), channel_id=1, source_target_pairs={{0,32},{32,64},{64,96},{96,0},{1,33},{33,65},{65,97},{97,1},{2,34}... | collective-permute-start | bytes 589832 | tf_op jit(solution)/shard_map/ppermute | solution.py:19
  147.7 26.2 %copy-start.19 = (s32[32,1]{0,1:T(1,128)S(1)}, s32[32,1]{0,1:T(1,128)}, u32[]{:S(2)}) copy-start(s32[32,1]{0,1:T(1,128)} %param.21) | copy-start | bytes 388
  147.7 26.4 %copy-start.7 = (bf16[768,256]{1,0:T(8,128)(2,1)S(1)}, bf16[768,256]{1,0:T(8,128)(2,1)}, u32[]{:S(2)}) copy-start(bf16[768,256]{1,0:T(8,128)(2,1)} %copy.25) | copy-start | bytes 1179652
  147.7 12.9 %collective-permute-start.8 = (bf16[256,384]{1,0:T(8,128)(2,1)S(1)}, bf16[256,384]{1,0:T(8,128)(2,1)S(1)}, u32[]{:S(2)}, u32[]{:S(2)}) collective-permute-start(bf16[256,384]{1,0:T(8,128)(2,1)S(1)} %get-tuple-element.11), channel_id=1, source_target_pairs={{0,64},{32,96},{64,0},{96,32},{1,65},{33,97},{65,1},{97,33},{2,66}... | collective-permute-start | bytes 589832 | tf_op jit(solution)/shard_map/ppermute | solution.py:19
  174.7 4.9 %collective-permute-start.11 = (bf16[384,384]{1,0:T(8,128)(2,1)S(1)}, bf16[384,384]{1,0:T(8,128)(2,1)S(1)}, u32[]{:S(2)}, u32[]{:S(2)}) collective-permute-start(bf16[384,384]{1,0:T(8,128)(2,1)S(1)} %fusion.12), channel_id=1, source_target_pairs={{0,128},{128,0},{1,129},{129,1},{2,130},{130,2},{3,131},{131,3},{4... | collective-permute-start | bytes 884744 | tf_op jit(solution)/shard_map/ppermute | solution.py:19
  209.9 4.6 %collective-permute-start.12 = (bf16[384,384]{1,0:T(8,128)(2,1)S(1)}, bf16[384,384]{1,0:T(8,128)(2,1)S(1)}, u32[]{:S(2)}, u32[]{:S(2)}) collective-permute-start(bf16[384,384]{1,0:T(8,128)(2,1)S(1)} %reshape.146), channel_id=1, source_target_pairs={{0,128},{128,0},{1,129},{129,1},{2,130},{130,2},{3,131},{131,3},{4... | collective-permute-start | bytes 884744 | tf_op jit(solution)/shard_map/ppermute | solution.py:19
  (11 other events, 51.2 us)

commit v3 on v2

v3 whole, which is shorter than its diff:
```python
import jax
import jax.numpy as jnp
from jax import lax
from jax.experimental import pallas as pl
from jax.experimental.pallas import tpu as pltpu
from jax.sharding import Mesh, PartitionSpec as P

D = 1536
SW = 768
PART = 384
YX = ("y", "x")
COL = ("zl", "y", "x")
EVERY = ("group", "zl", "y", "x")
IMAGES = 2048
MIB = 1024 * 1024


def shift(value, axis, size, by):
    return lax.ppermute(value, axis, [(i, (i + by) % size) for i in range(size)])


def norm_kernel(place, own, after, before, far_top, far_bottom, gain, out):
    row, group = place[0], place[1]
    far = jnp.where(pl.program_id(0) < 2, far_top[...], far_bottom[...])
    pieces = [own[0], after[0], far, before[0]]
    pieces = [piece.astype(jnp.float32) for piece in pieces]
    total = sum(jnp.sum(piece, axis=1, keepdims=True) for piece in pieces)
    mean = total * (1.0 / D)
    pieces = [piece - mean for piece in pieces]
    square = sum(jnp.sum(piece * piece, axis=1, keepdims=True) for piece in pieces)
    scale = lax.rsqrt(square * (1.0 / D) + 1e-06)
    for j, piece in enumerate(pieces):
        block = lax.rem(row + j, 4)
        source = pl.multiple_of(block * PART, PART)
        target = pl.multiple_of(lax.rem(block + 2 * group, 4) * PART, PART)
        value = piece * scale * gain[:, pl.ds(source, PART)]
        out[:, pl.ds(target, PART)] = value.astype(jnp.bfloat16)


def norm(place, own, after, before, far_top, far_bottom, gain):
    piece = pl.BlockSpec((1, 256, PART), lambda b: (b // 2, b % 2, 0))
    return pl.pallas_call(
        norm_kernel,
        grid=(4,),
        in_specs=[
            pl.BlockSpec(memory_space=pltpu.SMEM),
            piece,
            piece,
            piece,
            pl.BlockSpec((256, PART), lambda b: (jnp.minimum(b, 1), 0)),
            pl.BlockSpec((256, PART), lambda b: (jnp.maximum(b - 2, 0), 0)),
            pl.BlockSpec((1, D), lambda b: (0, 0)),
        ],
        out_specs=pl.BlockSpec((256, D), lambda b: (b, 0)),
        out_shape=jax.ShapeDtypeStruct((1024, D), jnp.bfloat16),
        compiler_params=pltpu.CompilerParams(vmem_limit_bytes=24 * MIB),
        cost_estimate=pl.CostEstimate(
            flops=30 * 10**9, bytes_accessed=4 * 1024 * D, transcendentals=0
        ),
    )(place, own, after, before, far_top, far_bottom, gain)


SPANS = ((0, 512), (1024, 512), (512, 512), (1536, 512), (2048, 1024))


def branch_kernel(place, normed, *refs):
    row, group, y, x = place[0], place[1], place[2], place[3]
    sources = (refs[:4], refs[4:8])
    part, away1, away2, away3 = refs[8:12]
    weights, hidden, down, sems = refs[12:]

    def copy(side, k, span, along_y):
        start, width = SPANS[span]
        columns = pl.ds(start, width)
        block = weights.at[side]
        if along_y:
            block = block.at[lax.rem(y + k, 4), :, :, columns]
        else:
            block = block.at[:, lax.rem(x + k, 4), :, columns]
        return pltpu.make_async_copy(
            sources[side][k].at[:, :, columns], block, sems.at[side, k, span]
        )

    def start_all(side, along_y, span):
        for k in range(4):
            copy(side, k, span, along_y).start()

    def wait_all(spans):
        for span in spans:
            for side in (0, 1):
                for k in range(4):
                    copy(side, k, span, True).wait()

    for span in range(5):
        for side in (0, 1):
            along = group == side

            @pl.when(along)
            def _():
                start_all(side, True, span)

            @pl.when(jnp.logical_not(along))
            def _():
                start_all(side, False, span)

    def project(kind, n):
        start = kind * 1024 + n * 256
        return sum(
            jnp.dot(
                normed[:, 768 * side : 768 * side + 768],
                weights[side, :, :, :, start : start + 256].reshape(768, 256),
                preferred_element_type=jnp.float32,
            )
            for side in (0, 1)
        )

    for n in range(4):
        if n == 0:
            wait_all((0, 1))
        if n == 2:
            wait_all((2, 3))
        gate = project(0, n)
        upward = project(1, n)
        value = gate * upward / (1.0 + jnp.exp(-gate))
        value = jnp.sum(value.reshape(32, 4, 8, 256), axis=1).reshape(256, 256) * 0.25
        target = pl.multiple_of(lax.rem(n + 2 * group, 4) * 256, 256)
        hidden[:, pl.ds(target, 256)] = value.astype(jnp.bfloat16)

    wait_all((4,))

    def unpack(c, carry):
        rows = pl.multiple_of(c * 32, 32)
        for side in (0, 1):
            half = weights.at[side, c // 4, lax.rem(c, 4)]
            down[pl.ds(side * 512 + rows, 32), 0:1024] = half[0:32, 2048:3072]
            tail = half[32:48, 2048:3072]
            down[pl.ds(side * 512 + rows, 16), 1024:1536] = tail[:, :512]
            down[pl.ds(side * 512 + rows + 16, 16), 1024:1536] = tail[:, 512:]
        return carry

    lax.fori_loop(0, 16, unpack, 0)
    for j, out in ((2, away2), (1, away1), (3, away3), (0, part)):
        start = pl.multiple_of(lax.rem(row + j, 4) * PART, PART)
        value = jnp.dot(
            hidden[...], down[:, pl.ds(start, PART)], preferred_element_type=jnp.float32
        )
        out[...] = value.astype(out.dtype)


def branch(place, normed, own, other):
    narrow = jax.ShapeDtypeStruct((256, PART), jnp.bfloat16)
    vmem = pl.BlockSpec(memory_space=pltpu.VMEM)
    return pl.pallas_call(
        branch_kernel,
        in_specs=[pl.BlockSpec(memory_space=pltpu.SMEM), vmem]
        + [pl.BlockSpec(memory_space=pl.ANY)] * 8,
        out_specs=[vmem] * 4,
        out_shape=[jax.ShapeDtypeStruct((256, PART), jnp.float32), narrow, narrow, narrow],
        scratch_shapes=[
            pltpu.VMEM((2, 4, 4, 48, 3072), jnp.bfloat16),
            pltpu.VMEM((256, 1024), jnp.bfloat16),
            pltpu.VMEM((1024, D), jnp.bfloat16),
            pltpu.SemaphoreType.DMA((2, 4, 5)),
        ],
        compiler_params=pltpu.CompilerParams(vmem_limit_bytes=40 * MIB),
        cost_estimate=pl.CostEstimate(
            flops=2 * 1024 * D * 2048, bytes_accessed=10 * MIB, transcendentals=1024 * 1024
        ),
    )(place, normed, *own, *other)


def gather_kernel(place, *refs):
    sources, out = refs[:4], refs[4]
    position = jnp.where(place[1] == 0, place[3], place[2])
    for k, source in enumerate(sources):
        out[lax.rem(position + k, 4)] = source[...]


def gather(place, blocks):
    vmem = pl.BlockSpec(memory_space=pltpu.VMEM)
    return pl.pallas_call(
        gather_kernel,
        in_specs=[pl.BlockSpec(memory_space=pltpu.SMEM)] + [vmem] * 4,
        out_specs=vmem,
        out_shape=jax.ShapeDtypeStruct((4,) + blocks[0].shape, jnp.bfloat16),
        compiler_params=pltpu.CompilerParams(vmem_limit_bytes=16 * MIB),
        cost_estimate=pl.CostEstimate(flops=0, bytes_accessed=3 * MIB, transcendentals=0),
    )(place, *blocks)


def student_kernel(place, own, after, before, far_top, far_bottom, weight, pupils, head, gathered):
    row = place[0]
    pieces = (
        (own[0], own[1]),
        (after[0], after[1]),
        (far_top[...], far_bottom[...]),
        (before[0], before[1]),
    )
    for j, piece in enumerate(pieces):
        for i, half in enumerate(piece):
            rows = (2 * j + i) * 32
            gathered[rows : rows + 32, 0:PART] = half[0:32]
            gathered[rows : rows + 32, PART:SW] = half[32:64]
    target = lax.broadcasted_iota(jnp.int32, (256, 256), 0)
    source = lax.broadcasted_iota(jnp.int32, (256, 256), 1)
    image, patch = target // 8, lax.rem(target, 8)
    place_of = lax.rem(patch - 2 * row + 8, 8) * 32 + image
    order = jnp.where(source == place_of, 1.0, 0.0).astype(jnp.bfloat16)
    value = jnp.dot(order, gathered[...], preferred_element_type=jnp.float32)
    value = value.astype(jnp.bfloat16)
    pupils[...] = value
    head[...] = jnp.dot(value, weight[...], preferred_element_type=jnp.float32)


def student(place, own, after, before, far_top, far_bottom, weight):
    piece = pl.BlockSpec((2, 64, PART), lambda b: (0, 8, 0))
    half = pl.BlockSpec((64, PART), lambda b: (8, 0))
    return pl.pallas_call(
        student_kernel,
        grid=(1,),
        in_specs=[
            pl.BlockSpec(memory_space=pltpu.SMEM),
            piece,
            piece,
            piece,
            half,
            half,
            pl.BlockSpec((SW, PART), lambda b: (0, 0)),
        ],
        out_specs=[
            pl.BlockSpec((256, SW), lambda b: (0, 0)),
            pl.BlockSpec((256, PART), lambda b: (0, 0)),
        ],
        out_shape=[
            jax.ShapeDtypeStruct((256, SW), jnp.bfloat16),
            jax.ShapeDtypeStruct((256, PART), jnp.float32),
        ],
        scratch_shapes=[pltpu.VMEM((256, SW), jnp.bfloat16)],
        compiler_params=pltpu.CompilerParams(vmem_limit_bytes=16 * MIB),
        cost_estimate=pl.CostEstimate(
            flops=2 * 256 * SW * 640, bytes_accessed=2 * MIB, transcendentals=0
        ),
    )(place, own, after, before, far_top, far_bottom, weight)


def shards(
    teacher_tokens,
    view_index,
    aug_embed,
    norm_gain,
    layer_scale,
    gate_weight,
    up_weight,
    down_weight,
    student_tokens,
    head_weight,
    owner,
):
    group, row, zl = lax.axis_index("group"), lax.axis_index("row"), lax.axis_index("zl")
    images = teacher_tokens.shape[0]
    place = jnp.stack([row, group, lax.axis_index("y"), lax.axis_index("x")]).astype(jnp.int32)

    down = jnp.concatenate(
        [
            down_weight[:, :1024],
            jnp.concatenate([down_weight[:16, 1024:], down_weight[16:, 1024:]], axis=1),
        ],
        axis=0,
    )
    block = jnp.concatenate([gate_weight, up_weight, down], axis=1)
    twin = lax.ppermute(block, ("group", "zl"), [(0, 1), (3, 2)])
    block = jnp.where(group == zl, block, twin)
    def collect(value, first):
        pieces = [value]
        for by in (-1, 2, 1):
            pairs = []
            for y in range(4):
                for x in range(4):
                    along_x = (y, (x + by) % 4)
                    along_y = ((y + by) % 4, x)
                    for core, (to_y, to_x) in enumerate(
                        (along_x, along_y) if first else (along_y, along_x)
                    ):
                        pairs.append((core * 16 + y * 4 + x, core * 16 + to_y * 4 + to_x))
            pieces.append(lax.ppermute(value, ("group", "y", "x"), pairs))
        return pieces

    weights_own = collect(gather(place, collect(block, True)), False)
    weights_other = [shift(piece, "group", 2, 1) for piece in weights_own]

    kinds = aug_embed.shape[0]
    kind_table = (
        view_index.reshape(-1)[:, None] == jnp.arange(kinds, dtype=jnp.int32)[None, :]
    ).astype(jnp.bfloat16)
    embedded = jnp.dot(kind_table, aug_embed, preferred_element_type=jnp.float32).reshape(
        images, 4, 1, PART
    )
    shifted = (teacher_tokens.astype(jnp.float32) + embedded).astype(jnp.bfloat16)
    residual = jnp.mean(shifted.astype(jnp.float32), axis=1).reshape(256, PART)
    quarters = [student_tokens[:, PART * c : PART * c + PART] for c in range(4)]
    own = jnp.concatenate(
        [
            shifted.reshape(2, 512, PART),
            jnp.stack([jnp.concatenate(quarters[:2]), jnp.concatenate(quarters[2:])]),
        ],
        axis=1,
    )
    own, twin = lax.optimization_barrier((own, twin))
    before = shift(own, "row", 4, 1)
    after = shift(own, "row", 4, -1)
    far_top = shift(before[0], "row", 4, 1)
    far_bottom = shift(after[1], "row", 4, -1)

    gain = norm_gain.astype(jnp.float32).reshape(1, D)
    normed = norm(place, own, after, before, far_top, far_bottom, gain)
    part, *away = branch(place, normed, weights_own, weights_other)
    held = (own, after, before, far_top, far_bottom)
    away, held = lax.optimization_barrier((away, held))
    got = [shift(away[j - 1], "row", 4, j) for j in (2, 1, 3)]
    pupils, head = student(place, *held, head_weight)

    averaged = part + sum(piece.astype(jnp.float32) for piece in got)
    target = (residual + layer_scale.astype(jnp.float32) * averaged).astype(jnp.bfloat16)
    target = target.astype(jnp.float32)
    sums = jnp.stack(
        [
            jnp.sum(head, axis=1),
            jnp.sum(head * head, axis=1),
            jnp.sum(target, axis=1),
            jnp.sum(head * target, axis=1),
            jnp.sum(target * target, axis=1),
        ]
    )
    sums = jnp.sum(lax.all_gather(sums, "row"), axis=0)
    center = sums[0] / D
    spread = sums[1] / D - center * center
    scaler = lax.rsqrt(spread + 1e-05)
    pred_square = scaler * scaler * (sums[1] - D * center * center)
    pred_target = scaler * (sums[3] - center * sums[2])
    diff_square = pred_square - 2.0 * pred_target + sums[4]
    mean_first = -2.0 / IMAGES * sums[2] / D
    mean_second = 2.0 / IMAGES * (pred_square - pred_target) / D
    pred = (head - center[:, None]) * scaler[:, None]
    dpred = 2.0 / IMAGES * (pred - target)
    dz = (
        scaler[:, None] * (dpred - mean_first[:, None] - pred * mean_second[:, None])
    ).astype(jnp.bfloat16)
    errors = jnp.sum(diff_square.reshape(images, 8), axis=1) / (8 * D)
    mine = owner == jnp.arange(32, dtype=jnp.int32)[None, :]
    loss = jnp.sum(jnp.where(mine, errors[:, None], 0.0), axis=0)
    loss_high = loss.astype(jnp.bfloat16)
    loss_low = (loss - loss_high.astype(jnp.float32)).astype(jnp.bfloat16)

    grad = lax.dot_general(pupils, dz, (((0,), (0,)), ((), ())), preferred_element_type=jnp.float32)
    grad = grad.reshape(2, PART, PART)
    keep = lax.dynamic_index_in_dim(grad, group, 0, keepdims=False)
    give = lax.dynamic_index_in_dim(grad, 1 - group, 0, keepdims=False)
    half = keep + shift(give.astype(jnp.bfloat16), "group", 2, 1).astype(jnp.float32)
    half = half.astype(jnp.bfloat16).reshape(32, 12, PART)
    note = jnp.stack([loss_high, loss_low], axis=1)[:, :, None]
    note = jnp.broadcast_to(note, (32, 2, PART))
    packet = jnp.concatenate([half, note], axis=1)
    packet = lax.all_to_all(packet, COL, 0, 0, tiled=True).astype(jnp.float32)
    summed = jnp.sum(packet, axis=0)
    owner_loss = summed[12, :1] + summed[13, :1]
    piece = summed[:12].astype(jnp.bfloat16)
    piece = lax.all_to_all(jnp.broadcast_to(piece[None], (32, 12, PART)), COL, 0, 0, tiled=True)
    piece = piece.reshape(PART, PART)
    other = shift(piece, "group", 2, 1)
    head_grad = jnp.concatenate(
        [jnp.where(group == 0, piece, other), jnp.where(group == 0, other, piece)], axis=0
    ).astype(jnp.float32)
    return (head_grad, owner_loss)


def solution(mesh):
    fine = Mesh(mesh.devices.reshape(2, 4, 2, 4, 4), ("group", "row", "zl", "y", "x"))
    return jax.shard_map(
        shards,
        mesh=fine,
        in_specs=(
            P(EVERY, None, None, "row"),
            P(EVERY, None),
            P(None, "row"),
            P(),
            P("row"),
            P(COL, "row"),
            P(COL, "row"),
            P(("row",) + COL, None),
            P(EVERY, "row"),
            P(None, "row"),
            P(EVERY, None),
        ),
        out_specs=(P(None, "row"), P(EVERY)),
        check_vma=False,
    )
```

time: 218 us -> 172 us (0.79)
  local copies, waits for them, and re-layouts: 20.1 us -> 7.01 us
  other arithmetic: 14.4 us -> 5.41 us
  starting transfers between devices: 42.5 us -> 33.6 us
  Pallas kernels: 23.5 us -> 16.9 us
  waiting for transfers between devices: 69.6 us -> 63.6 us
    all_to_all x2 -> x0, waiting for transfers between devices: 39 us -> none  [fetch(): lax.all_to_all(spread, YX, 0, 0, tiled=True).reshape(-1, mine.shape[-1])]
    ppermute x11 -> x13, waiting for transfers between devices: 25.1 us -> 49.9 us  [shift(): lax.ppermute(value, axis, [(i, (i + by) % size) for i in range(size)])]
    pallas_call x1 -> x2, Pallas kernels: 16 us -> 2.18 us  [the longest x1 1.14 us: gather(): pl.pallas_call(gather_kernel, in_specs=[pl.BlockSpec(memory_space=pltpu.S...]
    all_to_all x2 -> x0, starting transfers between devices: 11.5 us -> none  [fetch(): lax.all_to_all(spread, YX, 0, 0, tiled=True).reshape(-1, mine.shape[-1])]
    ppermute x2 -> x7, waiting for transfers between devices: 5.49 us -> 13.7 us  [the longest x6 9.53 us: collect(): pieces.append(lax.ppermute(value, ('group', 'y', 'x'), pairs))]
    pallas_call x1, Pallas kernels: 3.42 us -> 11.4 us  [branch(): pl.pallas_call(branch_kernel, in_specs=[pl.BlockSpec(memory_space=pltpu.S...]
    unnamed x7 -> x0, other arithmetic: 6.93 us -> none
    ppermute x2 -> x7, starting transfers between devices: 2.56 us -> 8.72 us  [the longest x6 7.43 us: collect(): pieces.append(lax.ppermute(value, ('group', 'y', 'x'), pairs))]
  transfers between devices with their start and end apart: 15 -> 20, of which waited for: 8 -> 12; matrix products, arithmetic and copies ran while one was open for 11% -> 2% of each run, Pallas kernels for 9% -> 3%
where the time goes in v3:
time: 172 us
  waiting for transfers between devices  63.6 us (37%)
  blocking collectives  39.9 us (23%)
  starting transfers between devices  33.6 us (20%)
  Pallas kernels  16.9 us (10%)
  local copies, waits for them, and re-layouts  7.01 us (4%)
  other arithmetic  5.41 us (3%)
  between operations  3.44 us (2%)
  matrix products  1.77 us (1%)
    ppermute x13, waiting for transfers between devices, shift(): lax.ppermute(value, axis, [(i, (i + by) % size) for i in range(size)])  49.9 us
    ppermute x13, starting transfers between devices, shift(): lax.ppermute(value, axis, [(i, (i + by) % size) for i in range(size)])  24.9 us
    all_to_all x1, blocking collectives, shards(): packet = lax.all_to_all(packet, COL, 0, 0, tiled=True).astype(jnp.float32)  16 us
    all_to_all x1, blocking collectives, shards(): lax.all_to_all(jnp.broadcast_to(piece[None], (32, 12, PART)), COL, 0, 0,...  12.7 us
    pallas_call x1, Pallas kernels, branch(): pl.pallas_call(branch_kernel, in_specs=[pl.BlockSpec(memory_space=pltpu.S...  11.4 us
    all_gather x1, blocking collectives, shards(): sums = jnp.sum(lax.all_gather(sums, 'row'), axis=0)  11.2 us
    ppermute x6, waiting for transfers between devices, collect(): pieces.append(lax.ppermute(value, ('group', 'y', 'x'), pairs))  9.53 us
    ppermute x6, starting transfers between devices, collect(): pieces.append(lax.ppermute(value, ('group', 'y', 'x'), pairs))  7.43 us
  transfers between devices with their start and end apart: 20, of which 12 were waited for; matrix products, arithmetic and copies ran while one was open for 2% of the time, Pallas kernels for 3%

profile of v3, /device:TPU:1, one launch (start us, length us, event | category | flops | bytes accessed | tf_op | source)
XLA Modules:
  0.0 171.6 jit_solution(14254640617248784666)
XLA Ops:
  6.9 4.2 %collective-permute-done = bf16[48,3072]{1,0:T(8,128)(2,1)S(1)} collective-permute-done((bf16[48,3072]{1,0:T(8,128)(2,1)S(1)}, bf16[48,3072]{1,0:T(8,128)(2,1)S(1)}, u32[]{:S(2)}, u32[]{:S(2)}) %collective-permute-start) | collective-permute-done | bytes 294944 | tf_op jit(solution)/shard_map/ppermute | solution.py:271
  11.1 3.4 %collective-permute-start.2 = (bf16[2,576,384]{2,1,0:T(8,128)(2,1)S(1)}, bf16[2,576,384]{2,1,0:T(8,128)(2,1)S(1)}, u32[]{:S(2)}, u32[]{:S(2)}) collective-permute-start(bf16[2,576,384]{2,1,0:T(8,128)(2,1)S(1)} %maximum_maximum_fusion.own), channel_id=1, source_target_pairs={{0,32},{32,64},{64,96},{96,0},{1,33},{33,65},{65,97},{97,1},{2,34}... | collective-permute-start | bytes 2654216 | tf_op jit(solution)/shard_map/ppermute | solution.py:19
  14.6 3.0 %collective-permute-start.1 = (bf16[2,576,384]{2,1,0:T(8,128)(2,1)S(1)}, bf16[2,576,384]{2,1,0:T(8,128)(2,1)S(1)}, u32[]{:S(2)}, u32[]{:S(2)}) collective-permute-start(bf16[2,576,384]{2,1,0:T(8,128)(2,1)S(1)} %maximum_maximum_fusion.own), channel_id=1, source_target_pairs={{0,96},{32,0},{64,32},{96,64},{1,97},{33,1},{65,33},{97,65},{2,98}... | collective-permute-start | bytes 2654216 | tf_op jit(solution)/shard_map/ppermute | solution.py:19
  17.7 2.8 %collective-permute-start.5 = (bf16[48,3072]{1,0:T(8,128)(2,1)S(1)}, bf16[48,3072]{1,0:T(8,128)(2,1)S(1)}, u32[]{:S(2)}, u32[]{:S(2)}) collective-permute-start(bf16[48,3072]{1,0:T(8,128)(2,1)S(1)} %broadcast_select_fusion.refs_0_), channel_id=1, source_target_pairs={{0,3},{128,140},{1,0},{129,141},{2,1},{130,142},{3,2},{131,143},{4... | collective-permute-start | bytes 884744 | tf_op jit(solution)/shard_map/ppermute | solution.py:285
  21.6 5.7 %collective-permute-done.5.refs_1_ = bf16[48,3072]{1,0:T(8,128)(2,1)S(1)} collective-permute-done((bf16[48,3072]{1,0:T(8,128)(2,1)S(1)}, bf16[48,3072]{1,0:T(8,128)(2,1)S(1)}, u32[]{:S(2)}, u32[]{:S(2)}) %collective-permute-start.5) | collective-permute-done | bytes 294944 | tf_op jit(solution)/shard_map/ppermute | solution.py:285
  28.0 3.1 %collective-permute-done.7.refs_3_ = bf16[48,3072]{1,0:T(8,128)(2,1)} collective-permute-done((bf16[48,3072]{1,0:T(8,128)(2,1)S(1)}, bf16[48,3072]{1,0:T(8,128)(2,1)}, u32[]{:S(2)}, u32[]{:S(2)}) %collective-permute-start.7) | collective-permute-done | bytes 294944 | tf_op jit(solution)/shard_map/ppermute | solution.py:285
  32.3 2.5 %collective-permute-start.8 = (bf16[4,48,3072]{2,1,0:T(8,128)(2,1)S(1)}, bf16[4,48,3072]{2,1,0:T(8,128)(2,1)S(1)}, u32[]{:S(2)}, u32[]{:S(2)}) collective-permute-start(bf16[4,48,3072]{2,1,0:T(8,128)(2,1)S(1)} %shard_map.123.refs_0_), channel_id=1, source_target_pairs={{0,12},{128,131},{1,13},{129,128},{2,14},{130,129},{3,15},{131,130... | collective-permute-start | bytes 3538952 | tf_op jit(solution)/shard_map/ppermute | solution.py:285
  35.9 30.0 %collective-permute-done.2.before = bf16[2,576,384]{2,1,0:T(8,128)(2,1)S(1)} collective-permute-done((bf16[2,576,384]{2,1,0:T(8,128)(2,1)S(1)}, bf16[2,576,384]{2,1,0:T(8,128)(2,1)S(1)}, u32[]{:S(2)}, u32[]{:S(2)}) %collective-permute-start.2) | collective-permute-done | bytes 884768 | tf_op jit(solution)/shard_map/ppermute | solution.py:19
  66.1 3.6 %collective-permute-start.4 = (bf16[576,384]{1,0:T(8,128)(2,1)S(1)}, bf16[576,384]{1,0:T(8,128)(2,1)S(1)}, u32[]{:S(2)}, u32[]{:S(2)}) collective-permute-start(bf16[576,384]{1,0:T(8,128)(2,1)S(1)} %slice_bitcast_fusion), channel_id=1, source_target_pairs={{0,96},{32,0},{64,32},{96,64},{1,97},{33,1},{65,33},{97,65},{2,98}... | collective-permute-start | bytes 1327112 | tf_op jit(solution)/shard_map/ppermute | solution.py:19
  69.7 9.2 %collective-permute-done.3.far_top = bf16[576,384]{1,0:T(8,128)(2,1)S(1)} collective-permute-done((bf16[576,384]{1,0:T(8,128)(2,1)S(1)}, bf16[576,384]{1,0:T(8,128)(2,1)S(1)}, u32[]{:S(2)}, u32[]{:S(2)}) %collective-permute-start.3) | collective-permute-done | bytes 442400 | tf_op jit(solution)/shard_map/ppermute | solution.py:19
  78.9 1.8 %collective-permute-start.11 = (bf16[4,48,3072]{2,1,0:T(8,128)(2,1)S(1)}, bf16[4,48,3072]{2,1,0:T(8,128)(2,1)S(1)}, u32[]{:S(2)}, u32[]{:S(2)}) collective-permute-start(bf16[4,48,3072]{2,1,0:T(8,128)(2,1)S(1)} %shard_map.123.refs_0_), channel_id=1, source_target_pairs={{0,128},{128,0},{1,129},{129,1},{2,130},{130,2},{3,131},{131,3},{4... | collective-permute-start | bytes 3538952 | tf_op jit(solution)/shard_map/ppermute | solution.py:19
  81.3 3.3 %shard_map.122.normed = bf16[1024,1536]{1,0:T(8,128)(2,1)S(1)} custom-call(s32[4]{0:T(128)S(1)} %pad_add_fusion.place, bf16[2,576,384]{2,1,0:T(8,128)(2,1)S(1)} %maximum_maximum_fusion.own, bf16[2,576,384]{2,1,0:T(8,128)(2,1)S(1)} %collective-permute-done.1.after, bf16[2,576,384]{2,1,0:T(8,128)(2,1)S(1)} %collective-permute-done.2.before, ...), custom_call_target="tpu_custom_call" | custom-call | flops 30000001024 | bytes 6291456 | tf_op jit(solution)/shard_map/pallas_call | solution.py:42
  84.9 1.7 collective-permute-done.13.refs_6_
  86.5 1.7 collective-permute-done.14.refs_7_
  88.2 11.4 %shard_map.124 = (f32[256,384]{1,0:T(8,128)S(1)}, bf16[256,384]{1,0:T(8,128)(2,1)}, bf16[256,384]{1,0:T(8,128)(2,1)}, bf16[256,384]{1,0:T(8,128)(2,1)}) custom-call(s32[4]{0:T(128)S(1)} %pad_add_fusion.place, bf16[1024,1536]{1,0:T(8,128)(2,1)S(1)} %shard_map.122.normed, bf16[4,48,3072]{2,1,0:T(8,128)(2,1)S(1)} %shard_map.123.refs_0_, ...), custom_call_target="tpu_custom_call" | custom-call | flops 6442450944 | bytes 10485760 | tf_op jit(solution)/shard_map/pallas_call | solution.py:153
  100.4 2.3 %collective-permute-start.15 = (bf16[256,384]{1,0:T(8,128)(2,1)}, bf16[256,384]{1,0:T(8,128)(2,1)}, u32[]{:S(2)}, u32[]{:S(2)}) collective-permute-start(bf16[256,384]{1,0:T(8,128)(2,1)} %get-tuple-element.29), channel_id=1, source_target_pairs={{0,64},{32,96},{64,0},{96,32},{1,65},{33,97},{65,1},{97,33},{2,66}... | collective-permute-start | bytes 589832 | tf_op jit(solution)/shard_map/ppermute | solution.py:19
  102.7 3.6 %collective-permute-start.17 = (bf16[256,384]{1,0:T(8,128)(2,1)}, bf16[256,384]{1,0:T(8,128)(2,1)}, u32[]{:S(2)}, u32[]{:S(2)}) collective-permute-start(bf16[256,384]{1,0:T(8,128)(2,1)} %get-tuple-element.31), channel_id=1, source_target_pairs={{0,96},{32,0},{64,32},{96,64},{1,97},{33,1},{65,33},{97,65},{2,98}... | collective-permute-start | bytes 589832 | tf_op jit(solution)/shard_map/ppermute | solution.py:19
  109.5 5.9 %collective-permute-done.15 = bf16[256,384]{1,0:T(8,128)(2,1)} collective-permute-done((bf16[256,384]{1,0:T(8,128)(2,1)}, bf16[256,384]{1,0:T(8,128)(2,1)}, u32[]{:S(2)}, u32[]{:S(2)}) %collective-permute-start.15) | collective-permute-done | bytes 196640 | tf_op jit(solution)/shard_map/ppermute | solution.py:19
  117.7 11.2 %all-gather.1 = f32[4,5,256]{2,1,0:T(8,128)S(1)} all-gather(f32[1,5,256]{2,1,0:T(8,128)S(1)} %bitcast.49), channel_id=2, replica_groups=mesh['group'=2,'row'=4,'zl'=2,'y'=4,'x'=4] {'row'}, dimensions={0}, use_global_device_ids=true | all-gather | bytes 25600 | tf_op jit(solution)/shard_map/all_gather | solution.py:334
  129.0 1.6 fusion.10
  130.6 3.6 %collective-permute-start.18 = (bf16[384,384]{1,0:T(8,128)(2,1)S(1)}, bf16[384,384]{1,0:T(8,128)(2,1)S(1)}, u32[]{:S(2)}, u32[]{:S(2)}) collective-permute-start(bf16[384,384]{1,0:T(8,128)(2,1)S(1)} %fusion.9), channel_id=1, source_target_pairs={{0,128},{128,0},{1,129},{129,1},{2,130},{130,2},{3,131},{131,3},{4... | collective-permute-start | bytes 884744 | tf_op jit(solution)/shard_map/ppermute | solution.py:19
  135.8 16.0 %all_to_all.10 = bf16[32,14,384]{2,1,0:T(8,128)(2,1)S(1)} all-to-all(bf16[32,14,384]{2,1,0:T(8,128)(2,1)S(1)} %pad_maximum_fusion), channel_id=1, replica_groups=mesh['group'=2,'row'=4,'zl'=2,'y'=4,'x'=4] {'zl','y','x'}, dimensions={0} | all-to-all | bytes 688128 | tf_op jit(solution)/shard_map/all_to_all | solution.py:363
  151.9 12.7 %all_to_all.11 = bf16[32,12,384]{2,1,0:T(8,128)(2,1)S(1)} all-to-all(bf16[32,12,384]{2,1,0:T(8,128)(2,1)S(1)} %broadcast_in_dim.19), channel_id=1, replica_groups=mesh['group'=2,'row'=4,'zl'=2,'y'=4,'x'=4] {'zl','y','x'}, dimensions={0} | all-to-all | bytes 589824 | tf_op jit(solution)/shard_map/all_to_all | solution.py:367
  164.7 2.8 %collective-permute-start.19 = (bf16[384,384]{1,0:T(8,128)(2,1)S(1)}, bf16[384,384]{1,0:T(8,128)(2,1)S(1)}, u32[]{:S(2)}, u32[]{:S(2)}) collective-permute-start(bf16[384,384]{1,0:T(8,128)(2,1)S(1)} %reshape.118), channel_id=1, source_target_pairs={{0,128},{128,0},{1,129},{129,1},{2,130},{130,2},{3,131},{131,3},{4... | collective-permute-start | bytes 884744 | tf_op jit(solution)/shard_map/ppermute | solution.py:19
  (104 shorter events, 21.0 us)
Async XLA Ops:
  3.3 7.9 %collective-permute-start = (bf16[48,3072]{1,0:T(8,128)(2,1)S(1)}, bf16[48,3072]{1,0:T(8,128)(2,1)S(1)}, u32[]{:S(2)}, u32[]{:S(2)}) collective-permute-start(bf16[48,3072]{1,0:T(8,128)(2,1)S(1)} %maximum_maximum_fusion.1), channel_id=1, source_target_pairs={{0,16},{144,128},{1,17},{145,129},{2,18},{146,130},{3,19},{147,131... | collective-permute-start | bytes 884744 | tf_op jit(solution)/shard_map/ppermute | solution.py:271
  6.8 10.8 %copy-start.9 = (bf16[48,1024]{1,0:T(8,128)(2,1)S(1)}, bf16[48,1024]{1,0:T(8,128)(2,1)}, u32[]{:S(2)}) copy-start(bf16[48,1024]{1,0:T(8,128)(2,1)} %param.17) | copy-start | bytes 294916
  6.8 10.8 %copy-start.10 = (bf16[48,1024]{1,0:T(8,128)(2,1)S(1)}, bf16[48,1024]{1,0:T(8,128)(2,1)}, u32[]{:S(2)}) copy-start(bf16[48,1024]{1,0:T(8,128)(2,1)} %param.16) | copy-start | bytes 294916
  11.1 54.7 %collective-permute-start.2 = (bf16[2,576,384]{2,1,0:T(8,128)(2,1)S(1)}, bf16[2,576,384]{2,1,0:T(8,128)(2,1)S(1)}, u32[]{:S(2)}, u32[]{:S(2)}) collective-permute-start(bf16[2,576,384]{2,1,0:T(8,128)(2,1)S(1)} %maximum_maximum_fusion.own), channel_id=1, source_target_pairs={{0,32},{32,64},{64,96},{96,0},{1,33},{33,65},{65,97},{97,1},{2,34}... | collective-permute-start | bytes 2654216 | tf_op jit(solution)/shard_map/ppermute | solution.py:19
  14.6 51.4 %collective-permute-start.1 = (bf16[2,576,384]{2,1,0:T(8,128)(2,1)S(1)}, bf16[2,576,384]{2,1,0:T(8,128)(2,1)S(1)}, u32[]{:S(2)}, u32[]{:S(2)}) collective-permute-start(bf16[2,576,384]{2,1,0:T(8,128)(2,1)S(1)} %maximum_maximum_fusion.own), channel_id=1, source_target_pairs={{0,96},{32,0},{64,32},{96,64},{1,97},{33,1},{65,33},{97,65},{2,98}... | collective-permute-start | bytes 2654216 | tf_op jit(solution)/shard_map/ppermute | solution.py:19
  17.7 9.6 %collective-permute-start.5 = (bf16[48,3072]{1,0:T(8,128)(2,1)S(1)}, bf16[48,3072]{1,0:T(8,128)(2,1)S(1)}, u32[]{:S(2)}, u32[]{:S(2)}) collective-permute-start(bf16[48,3072]{1,0:T(8,128)(2,1)S(1)} %broadcast_select_fusion.refs_0_), channel_id=1, source_target_pairs={{0,3},{128,140},{1,0},{129,141},{2,1},{130,142},{3,2},{131,143},{4... | collective-permute-start | bytes 884744 | tf_op jit(solution)/shard_map/ppermute | solution.py:285
  20.5 7.5 %collective-permute-start.6 = (bf16[48,3072]{1,0:T(8,128)(2,1)S(1)}, bf16[48,3072]{1,0:T(8,128)(2,1)}, u32[]{:S(2)}, u32[]{:S(2)}) collective-permute-start(bf16[48,3072]{1,0:T(8,128)(2,1)S(1)} %broadcast_select_fusion.refs_0_), channel_id=1, source_target_pairs={{0,2},{128,136},{1,3},{129,137},{2,0},{130,138},{3,1},{131,139},{4... | collective-permute-start | bytes 884744 | tf_op jit(solution)/shard_map/ppermute | solution.py:285
  20.9 10.3 %collective-permute-start.7 = (bf16[48,3072]{1,0:T(8,128)(2,1)S(1)}, bf16[48,3072]{1,0:T(8,128)(2,1)}, u32[]{:S(2)}, u32[]{:S(2)}) collective-permute-start(bf16[48,3072]{1,0:T(8,128)(2,1)S(1)} %broadcast_select_fusion.refs_0_), channel_id=1, source_target_pairs={{0,1},{128,132},{1,2},{129,133},{2,3},{130,134},{3,0},{131,135},{4... | collective-permute-start | bytes 884744 | tf_op jit(solution)/shard_map/ppermute | solution.py:285
  32.3 37.4 %copy-start.14 = (bf16[1536]{0:T(1024)(128)(2,1)S(1)}, bf16[1536]{0:T(1024)(128)(2,1)}, u32[]{:S(2)}) copy-start(bf16[1536]{0:T(1024)(128)(2,1)} %param.14) | copy-start | bytes 9220
  32.3 48.4 %collective-permute-start.8 = (bf16[4,48,3072]{2,1,0:T(8,128)(2,1)S(1)}, bf16[4,48,3072]{2,1,0:T(8,128)(2,1)S(1)}, u32[]{:S(2)}, u32[]{:S(2)}) collective-permute-start(bf16[4,48,3072]{2,1,0:T(8,128)(2,1)S(1)} %shard_map.123.refs_0_), channel_id=1, source_target_pairs={{0,12},{128,131},{1,13},{129,128},{2,14},{130,129},{3,15},{131,130... | collective-permute-start | bytes 3538952 | tf_op jit(solution)/shard_map/ppermute | solution.py:285
  34.8 45.9 %collective-permute-start.9 = (bf16[4,48,3072]{2,1,0:T(8,128)(2,1)S(1)}, bf16[4,48,3072]{2,1,0:T(8,128)(2,1)S(1)}, u32[]{:S(2)}, u32[]{:S(2)}) collective-permute-start(bf16[4,48,3072]{2,1,0:T(8,128)(2,1)S(1)} %shard_map.123.refs_0_), channel_id=1, source_target_pairs={{0,8},{128,130},{1,9},{129,131},{2,10},{130,128},{3,11},{131,129},... | collective-permute-start | bytes 3538952 | tf_op jit(solution)/shard_map/ppermute | solution.py:285
  35.3 45.9 %collective-permute-start.10 = (bf16[4,48,3072]{2,1,0:T(8,128)(2,1)S(1)}, bf16[4,48,3072]{2,1,0:T(8,128)(2,1)S(1)}, u32[]{:S(2)}, u32[]{:S(2)}) collective-permute-start(bf16[4,48,3072]{2,1,0:T(8,128)(2,1)S(1)} %shard_map.123.refs_0_), channel_id=1, source_target_pairs={{0,4},{128,129},{1,5},{129,130},{2,6},{130,131},{3,7},{131,128},{4... | collective-permute-start | bytes 3538952 | tf_op jit(solution)/shard_map/ppermute | solution.py:285
  65.9 13.0 %collective-permute-start.3 = (bf16[576,384]{1,0:T(8,128)(2,1)S(1)}, bf16[576,384]{1,0:T(8,128)(2,1)S(1)}, u32[]{:S(2)}, u32[]{:S(2)}) collective-permute-start(bf16[576,384]{1,0:T(8,128)(2,1)S(1)} %slice_bitcast_fusion.1), channel_id=1, source_target_pairs={{0,32},{32,64},{64,96},{96,0},{1,33},{33,65},{65,97},{97,1},{2,34}... | collective-permute-start | bytes 1327112 | tf_op jit(solution)/shard_map/ppermute | solution.py:19
  66.1 15.2 %collective-permute-start.4 = (bf16[576,384]{1,0:T(8,128)(2,1)S(1)}, bf16[576,384]{1,0:T(8,128)(2,1)S(1)}, u32[]{:S(2)}, u32[]{:S(2)}) collective-permute-start(bf16[576,384]{1,0:T(8,128)(2,1)S(1)} %slice_bitcast_fusion), channel_id=1, source_target_pairs={{0,96},{32,0},{64,32},{96,64},{1,97},{33,1},{65,33},{97,65},{2,98}... | collective-permute-start | bytes 1327112 | tf_op jit(solution)/shard_map/ppermute | solution.py:19
  78.9 5.8 %collective-permute-start.11 = (bf16[4,48,3072]{2,1,0:T(8,128)(2,1)S(1)}, bf16[4,48,3072]{2,1,0:T(8,128)(2,1)S(1)}, u32[]{:S(2)}, u32[]{:S(2)}) collective-permute-start(bf16[4,48,3072]{2,1,0:T(8,128)(2,1)S(1)} %shard_map.123.refs_0_), channel_id=1, source_target_pairs={{0,128},{128,0},{1,129},{129,1},{2,130},{130,2},{3,131},{131,3},{4... | collective-permute-start | bytes 3538952 | tf_op jit(solution)/shard_map/ppermute | solution.py:19
  80.7 4.2 %collective-permute-start.12 = (bf16[4,48,3072]{2,1,0:T(8,128)(2,1)S(1)}, bf16[4,48,3072]{2,1,0:T(8,128)(2,1)S(1)}, u32[]{:S(2)}, u32[]{:S(2)}) collective-permute-start(bf16[4,48,3072]{2,1,0:T(8,128)(2,1)S(1)} %collective-permute-done.8.refs_1_), channel_id=1, source_target_pairs={{0,128},{128,0},{1,129},{129,1},{2,130},{130,2},{3,131},{131,3},{4... | collective-permute-start | bytes 3538952 | tf_op jit(solution)/shard_map/ppermute | solution.py:19
  80.7 5.8 %collective-permute-start.13 = (bf16[4,48,3072]{2,1,0:T(8,128)(2,1)S(1)}, bf16[4,48,3072]{2,1,0:T(8,128)(2,1)S(1)}, u32[]{:S(2)}, u32[]{:S(2)}) collective-permute-start(bf16[4,48,3072]{2,1,0:T(8,128)(2,1)S(1)} %collective-permute-done.9.refs_2_), channel_id=1, source_target_pairs={{0,128},{128,0},{1,129},{129,1},{2,130},{130,2},{3,131},{131,3},{4... | collective-permute-start | bytes 3538952 | tf_op jit(solution)/shard_map/ppermute | solution.py:19
  81.2 7.0 %collective-permute-start.14 = (bf16[4,48,3072]{2,1,0:T(8,128)(2,1)S(1)}, bf16[4,48,3072]{2,1,0:T(8,128)(2,1)S(1)}, u32[]{:S(2)}, u32[]{:S(2)}) collective-permute-start(bf16[4,48,3072]{2,1,0:T(8,128)(2,1)S(1)} %collective-permute-done.10.refs_3_), channel_id=1, source_target_pairs={{0,128},{128,0},{1,129},{129,1},{2,130},{130,2},{3,131},{131,3},{4... | collective-permute-start | bytes 3538952 | tf_op jit(solution)/shard_map/ppermute | solution.py:19
  84.7 21.6 %copy-start.15 = (bf16[384]{0:T(512)(128)(2,1)S(1)}, bf16[384]{0:T(512)(128)(2,1)}, u32[]{:S(2)}) copy-start(bf16[384]{0:T(512)(128)(2,1)} %param.15) | copy-start | bytes 2308
  100.4 15.0 %collective-permute-start.15 = (bf16[256,384]{1,0:T(8,128)(2,1)}, bf16[256,384]{1,0:T(8,128)(2,1)}, u32[]{:S(2)}, u32[]{:S(2)}) collective-permute-start(bf16[256,384]{1,0:T(8,128)(2,1)} %get-tuple-element.29), channel_id=1, source_target_pairs={{0,64},{32,96},{64,0},{96,32},{1,65},{33,97},{65,1},{97,33},{2,66}... | collective-permute-start | bytes 589832 | tf_op jit(solution)/shard_map/ppermute | solution.py:19
  102.7 13.4 %collective-permute-start.16 = (bf16[256,384]{1,0:T(8,128)(2,1)}, bf16[256,384]{1,0:T(8,128)(2,1)}, u32[]{:S(2)}, u32[]{:S(2)}) collective-permute-start(bf16[256,384]{1,0:T(8,128)(2,1)} %get-tuple-element.30), channel_id=1, source_target_pairs={{0,32},{32,64},{64,96},{96,0},{1,33},{33,65},{65,97},{97,1},{2,34}... | collective-permute-start | bytes 589832 | tf_op jit(solution)/shard_map/ppermute | solution.py:19
  102.7 13.4 %collective-permute-start.17 = (bf16[256,384]{1,0:T(8,128)(2,1)}, bf16[256,384]{1,0:T(8,128)(2,1)}, u32[]{:S(2)}, u32[]{:S(2)}) collective-permute-start(bf16[256,384]{1,0:T(8,128)(2,1)} %get-tuple-element.31), channel_id=1, source_target_pairs={{0,96},{32,0},{64,32},{96,64},{1,97},{33,1},{65,33},{97,65},{2,98}... | collective-permute-start | bytes 589832 | tf_op jit(solution)/shard_map/ppermute | solution.py:19
  130.6 4.8 %collective-permute-start.18 = (bf16[384,384]{1,0:T(8,128)(2,1)S(1)}, bf16[384,384]{1,0:T(8,128)(2,1)S(1)}, u32[]{:S(2)}, u32[]{:S(2)}) collective-permute-start(bf16[384,384]{1,0:T(8,128)(2,1)S(1)} %fusion.9), channel_id=1, source_target_pairs={{0,128},{128,0},{1,129},{129,1},{2,130},{130,2},{3,131},{131,3},{4... | collective-permute-start | bytes 884744 | tf_op jit(solution)/shard_map/ppermute | solution.py:19
  164.7 4.6 %collective-permute-start.19 = (bf16[384,384]{1,0:T(8,128)(2,1)S(1)}, bf16[384,384]{1,0:T(8,128)(2,1)S(1)}, u32[]{:S(2)}, u32[]{:S(2)}) collective-permute-start(bf16[384,384]{1,0:T(8,128)(2,1)S(1)} %reshape.118), channel_id=1, source_target_pairs={{0,128},{128,0},{1,129},{129,1},{2,130},{130,2},{3,131},{131,3},{4... | collective-permute-start | bytes 884744 | tf_op jit(solution)/shard_map/ppermute | solution.py:19
  (13 other events, 63.0 us)

commit v4 on v3

--- a/solution.py
+++ b/solution.py
@@ -285,8 +285,13 @@
             pieces.append(lax.ppermute(value, ("group", "y", "x"), pairs))
         return pieces
 
-    weights_own = collect(gather(place, collect(block, True)), False)
-    weights_other = [shift(piece, "group", 2, 1) for piece in weights_own]
+    line = gather(place, collect(block, True))
+    weights_own = collect(line, False)
+    both = lax.all_to_all(
+        jnp.broadcast_to(line[None], (2,) + line.shape), "group", 0, 0, tiled=True
+    )
+    weights_other = [lax.dynamic_index_in_dim(both, 1 - group, 0, keepdims=False)]
+    weights_other += [shift(piece, "group", 2, 1) for piece in weights_own[1:]]
 
     kinds = aug_embed.shape[0]
     kind_table = (
@@ -331,7 +336,8 @@
             jnp.sum(target * target, axis=1),
         ]
     )
-    sums = jnp.sum(lax.all_gather(sums, "row"), axis=0)
+    sums = sums + lax.ppermute(sums, "row", [(0, 1), (1, 0), (2, 3), (3, 2)])
+    sums = sums + lax.ppermute(sums, "row", [(0, 2), (1, 3), (2, 0), (3, 1)])
     center = sums[0] / D
     spread = sums[1] / D - center * center
     scaler = lax.rsqrt(spread + 1e-05)

time: 172 us -> 167 us (0.971)
  waiting for transfers between devices: 63.6 us -> 48.1 us
  starting transfers between devices: 33.6 us -> 40.7 us
  local copies, waits for them, and re-layouts: 7.01 us -> 12.1 us
    ppermute x13 -> x12, waiting for transfers between devices: 49.9 us -> 32.4 us  [shift(): lax.ppermute(value, axis, [(i, (i + by) % size) for i in range(size)])]
    all_gather x1 -> x0, blocking collectives: 11.2 us -> none  [shards(): sums = jnp.sum(lax.all_gather(sums, 'row'), axis=0)]
    ppermute x0 -> x2, starting transfers between devices: none -> 6.47 us  [the longest x1 5.21 us: shards(): sums = sums + lax.ppermute(sums, 'row', [(0, 2), (1, 3), (2, 0), (3, 1)])]
    all_to_all x0 -> x1, blocking collectives: none -> 6.45 us  [shards(): lax.all_to_all(jnp.broadcast_to(line[None], (2,) + line.shape), 'group',...]
    ppermute x0 -> x2, waiting for transfers between devices: none -> 3.42 us  [the longest x1 2.22 us: shards(): sums = sums + lax.ppermute(sums, 'row', [(0, 1), (1, 0), (2, 3), (3, 2)])]
    all_to_all x1, blocking collectives: 16 us -> 19.3 us  [shards(): packet = lax.all_to_all(packet, COL, 0, 0, tiled=True).astype(jnp.float32)]
    unnamed x35 -> x33, local copies, waits for them, and re-layouts: 3.65 us -> 5.87 us
    squeeze x1, local copies, waits for them, and re-layouts: 0.05 us -> 1.82 us  [shards(): far_bottom = shift(after[1], 'row', 4, -1)]
  transfers between devices with their start and end apart: 20 -> 21, of which waited for: 12 -> 11; matrix products, arithmetic and copies ran while one was open for 2% -> 5% of each run, Pallas kernels for 3% -> 4%
where the time goes in v4:
time: 167 us; the launch traced here: 166 us
  waiting for transfers between devices  48.1 us (29%)
  starting transfers between devices  40.7 us (24%)
  blocking collectives  38.5 us (23%)
  Pallas kernels  17.3 us (10%)
  local copies, waits for them, and re-layouts  12.1 us (7%)
  other arithmetic  5.29 us (3%)
  between operations  3.41 us (2%)
    ppermute x12, waiting for transfers between devices, shift(): lax.ppermute(value, axis, [(i, (i + by) % size) for i in range(size)])  32.4 us
    ppermute x12, starting transfers between devices, shift(): lax.ppermute(value, axis, [(i, (i + by) % size) for i in range(size)])  25.4 us
    all_to_all x1, blocking collectives, shards(): packet = lax.all_to_all(packet, COL, 0, 0, tiled=True).astype(jnp.float32)  19.3 us
    all_to_all x1, blocking collectives, shards(): lax.all_to_all(jnp.broadcast_to(piece[None], (32, 12, PART)), COL, 0, 0,...  12.7 us
    pallas_call x1, Pallas kernels, branch(): pl.pallas_call(branch_kernel, in_specs=[pl.BlockSpec(memory_space=pltpu.S...  10.9 us
    ppermute x6, waiting for transfers between devices, collect(): pieces.append(lax.ppermute(value, ('group', 'y', 'x'), pairs))  7.98 us
    ppermute x6, starting transfers between devices, collect(): pieces.append(lax.ppermute(value, ('group', 'y', 'x'), pairs))  7.53 us
    all_to_all x1, blocking collectives, shards(): lax.all_to_all(jnp.broadcast_to(line[None], (2,) + line.shape), 'group',...  6.45 us
  transfers between devices with their start and end apart: 21, of which 11 were waited for; matrix products, arithmetic and copies ran while one was open for 5% of the time, Pallas kernels for 4%

profile of v4, /device:TPU:1, one launch (start us, length us, event | category | flops | bytes accessed | tf_op | source)
XLA Modules:
  0.0 166.2 jit_solution(10022861722860792313)
XLA Ops:
  6.9 4.3 %collective-permute-done = bf16[48,3072]{1,0:T(8,128)(2,1)} collective-permute-done((bf16[48,3072]{1,0:T(8,128)(2,1)S(1)}, bf16[48,3072]{1,0:T(8,128)(2,1)}, u32[]{:S(2)}, u32[]{:S(2)}) %collective-permute-start) | collective-permute-done | bytes 294944 | tf_op jit(solution)/shard_map/ppermute | solution.py:271
  11.2 3.4 %collective-permute-start.2 = (bf16[2,576,384]{2,1,0:T(8,128)(2,1)S(1)}, bf16[2,576,384]{2,1,0:T(8,128)(2,1)S(1)}, u32[]{:S(2)}, u32[]{:S(2)}) collective-permute-start(bf16[2,576,384]{2,1,0:T(8,128)(2,1)S(1)} %maximum_maximum_fusion.own), channel_id=1, source_target_pairs={{0,32},{32,64},{64,96},{96,0},{1,33},{33,65},{65,97},{97,1},{2,34}... | collective-permute-start | bytes 2654216 | tf_op jit(solution)/shard_map/ppermute | solution.py:19
  14.7 3.0 %collective-permute-start.1 = (bf16[2,576,384]{2,1,0:T(8,128)(2,1)S(1)}, bf16[2,576,384]{2,1,0:T(8,128)(2,1)}, u32[]{:S(2)}, u32[]{:S(2)}) collective-permute-start(bf16[2,576,384]{2,1,0:T(8,128)(2,1)S(1)} %maximum_maximum_fusion.own), channel_id=1, source_target_pairs={{0,96},{32,0},{64,32},{96,64},{1,97},{33,1},{65,33},{97,65},{2,98}... | collective-permute-start | bytes 2654216 | tf_op jit(solution)/shard_map/ppermute | solution.py:19
  18.7 2.8 %collective-permute-start.5 = (bf16[48,3072]{1,0:T(8,128)(2,1)S(1)}, bf16[48,3072]{1,0:T(8,128)(2,1)S(1)}, u32[]{:S(2)}, u32[]{:S(2)}) collective-permute-start(bf16[48,3072]{1,0:T(8,128)(2,1)S(1)} %broadcast_select_fusion.refs_0_), channel_id=1, source_target_pairs={{0,3},{128,140},{1,0},{129,141},{2,1},{130,142},{3,2},{131,143},{4... | collective-permute-start | bytes 884744 | tf_op jit(solution)/shard_map/ppermute | solution.py:285
  22.7 5.7 %collective-permute-done.5.refs_1_ = bf16[48,3072]{1,0:T(8,128)(2,1)S(1)} collective-permute-done((bf16[48,3072]{1,0:T(8,128)(2,1)S(1)}, bf16[48,3072]{1,0:T(8,128)(2,1)S(1)}, u32[]{:S(2)}, u32[]{:S(2)}) %collective-permute-start.5) | collective-permute-done | bytes 294944 | tf_op jit(solution)/shard_map/ppermute | solution.py:285
  29.8 2.3 %collective-permute-done.7.refs_3_ = bf16[48,3072]{1,0:T(8,128)(2,1)S(1)} collective-permute-done((bf16[48,3072]{1,0:T(8,128)(2,1)S(1)}, bf16[48,3072]{1,0:T(8,128)(2,1)S(1)}, u32[]{:S(2)}, u32[]{:S(2)}) %collective-permute-start.7) | collective-permute-done | bytes 294944 | tf_op jit(solution)/shard_map/ppermute | solution.py:285
  36.4 2.6 %collective-permute-start.8 = (bf16[4,48,3072]{2,1,0:T(8,128)(2,1)S(1)}, bf16[4,48,3072]{2,1,0:T(8,128)(2,1)}, u32[]{:S(2)}, u32[]{:S(2)}) collective-permute-start(bf16[4,48,3072]{2,1,0:T(8,128)(2,1)S(1)} %shard_map.123.refs_0_), channel_id=1, source_target_pairs={{0,12},{128,131},{1,13},{129,128},{2,14},{130,129},{3,15},{131,130... | collective-permute-start | bytes 3538952 | tf_op jit(solution)/shard_map/ppermute | solution.py:285
  40.0 16.8 %collective-permute-done.2.before = bf16[2,576,384]{2,1,0:T(8,128)(2,1)S(1)} collective-permute-done((bf16[2,576,384]{2,1,0:T(8,128)(2,1)S(1)}, bf16[2,576,384]{2,1,0:T(8,128)(2,1)S(1)}, u32[]{:S(2)}, u32[]{:S(2)}) %collective-permute-start.2) | collective-permute-done | bytes 884768 | tf_op jit(solution)/shard_map/ppermute | solution.py:19
  57.6 1.8 %slice_bitcast_fusion = bf16[576,384]{1,0:T(8,128)(2,1)} fusion(bf16[2,576,384]{2,1,0:T(8,128)(2,1)} %collective-permute-done.1.after), kind=kLoop, calls=%fused_computation.13 | loop fusion | bytes 884736 | tf_op jit(solution)/shard_map/squeeze | solution.py:317
  59.4 3.6 %collective-permute-start.4 = (bf16[576,384]{1,0:T(8,128)(2,1)}, bf16[576,384]{1,0:T(8,128)(2,1)}, u32[]{:S(2)}, u32[]{:S(2)}) collective-permute-start(bf16[576,384]{1,0:T(8,128)(2,1)} %slice_bitcast_fusion), channel_id=1, source_target_pairs={{0,96},{32,0},{64,32},{96,64},{1,97},{33,1},{65,33},{97,65},{2,98}... | collective-permute-start | bytes 1327112 | tf_op jit(solution)/shard_map/ppermute | solution.py:19
  63.3 6.5 %all_to_all.15 = bf16[2,4,48,3072]{3,2,1,0:T(8,128)(2,1)S(1)} all-to-all(bf16[2,4,48,3072]{3,2,1,0:T(8,128)(2,1)S(1)} %broadcast_in_dim.14), channel_id=1, replica_groups=mesh['group'=2,'row'=4,'zl'=2,'y'=4,'x'=4] {'group'}, dimensions={0} | all-to-all | bytes 4718592 | tf_op jit(solution)/shard_map/all_to_all | solution.py:290
  70.8 4.4 %collective-permute-done.3.far_top = bf16[576,384]{1,0:T(8,128)(2,1)S(1)} collective-permute-done((bf16[576,384]{1,0:T(8,128)(2,1)}, bf16[576,384]{1,0:T(8,128)(2,1)S(1)}, u32[]{:S(2)}, u32[]{:S(2)}) %collective-permute-start.3) | collective-permute-done | bytes 442400 | tf_op jit(solution)/shard_map/ppermute | solution.py:19
  76.6 4.3 %shard_map.122.normed = bf16[1024,1536]{1,0:T(8,128)(2,1)S(1)} custom-call(s32[4]{0:T(128)S(1)} %pad_add_fusion.place, bf16[2,576,384]{2,1,0:T(8,128)(2,1)S(1)} %maximum_maximum_fusion.own, bf16[2,576,384]{2,1,0:T(8,128)(2,1)} %collective-permute-done.1.after, bf16[2,576,384]{2,1,0:T(8,128)(2,1)S(1)} %collective-permute-done.2.before, ...), custom_call_target="tpu_custom_call" | custom-call | flops 30000001024 | bytes 6291456 | tf_op jit(solution)/shard_map/pallas_call | solution.py:42
  80.9 10.9 %shard_map.124 = (f32[256,384]{1,0:T(8,128)S(1)}, bf16[256,384]{1,0:T(8,128)(2,1)S(1)}, bf16[256,384]{1,0:T(8,128)(2,1)S(1)}, bf16[256,384]{1,0:T(8,128)(2,1)S(1)}) custom-call(s32[4]{0:T(128)S(1)} %pad_add_fusion.place, bf16[1024,1536]{1,0:T(8,128)(2,1)S(1)} %shard_map.122.normed, bf16[4,48,3072]{2,1,0:T(8,128)(2,1)S(1)} %shard_map.123.refs_0_, ...), custom_call_target="tpu_custom_call" | custom-call | flops 6442450944 | bytes 10485760 | tf_op jit(solution)/shard_map/pallas_call | solution.py:153
  91.8 2.1 %collective-permute-start.14 = (bf16[256,384]{1,0:T(8,128)(2,1)S(1)}, bf16[256,384]{1,0:T(8,128)(2,1)S(1)}, u32[]{:S(2)}, u32[]{:S(2)}) collective-permute-start(bf16[256,384]{1,0:T(8,128)(2,1)S(1)} %get-tuple-element.29), channel_id=1, source_target_pairs={{0,64},{32,96},{64,0},{96,32},{1,65},{33,97},{65,1},{97,33},{2,66}... | collective-permute-start | bytes 589832 | tf_op jit(solution)/shard_map/ppermute | solution.py:19
  93.9 2.6 %collective-permute-start.15 = (bf16[256,384]{1,0:T(8,128)(2,1)S(1)}, bf16[256,384]{1,0:T(8,128)(2,1)S(1)}, u32[]{:S(2)}, u32[]{:S(2)}) collective-permute-start(bf16[256,384]{1,0:T(8,128)(2,1)S(1)} %get-tuple-element.30), channel_id=1, source_target_pairs={{0,32},{32,64},{64,96},{96,0},{1,33},{33,65},{65,97},{97,1},{2,34}... | collective-permute-start | bytes 589832 | tf_op jit(solution)/shard_map/ppermute | solution.py:19
  97.5 1.5 shard_map.125
  99.0 9.2 %collective-permute-done.14 = bf16[256,384]{1,0:T(8,128)(2,1)S(1)} collective-permute-done((bf16[256,384]{1,0:T(8,128)(2,1)S(1)}, bf16[256,384]{1,0:T(8,128)(2,1)S(1)}, u32[]{:S(2)}, u32[]{:S(2)}) %collective-permute-start.14) | collective-permute-done | bytes 196640 | tf_op jit(solution)/shard_map/ppermute | solution.py:19
  110.2 2.2 %collective-permute-done.17 = f32[5,256]{1,0:T(8,128)S(1)} collective-permute-done((f32[5,256]{1,0:T(8,128)S(1)}, f32[5,256]{1,0:T(8,128)S(1)}, u32[]{:S(2)}, u32[]{:S(2)}) %collective-permute-start.17) | collective-permute-done | bytes 5152 | tf_op jit(solution)/shard_map/ppermute | solution.py:339
  112.5 5.2 %collective-permute-start.18 = (f32[5,256]{1,0:T(8,128)S(1)}, f32[5,256]{1,0:T(8,128)S(1)}, u32[]{:S(2)}, u32[]{:S(2)}) collective-permute-start(f32[5,256]{1,0:T(8,128)S(1)} %add.85), channel_id=1, source_target_pairs={{0,64},{32,96},{64,0},{96,32},{1,65},{33,97},{65,1},{97,33},{2,66}... | collective-permute-start | bytes 15368 | tf_op jit(solution)/shard_map/ppermute | solution.py:340
  119.5 5.9 %collective-permute-start.19 = (bf16[384,384]{1,0:T(8,128)(2,1)S(1)}, bf16[384,384]{1,0:T(8,128)(2,1)S(1)}, u32[]{:S(2)}, u32[]{:S(2)}) collective-permute-start(bf16[384,384]{1,0:T(8,128)(2,1)S(1)} %fusion.9), channel_id=1, source_target_pairs={{0,128},{128,0},{1,129},{129,1},{2,130},{130,2},{3,131},{131,3},{4... | collective-permute-start | bytes 884744 | tf_op jit(solution)/shard_map/ppermute | solution.py:19
  127.0 19.3 %all_to_all.16 = bf16[32,14,384]{2,1,0:T(8,128)(2,1)S(1)} all-to-all(bf16[32,14,384]{2,1,0:T(8,128)(2,1)S(1)} %pad_maximum_fusion), channel_id=1, replica_groups=mesh['group'=2,'row'=4,'zl'=2,'y'=4,'x'=4] {'zl','y','x'}, dimensions={0} | all-to-all | bytes 688128 | tf_op jit(solution)/shard_map/all_to_all | solution.py:369
  146.5 12.7 %all_to_all.17 = bf16[32,12,384]{2,1,0:T(8,128)(2,1)S(1)} all-to-all(bf16[32,12,384]{2,1,0:T(8,128)(2,1)S(1)} %broadcast_in_dim.22), channel_id=1, replica_groups=mesh['group'=2,'row'=4,'zl'=2,'y'=4,'x'=4] {'zl','y','x'}, dimensions={0} | all-to-all | bytes 589824 | tf_op jit(solution)/shard_map/all_to_all | solution.py:373
  159.2 2.8 %collective-permute-start.20 = (bf16[384,384]{1,0:T(8,128)(2,1)S(1)}, bf16[384,384]{1,0:T(8,128)(2,1)S(1)}, u32[]{:S(2)}, u32[]{:S(2)}) collective-permute-start(bf16[384,384]{1,0:T(8,128)(2,1)S(1)} %reshape.119), channel_id=1, source_target_pairs={{0,128},{128,0},{1,129},{129,1},{2,130},{130,2},{3,131},{131,3},{4... | collective-permute-start | bytes 884744 | tf_op jit(solution)/shard_map/ppermute | solution.py:19
  (107 shorter events, 26.9 us)
Async XLA Ops:
  3.3 8.0 %collective-permute-start = (bf16[48,3072]{1,0:T(8,128)(2,1)S(1)}, bf16[48,3072]{1,0:T(8,128)(2,1)}, u32[]{:S(2)}, u32[]{:S(2)}) collective-permute-start(bf16[48,3072]{1,0:T(8,128)(2,1)S(1)} %maximum_maximum_fusion.1), channel_id=1, source_target_pairs={{0,16},{144,128},{1,17},{145,129},{2,18},{146,130},{3,19},{147,131... | collective-permute-start | bytes 884744 | tf_op jit(solution)/shard_map/ppermute | solution.py:271
  11.2 45.6 %collective-permute-start.2 = (bf16[2,576,384]{2,1,0:T(8,128)(2,1)S(1)}, bf16[2,576,384]{2,1,0:T(8,128)(2,1)S(1)}, u32[]{:S(2)}, u32[]{:S(2)}) collective-permute-start(bf16[2,576,384]{2,1,0:T(8,128)(2,1)S(1)} %maximum_maximum_fusion.own), channel_id=1, source_target_pairs={{0,32},{32,64},{64,96},{96,0},{1,33},{33,65},{65,97},{97,1},{2,34}... | collective-permute-start | bytes 2654216 | tf_op jit(solution)/shard_map/ppermute | solution.py:19
  14.7 42.9 %collective-permute-start.1 = (bf16[2,576,384]{2,1,0:T(8,128)(2,1)S(1)}, bf16[2,576,384]{2,1,0:T(8,128)(2,1)}, u32[]{:S(2)}, u32[]{:S(2)}) collective-permute-start(bf16[2,576,384]{2,1,0:T(8,128)(2,1)S(1)} %maximum_maximum_fusion.own), channel_id=1, source_target_pairs={{0,96},{32,0},{64,32},{96,64},{1,97},{33,1},{65,33},{97,65},{2,98}... | collective-permute-start | bytes 2654216 | tf_op jit(solution)/shard_map/ppermute | solution.py:19
  18.7 9.6 %collective-permute-start.5 = (bf16[48,3072]{1,0:T(8,128)(2,1)S(1)}, bf16[48,3072]{1,0:T(8,128)(2,1)S(1)}, u32[]{:S(2)}, u32[]{:S(2)}) collective-permute-start(bf16[48,3072]{1,0:T(8,128)(2,1)S(1)} %broadcast_select_fusion.refs_0_), channel_id=1, source_target_pairs={{0,3},{128,140},{1,0},{129,141},{2,1},{130,142},{3,2},{131,143},{4... | collective-permute-start | bytes 884744 | tf_op jit(solution)/shard_map/ppermute | solution.py:285
  21.6 7.5 %collective-permute-start.6 = (bf16[48,3072]{1,0:T(8,128)(2,1)S(1)}, bf16[48,3072]{1,0:T(8,128)(2,1)S(1)}, u32[]{:S(2)}, u32[]{:S(2)}) collective-permute-start(bf16[48,3072]{1,0:T(8,128)(2,1)S(1)} %broadcast_select_fusion.refs_0_), channel_id=1, source_target_pairs={{0,2},{128,136},{1,3},{129,137},{2,0},{130,138},{3,1},{131,139},{4... | collective-permute-start | bytes 884744 | tf_op jit(solution)/shard_map/ppermute | solution.py:285
  21.9 10.2 %collective-permute-start.7 = (bf16[48,3072]{1,0:T(8,128)(2,1)S(1)}, bf16[48,3072]{1,0:T(8,128)(2,1)S(1)}, u32[]{:S(2)}, u32[]{:S(2)}) collective-permute-start(bf16[48,3072]{1,0:T(8,128)(2,1)S(1)} %broadcast_select_fusion.refs_0_), channel_id=1, source_target_pairs={{0,1},{128,132},{1,2},{129,133},{2,3},{130,134},{3,0},{131,135},{4... | collective-permute-start | bytes 884744 | tf_op jit(solution)/shard_map/ppermute | solution.py:285
  36.3 26.7 %copy-start.13 = (bf16[1536]{0:T(1024)(128)(2,1)S(1)}, bf16[1536]{0:T(1024)(128)(2,1)}, u32[]{:S(2)}) copy-start(bf16[1536]{0:T(1024)(128)(2,1)} %param.14) | copy-start | bytes 9220
  36.4 33.5 %collective-permute-start.8 = (bf16[4,48,3072]{2,1,0:T(8,128)(2,1)S(1)}, bf16[4,48,3072]{2,1,0:T(8,128)(2,1)}, u32[]{:S(2)}, u32[]{:S(2)}) collective-permute-start(bf16[4,48,3072]{2,1,0:T(8,128)(2,1)S(1)} %shard_map.123.refs_0_), channel_id=1, source_target_pairs={{0,12},{128,131},{1,13},{129,128},{2,14},{130,129},{3,15},{131,130... | collective-permute-start | bytes 3538952 | tf_op jit(solution)/shard_map/ppermute | solution.py:285
  38.9 31.4 %collective-permute-start.9 = (bf16[4,48,3072]{2,1,0:T(8,128)(2,1)S(1)}, bf16[4,48,3072]{2,1,0:T(8,128)(2,1)}, u32[]{:S(2)}, u32[]{:S(2)}) collective-permute-start(bf16[4,48,3072]{2,1,0:T(8,128)(2,1)S(1)} %shard_map.123.refs_0_), channel_id=1, source_target_pairs={{0,8},{128,130},{1,9},{129,131},{2,10},{130,128},{3,11},{131,129},... | collective-permute-start | bytes 3538952 | tf_op jit(solution)/shard_map/ppermute | solution.py:285
  39.4 31.0 %collective-permute-start.10 = (bf16[4,48,3072]{2,1,0:T(8,128)(2,1)S(1)}, bf16[4,48,3072]{2,1,0:T(8,128)(2,1)}, u32[]{:S(2)}, u32[]{:S(2)}) collective-permute-start(bf16[4,48,3072]{2,1,0:T(8,128)(2,1)S(1)} %shard_map.123.refs_0_), channel_id=1, source_target_pairs={{0,4},{128,129},{1,5},{129,130},{2,6},{130,131},{3,7},{131,128},{4... | collective-permute-start | bytes 3538952 | tf_op jit(solution)/shard_map/ppermute | solution.py:285
  57.6 17.6 %collective-permute-start.3 = (bf16[576,384]{1,0:T(8,128)(2,1)}, bf16[576,384]{1,0:T(8,128)(2,1)S(1)}, u32[]{:S(2)}, u32[]{:S(2)}) collective-permute-start(bf16[576,384]{1,0:T(8,128)(2,1)} %slice_bitcast_fusion.1), channel_id=1, source_target_pairs={{0,32},{32,64},{64,96},{96,0},{1,33},{33,65},{65,97},{97,1},{2,34}... | collective-permute-start | bytes 1327112 | tf_op jit(solution)/shard_map/ppermute | solution.py:19
  59.4 17.1 %collective-permute-start.4 = (bf16[576,384]{1,0:T(8,128)(2,1)}, bf16[576,384]{1,0:T(8,128)(2,1)}, u32[]{:S(2)}, u32[]{:S(2)}) collective-permute-start(bf16[576,384]{1,0:T(8,128)(2,1)} %slice_bitcast_fusion), channel_id=1, source_target_pairs={{0,96},{32,0},{64,32},{96,64},{1,97},{33,1},{65,33},{97,65},{2,98}... | collective-permute-start | bytes 1327112 | tf_op jit(solution)/shard_map/ppermute | solution.py:19
  69.8 11.0 %collective-permute-start.11 = (bf16[4,48,3072]{2,1,0:T(8,128)(2,1)}, bf16[4,48,3072]{2,1,0:T(8,128)(2,1)S(1)}, u32[]{:S(2)}, u32[]{:S(2)}) collective-permute-start(bf16[4,48,3072]{2,1,0:T(8,128)(2,1)} %collective-permute-done.8.refs_1_), channel_id=1, source_target_pairs={{0,128},{128,0},{1,129},{129,1},{2,130},{130,2},{3,131},{131,3},{4... | collective-permute-start | bytes 3538952 | tf_op jit(solution)/shard_map/ppermute | solution.py:19
  70.3 10.6 %collective-permute-start.12 = (bf16[4,48,3072]{2,1,0:T(8,128)(2,1)}, bf16[4,48,3072]{2,1,0:T(8,128)(2,1)S(1)}, u32[]{:S(2)}, u32[]{:S(2)}) collective-permute-start(bf16[4,48,3072]{2,1,0:T(8,128)(2,1)} %collective-permute-done.9.refs_2_), channel_id=1, source_target_pairs={{0,128},{128,0},{1,129},{129,1},{2,130},{130,2},{3,131},{131,3},{4... | collective-permute-start | bytes 3538952 | tf_op jit(solution)/shard_map/ppermute | solution.py:19
  70.5 10.4 %collective-permute-start.13 = (bf16[4,48,3072]{2,1,0:T(8,128)(2,1)}, bf16[4,48,3072]{2,1,0:T(8,128)(2,1)S(1)}, u32[]{:S(2)}, u32[]{:S(2)}) collective-permute-start(bf16[4,48,3072]{2,1,0:T(8,128)(2,1)} %collective-permute-done.10.refs_3_), channel_id=1, source_target_pairs={{0,128},{128,0},{1,129},{129,1},{2,130},{130,2},{3,131},{131,3},{4... | collective-permute-start | bytes 3538952 | tf_op jit(solution)/shard_map/ppermute | solution.py:19
  80.8 16.6 %copy-start.14 = (bf16[384]{0:T(512)(128)(2,1)S(1)}, bf16[384]{0:T(512)(128)(2,1)}, u32[]{:S(2)}) copy-start(bf16[384]{0:T(512)(128)(2,1)} %param.15) | copy-start | bytes 2308
  80.9 16.6 %copy-start.1 = (bf16[768,384]{1,0:T(8,128)(2,1)S(1)}, bf16[768,384]{1,0:T(8,128)(2,1)}, u32[]{:S(2)}) copy-start(bf16[768,384]{1,0:T(8,128)(2,1)} %weight.1) | copy-start | bytes 1769476
  91.8 16.4 %collective-permute-start.14 = (bf16[256,384]{1,0:T(8,128)(2,1)S(1)}, bf16[256,384]{1,0:T(8,128)(2,1)S(1)}, u32[]{:S(2)}, u32[]{:S(2)}) collective-permute-start(bf16[256,384]{1,0:T(8,128)(2,1)S(1)} %get-tuple-element.29), channel_id=1, source_target_pairs={{0,64},{32,96},{64,0},{96,32},{1,65},{33,97},{65,1},{97,33},{2,66}... | collective-permute-start | bytes 589832 | tf_op jit(solution)/shard_map/ppermute | solution.py:19
  93.9 14.6 %collective-permute-start.15 = (bf16[256,384]{1,0:T(8,128)(2,1)S(1)}, bf16[256,384]{1,0:T(8,128)(2,1)S(1)}, u32[]{:S(2)}, u32[]{:S(2)}) collective-permute-start(bf16[256,384]{1,0:T(8,128)(2,1)S(1)} %get-tuple-element.30), channel_id=1, source_target_pairs={{0,32},{32,64},{64,96},{96,0},{1,33},{33,65},{65,97},{97,1},{2,34}... | collective-permute-start | bytes 589832 | tf_op jit(solution)/shard_map/ppermute | solution.py:19
  96.5 12.0 %collective-permute-start.16 = (bf16[256,384]{1,0:T(8,128)(2,1)S(1)}, bf16[256,384]{1,0:T(8,128)(2,1)S(1)}, u32[]{:S(2)}, u32[]{:S(2)}) collective-permute-start(bf16[256,384]{1,0:T(8,128)(2,1)S(1)} %get-tuple-element.31), channel_id=1, source_target_pairs={{0,96},{32,0},{64,32},{96,64},{1,97},{33,1},{65,33},{97,65},{2,98}... | collective-permute-start | bytes 589832 | tf_op jit(solution)/shard_map/ppermute | solution.py:19
  109.0 3.5 %collective-permute-start.17 = (f32[5,256]{1,0:T(8,128)S(1)}, f32[5,256]{1,0:T(8,128)S(1)}, u32[]{:S(2)}, u32[]{:S(2)}) collective-permute-start(f32[5,256]{1,0:T(8,128)S(1)} %stack.60), channel_id=1, source_target_pairs={{0,32},{32,0},{64,96},{96,64},{1,33},{33,1},{65,97},{97,65},{2,34}... | collective-permute-start | bytes 15368 | tf_op jit(solution)/shard_map/ppermute | solution.py:339
  112.5 6.4 %collective-permute-start.18 = (f32[5,256]{1,0:T(8,128)S(1)}, f32[5,256]{1,0:T(8,128)S(1)}, u32[]{:S(2)}, u32[]{:S(2)}) collective-permute-start(f32[5,256]{1,0:T(8,128)S(1)} %add.85), channel_id=1, source_target_pairs={{0,64},{32,96},{64,0},{96,32},{1,65},{33,97},{65,1},{97,33},{2,66}... | collective-permute-start | bytes 15368 | tf_op jit(solution)/shard_map/ppermute | solution.py:340
  119.5 7.1 %collective-permute-start.19 = (bf16[384,384]{1,0:T(8,128)(2,1)S(1)}, bf16[384,384]{1,0:T(8,128)(2,1)S(1)}, u32[]{:S(2)}, u32[]{:S(2)}) collective-permute-start(bf16[384,384]{1,0:T(8,128)(2,1)S(1)} %fusion.9), channel_id=1, source_target_pairs={{0,128},{128,0},{1,129},{129,1},{2,130},{130,2},{3,131},{131,3},{4... | collective-permute-start | bytes 884744 | tf_op jit(solution)/shard_map/ppermute | solution.py:19
  159.2 4.6 %collective-permute-start.20 = (bf16[384,384]{1,0:T(8,128)(2,1)S(1)}, bf16[384,384]{1,0:T(8,128)(2,1)S(1)}, u32[]{:S(2)}, u32[]{:S(2)}) collective-permute-start(bf16[384,384]{1,0:T(8,128)(2,1)S(1)} %reshape.119), channel_id=1, source_target_pairs={{0,128},{128,0},{1,129},{129,1},{2,130},{130,2},{3,131},{131,3},{4... | collective-permute-start | bytes 884744 | tf_op jit(solution)/shard_map/ppermute | solution.py:19
  (13 other events, 56.0 us)

commit v5 on v4

--- a/solution.py
+++ b/solution.py
@@ -336,8 +336,7 @@
             jnp.sum(target * target, axis=1),
         ]
     )
-    sums = sums + lax.ppermute(sums, "row", [(0, 1), (1, 0), (2, 3), (3, 2)])
-    sums = sums + lax.ppermute(sums, "row", [(0, 2), (1, 3), (2, 0), (3, 1)])
+    sums = sums + sum(shift(sums, "row", 4, by) for by in (2, 1, 3))
     center = sums[0] / D
     spread = sums[1] / D - center * center
     scaler = lax.rsqrt(spread + 1e-05)

time: 167 us -> 163 us (0.976)
  blocking collectives: 38.5 us -> 36.3 us
  waiting for transfers between devices: 48.1 us -> 46.3 us
    ppermute x12 -> x15, starting transfers between devices: 25.4 us -> 32.2 us  [shift(): lax.ppermute(value, axis, [(i, (i + by) % size) for i in range(size)])]
    ppermute x2 -> x0, starting transfers between devices: 6.47 us -> none  [the longest x1 5.21 us: shards(): sums = sums + lax.ppermute(sums, 'row', [(0, 2), (1, 3), (2, 0), (3, 1)])]
    ppermute x2 -> x0, waiting for transfers between devices: 3.42 us -> none  [the longest x1 2.22 us: shards(): sums = sums + lax.ppermute(sums, 'row', [(0, 1), (1, 0), (2, 3), (3, 2)])]
    all_to_all x1, blocking collectives: 19.3 us -> 17.2 us  [shards(): packet = lax.all_to_all(packet, COL, 0, 0, tiled=True).astype(jnp.float32)]
    ppermute x12 -> x15, waiting for transfers between devices: 32.4 us -> 34 us  [shift(): lax.ppermute(value, axis, [(i, (i + by) % size) for i in range(size)])]
  transfers between devices with their start and end apart: 21 -> 22, of which waited for: 11 -> 11; matrix products, arithmetic and copies ran while one was open for 5% -> 5% of each run, Pallas kernels for 4% -> 4%
where the time goes in v5:
time: 163 us; the launch traced here: 162 us
  waiting for transfers between devices  46.3 us (28%)
  starting transfers between devices  41 us (25%)
  blocking collectives  36.3 us (22%)
  Pallas kernels  17.3 us (11%)
  local copies, waits for them, and re-layouts  12.1 us (7%)
  other arithmetic  5.28 us (3%)
  between operations  3.41 us (2%)
    ppermute x15, waiting for transfers between devices, shift(): lax.ppermute(value, axis, [(i, (i + by) % size) for i in range(size)])  34 us
    ppermute x15, starting transfers between devices, shift(): lax.ppermute(value, axis, [(i, (i + by) % size) for i in range(size)])  32.2 us
    all_to_all x1, blocking collectives, shards(): packet = lax.all_to_all(packet, COL, 0, 0, tiled=True).astype(jnp.float32)  17.2 us
    all_to_all x1, blocking collectives, shards(): lax.all_to_all(jnp.broadcast_to(piece[None], (32, 12, PART)), COL, 0, 0,...  12.7 us
    pallas_call x1, Pallas kernels, branch(): pl.pallas_call(branch_kernel, in_specs=[pl.BlockSpec(memory_space=pltpu.S...  10.9 us
    ppermute x6, waiting for transfers between devices, collect(): pieces.append(lax.ppermute(value, ('group', 'y', 'x'), pairs))  7.98 us
    ppermute x6, starting transfers between devices, collect(): pieces.append(lax.ppermute(value, ('group', 'y', 'x'), pairs))  7.53 us
    all_to_all x1, blocking collectives, shards(): lax.all_to_all(jnp.broadcast_to(line[None], (2,) + line.shape), 'group',...  6.45 us
  transfers between devices with their start and end apart: 22, of which 11 were waited for; matrix products, arithmetic and copies ran while one was open for 5% of the time, Pallas kernels for 4%

profile of v5, /device:TPU:1, one launch (start us, length us, event | category | flops | bytes accessed | tf_op | source)
XLA Modules:
  0.0 162.5 jit_solution(6883035546575325481)
XLA Ops:
  6.9 4.3 %collective-permute-done = bf16[48,3072]{1,0:T(8,128)(2,1)} collective-permute-done((bf16[48,3072]{1,0:T(8,128)(2,1)S(1)}, bf16[48,3072]{1,0:T(8,128)(2,1)}, u32[]{:S(2)}, u32[]{:S(2)}) %collective-permute-start) | collective-permute-done | bytes 294944 | tf_op jit(solution)/shard_map/ppermute | solution.py:271
  11.2 3.4 %collective-permute-start.2 = (bf16[2,576,384]{2,1,0:T(8,128)(2,1)S(1)}, bf16[2,576,384]{2,1,0:T(8,128)(2,1)S(1)}, u32[]{:S(2)}, u32[]{:S(2)}) collective-permute-start(bf16[2,576,384]{2,1,0:T(8,128)(2,1)S(1)} %maximum_maximum_fusion.own), channel_id=1, source_target_pairs={{0,32},{32,64},{64,96},{96,0},{1,33},{33,65},{65,97},{97,1},{2,34}... | collective-permute-start | bytes 2654216 | tf_op jit(solution)/shard_map/ppermute | solution.py:19
  14.7 3.0 %collective-permute-start.1 = (bf16[2,576,384]{2,1,0:T(8,128)(2,1)S(1)}, bf16[2,576,384]{2,1,0:T(8,128)(2,1)}, u32[]{:S(2)}, u32[]{:S(2)}) collective-permute-start(bf16[2,576,384]{2,1,0:T(8,128)(2,1)S(1)} %maximum_maximum_fusion.own), channel_id=1, source_target_pairs={{0,96},{32,0},{64,32},{96,64},{1,97},{33,1},{65,33},{97,65},{2,98}... | collective-permute-start | bytes 2654216 | tf_op jit(solution)/shard_map/ppermute | solution.py:19
  18.7 2.8 %collective-permute-start.5 = (bf16[48,3072]{1,0:T(8,128)(2,1)S(1)}, bf16[48,3072]{1,0:T(8,128)(2,1)S(1)}, u32[]{:S(2)}, u32[]{:S(2)}) collective-permute-start(bf16[48,3072]{1,0:T(8,128)(2,1)S(1)} %broadcast_select_fusion.refs_0_), channel_id=1, source_target_pairs={{0,3},{128,140},{1,0},{129,141},{2,1},{130,142},{3,2},{131,143},{4... | collective-permute-start | bytes 884744 | tf_op jit(solution)/shard_map/ppermute | solution.py:285
  22.7 5.7 %collective-permute-done.5.refs_1_ = bf16[48,3072]{1,0:T(8,128)(2,1)S(1)} collective-permute-done((bf16[48,3072]{1,0:T(8,128)(2,1)S(1)}, bf16[48,3072]{1,0:T(8,128)(2,1)S(1)}, u32[]{:S(2)}, u32[]{:S(2)}) %collective-permute-start.5) | collective-permute-done | bytes 294944 | tf_op jit(solution)/shard_map/ppermute | solution.py:285
  29.8 2.3 %collective-permute-done.7.refs_3_ = bf16[48,3072]{1,0:T(8,128)(2,1)S(1)} collective-permute-done((bf16[48,3072]{1,0:T(8,128)(2,1)S(1)}, bf16[48,3072]{1,0:T(8,128)(2,1)S(1)}, u32[]{:S(2)}, u32[]{:S(2)}) %collective-permute-start.7) | collective-permute-done | bytes 294944 | tf_op jit(solution)/shard_map/ppermute | solution.py:285
  36.3 2.6 %collective-permute-start.8 = (bf16[4,48,3072]{2,1,0:T(8,128)(2,1)S(1)}, bf16[4,48,3072]{2,1,0:T(8,128)(2,1)}, u32[]{:S(2)}, u32[]{:S(2)}) collective-permute-start(bf16[4,48,3072]{2,1,0:T(8,128)(2,1)S(1)} %shard_map.123.refs_0_), channel_id=1, source_target_pairs={{0,12},{128,131},{1,13},{129,128},{2,14},{130,129},{3,15},{131,130... | collective-permute-start | bytes 3538952 | tf_op jit(solution)/shard_map/ppermute | solution.py:285
  40.0 16.8 %collective-permute-done.2.before = bf16[2,576,384]{2,1,0:T(8,128)(2,1)S(1)} collective-permute-done((bf16[2,576,384]{2,1,0:T(8,128)(2,1)S(1)}, bf16[2,576,384]{2,1,0:T(8,128)(2,1)S(1)}, u32[]{:S(2)}, u32[]{:S(2)}) %collective-permute-start.2) | collective-permute-done | bytes 884768 | tf_op jit(solution)/shard_map/ppermute | solution.py:19
  57.6 1.8 %slice_bitcast_fusion = bf16[576,384]{1,0:T(8,128)(2,1)} fusion(bf16[2,576,384]{2,1,0:T(8,128)(2,1)} %collective-permute-done.1.after), kind=kLoop, calls=%fused_computation.13 | loop fusion | bytes 884736 | tf_op jit(solution)/shard_map/squeeze | solution.py:317
  59.4 3.6 %collective-permute-start.4 = (bf16[576,384]{1,0:T(8,128)(2,1)}, bf16[576,384]{1,0:T(8,128)(2,1)}, u32[]{:S(2)}, u32[]{:S(2)}) collective-permute-start(bf16[576,384]{1,0:T(8,128)(2,1)} %slice_bitcast_fusion), channel_id=1, source_target_pairs={{0,96},{32,0},{64,32},{96,64},{1,97},{33,1},{65,33},{97,65},{2,98}... | collective-permute-start | bytes 1327112 | tf_op jit(solution)/shard_map/ppermute | solution.py:19
  63.3 6.5 %all_to_all.15 = bf16[2,4,48,3072]{3,2,1,0:T(8,128)(2,1)S(1)} all-to-all(bf16[2,4,48,3072]{3,2,1,0:T(8,128)(2,1)S(1)} %broadcast_in_dim.14), channel_id=1, replica_groups=mesh['group'=2,'row'=4,'zl'=2,'y'=4,'x'=4] {'group'}, dimensions={0} | all-to-all | bytes 4718592 | tf_op jit(solution)/shard_map/all_to_all | solution.py:290
  70.8 4.4 %collective-permute-done.3.far_top = bf16[576,384]{1,0:T(8,128)(2,1)S(1)} collective-permute-done((bf16[576,384]{1,0:T(8,128)(2,1)}, bf16[576,384]{1,0:T(8,128)(2,1)S(1)}, u32[]{:S(2)}, u32[]{:S(2)}) %collective-permute-start.3) | collective-permute-done | bytes 442400 | tf_op jit(solution)/shard_map/ppermute | solution.py:19
  76.6 4.3 %shard_map.122.normed = bf16[1024,1536]{1,0:T(8,128)(2,1)S(1)} custom-call(s32[4]{0:T(128)S(1)} %pad_add_fusion.place, bf16[2,576,384]{2,1,0:T(8,128)(2,1)S(1)} %maximum_maximum_fusion.own, bf16[2,576,384]{2,1,0:T(8,128)(2,1)} %collective-permute-done.1.after, bf16[2,576,384]{2,1,0:T(8,128)(2,1)S(1)} %collective-permute-done.2.before, ...), custom_call_target="tpu_custom_call" | custom-call | flops 30000001024 | bytes 6291456 | tf_op jit(solution)/shard_map/pallas_call | solution.py:42
  80.9 10.9 %shard_map.124 = (f32[256,384]{1,0:T(8,128)S(1)}, bf16[256,384]{1,0:T(8,128)(2,1)S(1)}, bf16[256,384]{1,0:T(8,128)(2,1)S(1)}, bf16[256,384]{1,0:T(8,128)(2,1)S(1)}) custom-call(s32[4]{0:T(128)S(1)} %pad_add_fusion.place, bf16[1024,1536]{1,0:T(8,128)(2,1)S(1)} %shard_map.122.normed, bf16[4,48,3072]{2,1,0:T(8,128)(2,1)S(1)} %shard_map.123.refs_0_, ...), custom_call_target="tpu_custom_call" | custom-call | flops 6442450944 | bytes 10485760 | tf_op jit(solution)/shard_map/pallas_call | solution.py:153
  91.8 2.1 %collective-permute-start.14 = (bf16[256,384]{1,0:T(8,128)(2,1)S(1)}, bf16[256,384]{1,0:T(8,128)(2,1)S(1)}, u32[]{:S(2)}, u32[]{:S(2)}) collective-permute-start(bf16[256,384]{1,0:T(8,128)(2,1)S(1)} %get-tuple-element.29), channel_id=1, source_target_pairs={{0,64},{32,96},{64,0},{96,32},{1,65},{33,97},{65,1},{97,33},{2,66}... | collective-permute-start | bytes 589832 | tf_op jit(solution)/shard_map/ppermute | solution.py:19
  93.9 2.6 %collective-permute-start.15 = (bf16[256,384]{1,0:T(8,128)(2,1)S(1)}, bf16[256,384]{1,0:T(8,128)(2,1)S(1)}, u32[]{:S(2)}, u32[]{:S(2)}) collective-permute-start(bf16[256,384]{1,0:T(8,128)(2,1)S(1)} %get-tuple-element.30), channel_id=1, source_target_pairs={{0,32},{32,64},{64,96},{96,0},{1,33},{33,65},{65,97},{97,1},{2,34}... | collective-permute-start | bytes 589832 | tf_op jit(solution)/shard_map/ppermute | solution.py:19
  99.0 9.1 %collective-permute-done.14 = bf16[256,384]{1,0:T(8,128)(2,1)S(1)} collective-permute-done((bf16[256,384]{1,0:T(8,128)(2,1)S(1)}, bf16[256,384]{1,0:T(8,128)(2,1)S(1)}, u32[]{:S(2)}, u32[]{:S(2)}) %collective-permute-start.14) | collective-permute-done | bytes 196640 | tf_op jit(solution)/shard_map/ppermute | solution.py:19
  109.0 5.3 %collective-permute-start.17 = (f32[5,256]{1,0:T(8,128)S(1)}, f32[5,256]{1,0:T(8,128)S(1)}, u32[]{:S(2)}, u32[]{:S(2)}) collective-permute-start(f32[5,256]{1,0:T(8,128)S(1)} %stack.60), channel_id=1, source_target_pairs={{0,64},{32,96},{64,0},{96,32},{1,65},{33,97},{65,1},{97,33},{2,66}... | collective-permute-start | bytes 15368 | tf_op jit(solution)/shard_map/ppermute | solution.py:19
  114.3 1.5 collective-permute-start.18
  115.7 2.1 %collective-permute-start.19 = (f32[5,256]{1,0:T(8,128)S(1)}, f32[5,256]{1,0:T(8,128)S(1)}, u32[]{:S(2)}, u32[]{:S(2)}) collective-permute-start(f32[5,256]{1,0:T(8,128)S(1)} %stack.60), channel_id=1, source_target_pairs={{0,96},{32,0},{64,32},{96,64},{1,97},{33,1},{65,33},{97,65},{2,98}... | collective-permute-start | bytes 15368 | tf_op jit(solution)/shard_map/ppermute | solution.py:19
  120.1 3.8 %collective-permute-start.20 = (bf16[384,384]{1,0:T(8,128)(2,1)S(1)}, bf16[384,384]{1,0:T(8,128)(2,1)S(1)}, u32[]{:S(2)}, u32[]{:S(2)}) collective-permute-start(bf16[384,384]{1,0:T(8,128)(2,1)S(1)} %fusion.9), channel_id=1, source_target_pairs={{0,128},{128,0},{1,129},{129,1},{2,130},{130,2},{3,131},{131,3},{4... | collective-permute-start | bytes 884744 | tf_op jit(solution)/shard_map/ppermute | solution.py:19
  125.5 17.2 %all_to_all.16 = bf16[32,14,384]{2,1,0:T(8,128)(2,1)S(1)} all-to-all(bf16[32,14,384]{2,1,0:T(8,128)(2,1)S(1)} %pad_maximum_fusion), channel_id=1, replica_groups=mesh['group'=2,'row'=4,'zl'=2,'y'=4,'x'=4] {'zl','y','x'}, dimensions={0} | all-to-all | bytes 688128 | tf_op jit(solution)/shard_map/all_to_all | solution.py:368
  142.8 12.7 %all_to_all.17 = bf16[32,12,384]{2,1,0:T(8,128)(2,1)S(1)} all-to-all(bf16[32,12,384]{2,1,0:T(8,128)(2,1)S(1)} %broadcast_in_dim.22), channel_id=1, replica_groups=mesh['group'=2,'row'=4,'zl'=2,'y'=4,'x'=4] {'zl','y','x'}, dimensions={0} | all-to-all | bytes 589824 | tf_op jit(solution)/shard_map/all_to_all | solution.py:372
  155.6 2.8 %collective-permute-start.21 = (bf16[384,384]{1,0:T(8,128)(2,1)S(1)}, bf16[384,384]{1,0:T(8,128)(2,1)S(1)}, u32[]{:S(2)}, u32[]{:S(2)}) collective-permute-start(bf16[384,384]{1,0:T(8,128)(2,1)S(1)} %reshape.119), channel_id=1, source_target_pairs={{0,128},{128,0},{1,129},{129,1},{2,130},{130,2},{3,131},{131,3},{4... | collective-permute-start | bytes 884744 | tf_op jit(solution)/shard_map/ppermute | solution.py:19
  (108 shorter events, 27.5 us)
Async XLA Ops:
  3.3 8.0 %collective-permute-start = (bf16[48,3072]{1,0:T(8,128)(2,1)S(1)}, bf16[48,3072]{1,0:T(8,128)(2,1)}, u32[]{:S(2)}, u32[]{:S(2)}) collective-permute-start(bf16[48,3072]{1,0:T(8,128)(2,1)S(1)} %maximum_maximum_fusion.1), channel_id=1, source_target_pairs={{0,16},{144,128},{1,17},{145,129},{2,18},{146,130},{3,19},{147,131... | collective-permute-start | bytes 884744 | tf_op jit(solution)/shard_map/ppermute | solution.py:271
  11.2 45.6 %collective-permute-start.2 = (bf16[2,576,384]{2,1,0:T(8,128)(2,1)S(1)}, bf16[2,576,384]{2,1,0:T(8,128)(2,1)S(1)}, u32[]{:S(2)}, u32[]{:S(2)}) collective-permute-start(bf16[2,576,384]{2,1,0:T(8,128)(2,1)S(1)} %maximum_maximum_fusion.own), channel_id=1, source_target_pairs={{0,32},{32,64},{64,96},{96,0},{1,33},{33,65},{65,97},{97,1},{2,34}... | collective-permute-start | bytes 2654216 | tf_op jit(solution)/shard_map/ppermute | solution.py:19
  14.7 42.9 %collective-permute-start.1 = (bf16[2,576,384]{2,1,0:T(8,128)(2,1)S(1)}, bf16[2,576,384]{2,1,0:T(8,128)(2,1)}, u32[]{:S(2)}, u32[]{:S(2)}) collective-permute-start(bf16[2,576,384]{2,1,0:T(8,128)(2,1)S(1)} %maximum_maximum_fusion.own), channel_id=1, source_target_pairs={{0,96},{32,0},{64,32},{96,64},{1,97},{33,1},{65,33},{97,65},{2,98}... | collective-permute-start | bytes 2654216 | tf_op jit(solution)/shard_map/ppermute | solution.py:19
  18.7 9.6 %collective-permute-start.5 = (bf16[48,3072]{1,0:T(8,128)(2,1)S(1)}, bf16[48,3072]{1,0:T(8,128)(2,1)S(1)}, u32[]{:S(2)}, u32[]{:S(2)}) collective-permute-start(bf16[48,3072]{1,0:T(8,128)(2,1)S(1)} %broadcast_select_fusion.refs_0_), channel_id=1, source_target_pairs={{0,3},{128,140},{1,0},{129,141},{2,1},{130,142},{3,2},{131,143},{4... | collective-permute-start | bytes 884744 | tf_op jit(solution)/shard_map/ppermute | solution.py:285
  21.6 7.5 %collective-permute-start.6 = (bf16[48,3072]{1,0:T(8,128)(2,1)S(1)}, bf16[48,3072]{1,0:T(8,128)(2,1)S(1)}, u32[]{:S(2)}, u32[]{:S(2)}) collective-permute-start(bf16[48,3072]{1,0:T(8,128)(2,1)S(1)} %broadcast_select_fusion.refs_0_), channel_id=1, source_target_pairs={{0,2},{128,136},{1,3},{129,137},{2,0},{130,138},{3,1},{131,139},{4... | collective-permute-start | bytes 884744 | tf_op jit(solution)/shard_map/ppermute | solution.py:285
  21.9 10.2 %collective-permute-start.7 = (bf16[48,3072]{1,0:T(8,128)(2,1)S(1)}, bf16[48,3072]{1,0:T(8,128)(2,1)S(1)}, u32[]{:S(2)}, u32[]{:S(2)}) collective-permute-start(bf16[48,3072]{1,0:T(8,128)(2,1)S(1)} %broadcast_select_fusion.refs_0_), channel_id=1, source_target_pairs={{0,1},{128,132},{1,2},{129,133},{2,3},{130,134},{3,0},{131,135},{4... | collective-permute-start | bytes 884744 | tf_op jit(solution)/shard_map/ppermute | solution.py:285
  36.3 26.7 %copy-start.13 = (bf16[1536]{0:T(1024)(128)(2,1)S(1)}, bf16[1536]{0:T(1024)(128)(2,1)}, u32[]{:S(2)}) copy-start(bf16[1536]{0:T(1024)(128)(2,1)} %param.14) | copy-start | bytes 9220
  36.3 33.5 %collective-permute-start.8 = (bf16[4,48,3072]{2,1,0:T(8,128)(2,1)S(1)}, bf16[4,48,3072]{2,1,0:T(8,128)(2,1)}, u32[]{:S(2)}, u32[]{:S(2)}) collective-permute-start(bf16[4,48,3072]{2,1,0:T(8,128)(2,1)S(1)} %shard_map.123.refs_0_), channel_id=1, source_target_pairs={{0,12},{128,131},{1,13},{129,128},{2,14},{130,129},{3,15},{131,130... | collective-permute-start | bytes 3538952 | tf_op jit(solution)/shard_map/ppermute | solution.py:285
  38.9 31.4 %collective-permute-start.9 = (bf16[4,48,3072]{2,1,0:T(8,128)(2,1)S(1)}, bf16[4,48,3072]{2,1,0:T(8,128)(2,1)}, u32[]{:S(2)}, u32[]{:S(2)}) collective-permute-start(bf16[4,48,3072]{2,1,0:T(8,128)(2,1)S(1)} %shard_map.123.refs_0_), channel_id=1, source_target_pairs={{0,8},{128,130},{1,9},{129,131},{2,10},{130,128},{3,11},{131,129},... | collective-permute-start | bytes 3538952 | tf_op jit(solution)/shard_map/ppermute | solution.py:285
  39.4 31.0 %collective-permute-start.10 = (bf16[4,48,3072]{2,1,0:T(8,128)(2,1)S(1)}, bf16[4,48,3072]{2,1,0:T(8,128)(2,1)}, u32[]{:S(2)}, u32[]{:S(2)}) collective-permute-start(bf16[4,48,3072]{2,1,0:T(8,128)(2,1)S(1)} %shard_map.123.refs_0_), channel_id=1, source_target_pairs={{0,4},{128,129},{1,5},{129,130},{2,6},{130,131},{3,7},{131,128},{4... | collective-permute-start | bytes 3538952 | tf_op jit(solution)/shard_map/ppermute | solution.py:285
  57.6 17.6 %collective-permute-start.3 = (bf16[576,384]{1,0:T(8,128)(2,1)}, bf16[576,384]{1,0:T(8,128)(2,1)S(1)}, u32[]{:S(2)}, u32[]{:S(2)}) collective-permute-start(bf16[576,384]{1,0:T(8,128)(2,1)} %slice_bitcast_fusion.1), channel_id=1, source_target_pairs={{0,32},{32,64},{64,96},{96,0},{1,33},{33,65},{65,97},{97,1},{2,34}... | collective-permute-start | bytes 1327112 | tf_op jit(solution)/shard_map/ppermute | solution.py:19
  59.4 17.1 %collective-permute-start.4 = (bf16[576,384]{1,0:T(8,128)(2,1)}, bf16[576,384]{1,0:T(8,128)(2,1)}, u32[]{:S(2)}, u32[]{:S(2)}) collective-permute-start(bf16[576,384]{1,0:T(8,128)(2,1)} %slice_bitcast_fusion), channel_id=1, source_target_pairs={{0,96},{32,0},{64,32},{96,64},{1,97},{33,1},{65,33},{97,65},{2,98}... | collective-permute-start | bytes 1327112 | tf_op jit(solution)/shard_map/ppermute | solution.py:19
  69.8 11.0 %collective-permute-start.11 = (bf16[4,48,3072]{2,1,0:T(8,128)(2,1)}, bf16[4,48,3072]{2,1,0:T(8,128)(2,1)S(1)}, u32[]{:S(2)}, u32[]{:S(2)}) collective-permute-start(bf16[4,48,3072]{2,1,0:T(8,128)(2,1)} %collective-permute-done.8.refs_1_), channel_id=1, source_target_pairs={{0,128},{128,0},{1,129},{129,1},{2,130},{130,2},{3,131},{131,3},{4... | collective-permute-start | bytes 3538952 | tf_op jit(solution)/shard_map/ppermute | solution.py:19
  70.3 10.6 %collective-permute-start.12 = (bf16[4,48,3072]{2,1,0:T(8,128)(2,1)}, bf16[4,48,3072]{2,1,0:T(8,128)(2,1)S(1)}, u32[]{:S(2)}, u32[]{:S(2)}) collective-permute-start(bf16[4,48,3072]{2,1,0:T(8,128)(2,1)} %collective-permute-done.9.refs_2_), channel_id=1, source_target_pairs={{0,128},{128,0},{1,129},{129,1},{2,130},{130,2},{3,131},{131,3},{4... | collective-permute-start | bytes 3538952 | tf_op jit(solution)/shard_map/ppermute | solution.py:19
  70.4 10.5 %collective-permute-start.13 = (bf16[4,48,3072]{2,1,0:T(8,128)(2,1)}, bf16[4,48,3072]{2,1,0:T(8,128)(2,1)S(1)}, u32[]{:S(2)}, u32[]{:S(2)}) collective-permute-start(bf16[4,48,3072]{2,1,0:T(8,128)(2,1)} %collective-permute-done.10.refs_3_), channel_id=1, source_target_pairs={{0,128},{128,0},{1,129},{129,1},{2,130},{130,2},{3,131},{131,3},{4... | collective-permute-start | bytes 3538952 | tf_op jit(solution)/shard_map/ppermute | solution.py:19
  80.9 16.6 %copy-start.14 = (bf16[384]{0:T(512)(128)(2,1)S(1)}, bf16[384]{0:T(512)(128)(2,1)}, u32[]{:S(2)}) copy-start(bf16[384]{0:T(512)(128)(2,1)} %param.15) | copy-start | bytes 2308
  91.8 16.3 %collective-permute-start.14 = (bf16[256,384]{1,0:T(8,128)(2,1)S(1)}, bf16[256,384]{1,0:T(8,128)(2,1)S(1)}, u32[]{:S(2)}, u32[]{:S(2)}) collective-permute-start(bf16[256,384]{1,0:T(8,128)(2,1)S(1)} %get-tuple-element.29), channel_id=1, source_target_pairs={{0,64},{32,96},{64,0},{96,32},{1,65},{33,97},{65,1},{97,33},{2,66}... | collective-permute-start | bytes 589832 | tf_op jit(solution)/shard_map/ppermute | solution.py:19
  93.9 14.6 %collective-permute-start.15 = (bf16[256,384]{1,0:T(8,128)(2,1)S(1)}, bf16[256,384]{1,0:T(8,128)(2,1)S(1)}, u32[]{:S(2)}, u32[]{:S(2)}) collective-permute-start(bf16[256,384]{1,0:T(8,128)(2,1)S(1)} %get-tuple-element.30), channel_id=1, source_target_pairs={{0,32},{32,64},{64,96},{96,0},{1,33},{33,65},{65,97},{97,1},{2,34}... | collective-permute-start | bytes 589832 | tf_op jit(solution)/shard_map/ppermute | solution.py:19
  96.6 12.0 %collective-permute-start.16 = (bf16[256,384]{1,0:T(8,128)(2,1)S(1)}, bf16[256,384]{1,0:T(8,128)(2,1)S(1)}, u32[]{:S(2)}, u32[]{:S(2)}) collective-permute-start(bf16[256,384]{1,0:T(8,128)(2,1)S(1)} %get-tuple-element.31), channel_id=1, source_target_pairs={{0,96},{32,0},{64,32},{96,64},{1,97},{33,1},{65,33},{97,65},{2,98}... | collective-permute-start | bytes 589832 | tf_op jit(solution)/shard_map/ppermute | solution.py:19
  109.0 8.9 %collective-permute-start.17 = (f32[5,256]{1,0:T(8,128)S(1)}, f32[5,256]{1,0:T(8,128)S(1)}, u32[]{:S(2)}, u32[]{:S(2)}) collective-permute-start(f32[5,256]{1,0:T(8,128)S(1)} %stack.60), channel_id=1, source_target_pairs={{0,64},{32,96},{64,0},{96,32},{1,65},{33,97},{65,1},{97,33},{2,66}... | collective-permute-start | bytes 15368 | tf_op jit(solution)/shard_map/ppermute | solution.py:19
  114.3 4.9 %collective-permute-start.18 = (f32[5,256]{1,0:T(8,128)S(1)}, f32[5,256]{1,0:T(8,128)S(1)}, u32[]{:S(2)}, u32[]{:S(2)}) collective-permute-start(f32[5,256]{1,0:T(8,128)S(1)} %stack.60), channel_id=1, source_target_pairs={{0,32},{32,64},{64,96},{96,0},{1,33},{33,65},{65,97},{97,1},{2,34}... | collective-permute-start | bytes 15368 | tf_op jit(solution)/shard_map/ppermute | solution.py:19
  115.7 3.7 %collective-permute-start.19 = (f32[5,256]{1,0:T(8,128)S(1)}, f32[5,256]{1,0:T(8,128)S(1)}, u32[]{:S(2)}, u32[]{:S(2)}) collective-permute-start(f32[5,256]{1,0:T(8,128)S(1)} %stack.60), channel_id=1, source_target_pairs={{0,96},{32,0},{64,32},{96,64},{1,97},{33,1},{65,33},{97,65},{2,98}... | collective-permute-start | bytes 15368 | tf_op jit(solution)/shard_map/ppermute | solution.py:19
  120.1 5.0 %collective-permute-start.20 = (bf16[384,384]{1,0:T(8,128)(2,1)S(1)}, bf16[384,384]{1,0:T(8,128)(2,1)S(1)}, u32[]{:S(2)}, u32[]{:S(2)}) collective-permute-start(bf16[384,384]{1,0:T(8,128)(2,1)S(1)} %fusion.9), channel_id=1, source_target_pairs={{0,128},{128,0},{1,129},{129,1},{2,130},{130,2},{3,131},{131,3},{4... | collective-permute-start | bytes 884744 | tf_op jit(solution)/shard_map/ppermute | solution.py:19
  155.6 4.6 %collective-permute-start.21 = (bf16[384,384]{1,0:T(8,128)(2,1)S(1)}, bf16[384,384]{1,0:T(8,128)(2,1)S(1)}, u32[]{:S(2)}, u32[]{:S(2)}) collective-permute-start(bf16[384,384]{1,0:T(8,128)(2,1)S(1)} %reshape.119), channel_id=1, source_target_pairs={{0,128},{128,0},{1,129},{129,1},{2,130},{130,2},{3,131},{131,3},{4... | collective-permute-start | bytes 884744 | tf_op jit(solution)/shard_map/ppermute | solution.py:19
  (14 other events, 70.5 us)

commit v6 on v5

--- a/solution.py
+++ b/solution.py
@@ -60,7 +60,15 @@
     )(place, own, after, before, far_top, far_bottom, gain)
 
 
-SPANS = ((0, 512), (1024, 512), (512, 512), (1536, 512), (2048, 1024))
+SPANS = (
+    (0, 48, 0, 256, None),
+    (0, 48, 1024, 256, None),
+    (0, 48, 256, 768, None),
+    (0, 48, 1280, 768, None),
+    (0, 32, 2048, 1024, (0, 0)),
+    (32, 16, 2048, 512, (0, 1024)),
+    (32, 16, 2560, 512, (16, 1024)),
+)
 
 
 def branch_kernel(place, normed, *refs):
@@ -70,16 +78,19 @@
     weights, hidden, down, sems = refs[12:]
 
     def copy(side, k, span, along_y):
-        start, width = SPANS[span]
+        top, height, start, width, spot = SPANS[span]
         columns = pl.ds(start, width)
-        block = weights.at[side]
+        if spot is None:
+            block, rows, target = weights.at[side], pl.ds(0, 48), columns
+        else:
+            block = down.at[side]
+            rows, target = pl.ds(spot[0], height), pl.ds(spot[1], width)
         if along_y:
-            block = block.at[lax.rem(y + k, 4), :, :, columns]
+            block = block.at[lax.rem(y + k, 4), :, rows, target]
         else:
-            block = block.at[:, lax.rem(x + k, 4), :, columns]
-        return pltpu.make_async_copy(
-            sources[side][k].at[:, :, columns], block, sems.at[side, k, span]
-        )
+            block = block.at[:, lax.rem(x + k, 4), rows, target]
+        source = sources[side][k].at[:, pl.ds(top, height), columns]
+        return pltpu.make_async_copy(source, block, sems.at[side, k, span])
 
     def start_all(side, along_y, span):
         for k in range(4):
@@ -91,7 +102,7 @@
                 for k in range(4):
                     copy(side, k, span, True).wait()
 
-    for span in range(5):
+    for span in range(7):
         for side in (0, 1):
             along = group == side
 
@@ -117,7 +128,7 @@
     for n in range(4):
         if n == 0:
             wait_all((0, 1))
-        if n == 2:
+        if n == 1:
             wait_all((2, 3))
         gate = project(0, n)
         upward = project(1, n)
@@ -126,23 +137,13 @@
         target = pl.multiple_of(lax.rem(n + 2 * group, 4) * 256, 256)
         hidden[:, pl.ds(target, 256)] = value.astype(jnp.bfloat16)
 
-    wait_all((4,))
-
-    def unpack(c, carry):
-        rows = pl.multiple_of(c * 32, 32)
-        for side in (0, 1):
-            half = weights.at[side, c // 4, lax.rem(c, 4)]
-            down[pl.ds(side * 512 + rows, 32), 0:1024] = half[0:32, 2048:3072]
-            tail = half[32:48, 2048:3072]
-            down[pl.ds(side * 512 + rows, 16), 1024:1536] = tail[:, :512]
-            down[pl.ds(side * 512 + rows + 16, 16), 1024:1536] = tail[:, 512:]
-        return carry
-
-    lax.fori_loop(0, 16, unpack, 0)
+    wait_all((4, 5, 6))
     for j, out in ((2, away2), (1, away1), (3, away3), (0, part)):
         start = pl.multiple_of(lax.rem(row + j, 4) * PART, PART)
         value = jnp.dot(
-            hidden[...], down[:, pl.ds(start, PART)], preferred_element_type=jnp.float32
+            hidden[...],
+            down[:, :, :, :, pl.ds(start, PART)].reshape(1024, PART),
+            preferred_element_type=jnp.float32,
         )
         out[...] = value.astype(out.dtype)
 
@@ -157,10 +158,10 @@
         out_specs=[vmem] * 4,
         out_shape=[jax.ShapeDtypeStruct((256, PART), jnp.float32), narrow, narrow, narrow],
         scratch_shapes=[
-            pltpu.VMEM((2, 4, 4, 48, 3072), jnp.bfloat16),
+            pltpu.VMEM((2, 4, 4, 48, 2048), jnp.bfloat16),
             pltpu.VMEM((256, 1024), jnp.bfloat16),
-            pltpu.VMEM((1024, D), jnp.bfloat16),
-            pltpu.SemaphoreType.DMA((2, 4, 5)),
+            pltpu.VMEM((2, 4, 4, 32, D), jnp.bfloat16),
+            pltpu.SemaphoreType.DMA((2, 4, 7)),
         ],
         compiler_params=pltpu.CompilerParams(vmem_limit_bytes=40 * MIB),
         cost_estimate=pl.CostEstimate(
@@ -241,6 +242,36 @@
             flops=2 * 256 * SW * 640, bytes_accessed=2 * MIB, transcendentals=0
         ),
     )(place, own, after, before, far_top, far_bottom, weight)
+
+
+def pack_kernel(gate, up, down, out, sems):
+    copies = [
+        pltpu.make_async_copy(gate, out.at[:, 0:1024], sems.at[0]),
+        pltpu.make_async_copy(up, out.at[:, 1024:2048], sems.at[1]),
+        pltpu.make_async_copy(down.at[:, 0:1024], out.at[0:32, 2048:3072], sems.at[2]),
+        pltpu.make_async_copy(
+            down.at[0:16, 1024:1536], out.at[32:48, 2048:2560], sems.at[3]
+        ),
+        pltpu.make_async_copy(
+            down.at[16:32, 1024:1536], out.at[32:48, 2560:3072], sems.at[4]
+        ),
+    ]
+    for copy in copies:
+        copy.start()
+    for copy in copies:
+        copy.wait()
+
+
+def pack(gate, up, down):
+    return pl.pallas_call(
+        pack_kernel,
+        in_specs=[pl.BlockSpec(memory_space=pl.ANY)] * 3,
+        out_specs=pl.BlockSpec(memory_space=pltpu.VMEM),
+        out_shape=jax.ShapeDtypeStruct((48, 3072), jnp.bfloat16),
+        scratch_shapes=[pltpu.SemaphoreType.DMA((5,))],
+        compiler_params=pltpu.CompilerParams(vmem_limit_bytes=56 * MIB),
+        cost_estimate=pl.CostEstimate(flops=0, bytes_accessed=MIB, transcendentals=0),
+    )(gate, up, down)
 
 
 def shards(
@@ -260,14 +291,7 @@
     images = teacher_tokens.shape[0]
     place = jnp.stack([row, group, lax.axis_index("y"), lax.axis_index("x")]).astype(jnp.int32)
 
-    down = jnp.concatenate(
-        [
-            down_weight[:, :1024],
-            jnp.concatenate([down_weight[:16, 1024:], down_weight[16:, 1024:]], axis=1),
-        ],
-        axis=0,
-    )
-    block = jnp.concatenate([gate_weight, up_weight, down], axis=1)
+    block = pack(gate_weight, up_weight, down_weight)
     twin = lax.ppermute(block, ("group", "zl"), [(0, 1), (3, 2)])
     block = jnp.where(group == zl, block, twin)
     def collect(value, first):

time: 163 us -> 163 us (level)
  waiting for transfers between devices: 46.3 us -> 50.4 us
  starting transfers between devices: 41 us -> 39.1 us
    ppermute x15, waiting for transfers between devices: 34 us -> 37.9 us  [shift(): lax.ppermute(value, axis, [(i, (i + by) % size) for i in range(size)])]
    ppermute x15, starting transfers between devices: 32.2 us -> 30.2 us  [shift(): lax.ppermute(value, axis, [(i, (i + by) % size) for i in range(size)])]
    pallas_call x0 -> x1, Pallas kernels: none -> 1.78 us  [pack(): pl.pallas_call(pack_kernel, in_specs=[pl.BlockSpec(memory_space=pl.ANY)]...]
    slice x2 -> x0, local copies, waits for them, and re-layouts: 1.66 us -> none  [the longest x1 0.84 us: shards(): down_weight[:, :1024]]
    unnamed x33 -> x31, local copies, waits for them, and re-layouts: 5.86 us -> 5.88 us
where the time goes in v6:
time: 163 us; the launch traced here: 162 us
  waiting for transfers between devices  50.4 us (31%)
  starting transfers between devices  39.1 us (24%)
  blocking collectives  35.4 us (22%)
  Pallas kernels  18.6 us (11%)
  local copies, waits for them, and re-layouts  10.5 us (6%)
  other arithmetic  4.29 us (3%)
  between operations  3.42 us (2%)
    ppermute x15, waiting for transfers between devices, shift(): lax.ppermute(value, axis, [(i, (i + by) % size) for i in range(size)])  37.9 us
    ppermute x15, starting transfers between devices, shift(): lax.ppermute(value, axis, [(i, (i + by) % size) for i in range(size)])  30.2 us
    all_to_all x1, blocking collectives, shards(): packet = lax.all_to_all(packet, COL, 0, 0, tiled=True).astype(jnp.float32)  16 us
    all_to_all x1, blocking collectives, shards(): lax.all_to_all(jnp.broadcast_to(piece[None], (32, 12, PART)), COL, 0, 0,...  12.7 us
    pallas_call x1, Pallas kernels, branch(): pl.pallas_call(branch_kernel, in_specs=[pl.BlockSpec(memory_space=pltpu.S...  10.5 us
    ppermute x6, waiting for transfers between devices, collect(): pieces.append(lax.ppermute(value, ('group', 'y', 'x'), pairs))  7.97 us
    ppermute x6, starting transfers between devices, collect(): pieces.append(lax.ppermute(value, ('group', 'y', 'x'), pairs))  7.53 us
    all_to_all x1, blocking collectives, shards(): lax.all_to_all(jnp.broadcast_to(line[None], (2,) + line.shape), 'group',...  6.69 us
  transfers between devices with their start and end apart: 22, of which 11 were waited for; matrix products, arithmetic and copies ran while one was open for 5% of the time, Pallas kernels for 4%

profile of v6, /device:TPU:1, one launch (start us, length us, event | category | flops | bytes accessed | tf_op | source)
XLA Modules:
  0.0 162.5 jit_solution(9172671015142444295)
XLA Ops:
  0.7 1.8 %shard_map.122 = bf16[48,3072]{1,0:T(8,128)(2,1)} custom-call(bf16[48,1024]{1,0:T(8,128)(2,1)} %gate.1, bf16[48,1024]{1,0:T(8,128)(2,1)} %up.1, bf16[32,1536]{1,0:T(8,128)(2,1)} %down.1), custom_call_target="tpu_custom_call" | custom-call | bytes 1048576 | tf_op jit(solution)/shard_map/pallas_call | solution.py:266
  6.1 4.5 %collective-permute-done = bf16[48,3072]{1,0:T(8,128)(2,1)} collective-permute-done((bf16[48,3072]{1,0:T(8,128)(2,1)}, bf16[48,3072]{1,0:T(8,128)(2,1)}, u32[]{:S(2)}, u32[]{:S(2)}) %collective-permute-start) | collective-permute-done | bytes 294944 | tf_op jit(solution)/shard_map/ppermute | solution.py:295
  10.6 3.4 %collective-permute-start.2 = (bf16[2,576,384]{2,1,0:T(8,128)(2,1)S(1)}, bf16[2,576,384]{2,1,0:T(8,128)(2,1)S(1)}, u32[]{:S(2)}, u32[]{:S(2)}) collective-permute-start(bf16[2,576,384]{2,1,0:T(8,128)(2,1)S(1)} %maximum_maximum_fusion.own), channel_id=1, source_target_pairs={{0,32},{32,64},{64,96},{96,0},{1,33},{33,65},{65,97},{97,1},{2,34}... | collective-permute-start | bytes 2654216 | tf_op jit(solution)/shard_map/ppermute | solution.py:19
  14.0 3.0 %collective-permute-start.1 = (bf16[2,576,384]{2,1,0:T(8,128)(2,1)S(1)}, bf16[2,576,384]{2,1,0:T(8,128)(2,1)}, u32[]{:S(2)}, u32[]{:S(2)}) collective-permute-start(bf16[2,576,384]{2,1,0:T(8,128)(2,1)S(1)} %maximum_maximum_fusion.own), channel_id=1, source_target_pairs={{0,96},{32,0},{64,32},{96,64},{1,97},{33,1},{65,33},{97,65},{2,98}... | collective-permute-start | bytes 2654216 | tf_op jit(solution)/shard_map/ppermute | solution.py:19
  18.1 2.8 %collective-permute-start.5 = (bf16[48,3072]{1,0:T(8,128)(2,1)S(1)}, bf16[48,3072]{1,0:T(8,128)(2,1)S(1)}, u32[]{:S(2)}, u32[]{:S(2)}) collective-permute-start(bf16[48,3072]{1,0:T(8,128)(2,1)S(1)} %broadcast_select_fusion.refs_0_), channel_id=1, source_target_pairs={{0,3},{128,140},{1,0},{129,141},{2,1},{130,142},{3,2},{131,143},{4... | collective-permute-start | bytes 884744 | tf_op jit(solution)/shard_map/ppermute | solution.py:309
  22.0 5.7 %collective-permute-done.5.refs_1_ = bf16[48,3072]{1,0:T(8,128)(2,1)S(1)} collective-permute-done((bf16[48,3072]{1,0:T(8,128)(2,1)S(1)}, bf16[48,3072]{1,0:T(8,128)(2,1)S(1)}, u32[]{:S(2)}, u32[]{:S(2)}) %collective-permute-start.5) | collective-permute-done | bytes 294944 | tf_op jit(solution)/shard_map/ppermute | solution.py:309
  29.2 2.3 %collective-permute-done.7.refs_3_ = bf16[48,3072]{1,0:T(8,128)(2,1)S(1)} collective-permute-done((bf16[48,3072]{1,0:T(8,128)(2,1)S(1)}, bf16[48,3072]{1,0:T(8,128)(2,1)S(1)}, u32[]{:S(2)}, u32[]{:S(2)}) %collective-permute-start.7) | collective-permute-done | bytes 294944 | tf_op jit(solution)/shard_map/ppermute | solution.py:309
  35.7 2.6 %collective-permute-start.8 = (bf16[4,48,3072]{2,1,0:T(8,128)(2,1)S(1)}, bf16[4,48,3072]{2,1,0:T(8,128)(2,1)}, u32[]{:S(2)}, u32[]{:S(2)}) collective-permute-start(bf16[4,48,3072]{2,1,0:T(8,128)(2,1)S(1)} %shard_map.124.refs_0_), channel_id=1, source_target_pairs={{0,12},{128,131},{1,13},{129,128},{2,14},{130,129},{3,15},{131,130... | collective-permute-start | bytes 3538952 | tf_op jit(solution)/shard_map/ppermute | solution.py:309
  39.4 20.8 %collective-permute-done.2.before = bf16[2,576,384]{2,1,0:T(8,128)(2,1)S(1)} collective-permute-done((bf16[2,576,384]{2,1,0:T(8,128)(2,1)S(1)}, bf16[2,576,384]{2,1,0:T(8,128)(2,1)S(1)}, u32[]{:S(2)}, u32[]{:S(2)}) %collective-permute-start.2) | collective-permute-done | bytes 884768 | tf_op jit(solution)/shard_map/ppermute | solution.py:19
  61.0 3.1 %collective-permute-start.3 = (bf16[576,384]{1,0:T(8,128)(2,1)}, bf16[576,384]{1,0:T(8,128)(2,1)S(1)}, u32[]{:S(2)}, u32[]{:S(2)}) collective-permute-start(bf16[576,384]{1,0:T(8,128)(2,1)} %slice_bitcast_fusion.1), channel_id=1, source_target_pairs={{0,32},{32,64},{64,96},{96,0},{1,33},{33,65},{65,97},{97,1},{2,34}... | collective-permute-start | bytes 1327112 | tf_op jit(solution)/shard_map/ppermute | solution.py:19
  64.2 1.8 %slice_bitcast_fusion = bf16[576,384]{1,0:T(8,128)(2,1)} fusion(bf16[2,576,384]{2,1,0:T(8,128)(2,1)} %collective-permute-done.1.after), kind=kLoop, calls=%fused_computation.13 | loop fusion | bytes 884736 | tf_op jit(solution)/shard_map/squeeze | solution.py:341
  66.7 6.7 %all_to_all.15 = bf16[2,4,48,3072]{3,2,1,0:T(8,128)(2,1)S(1)} all-to-all(bf16[2,4,48,3072]{3,2,1,0:T(8,128)(2,1)S(1)} %broadcast_in_dim.14), channel_id=1, replica_groups=mesh['group'=2,'row'=4,'zl'=2,'y'=4,'x'=4] {'group'}, dimensions={0} | all-to-all | bytes 4718592 | tf_op jit(solution)/shard_map/all_to_all | solution.py:314
  75.5 4.9 %collective-permute-done.4.far_bottom = bf16[576,384]{1,0:T(8,128)(2,1)} collective-permute-done((bf16[576,384]{1,0:T(8,128)(2,1)}, bf16[576,384]{1,0:T(8,128)(2,1)}, u32[]{:S(2)}, u32[]{:S(2)}) %collective-permute-start.4) | collective-permute-done | bytes 442400 | tf_op jit(solution)/shard_map/ppermute | solution.py:19
  80.5 4.3 %shard_map.123.normed = bf16[1024,1536]{1,0:T(8,128)(2,1)S(1)} custom-call(s32[4]{0:T(128)S(1)} %pad_add_fusion.place, bf16[2,576,384]{2,1,0:T(8,128)(2,1)S(1)} %maximum_maximum_fusion.own, bf16[2,576,384]{2,1,0:T(8,128)(2,1)} %collective-permute-done.1.after, bf16[2,576,384]{2,1,0:T(8,128)(2,1)S(1)} %collective-permute-done.2.before, ...), custom_call_target="tpu_custom_call" | custom-call | flops 30000001024 | bytes 6291456 | tf_op jit(solution)/shard_map/pallas_call | solution.py:42
  84.8 10.5 %shard_map.125 = (f32[256,384]{1,0:T(8,128)S(1)}, bf16[256,384]{1,0:T(8,128)(2,1)S(1)}, bf16[256,384]{1,0:T(8,128)(2,1)S(1)}, bf16[256,384]{1,0:T(8,128)(2,1)S(1)}) custom-call(s32[4]{0:T(128)S(1)} %pad_add_fusion.place, bf16[1024,1536]{1,0:T(8,128)(2,1)S(1)} %shard_map.123.normed, bf16[4,48,3072]{2,1,0:T(8,128)(2,1)S(1)} %shard_map.124.refs_0_, ...), custom_call_target="tpu_custom_call" | custom-call | flops 6442450944 | bytes 10485760 | tf_op jit(solution)/shard_map/pallas_call | solution.py:154
  95.3 2.3 %collective-permute-start.14 = (bf16[256,384]{1,0:T(8,128)(2,1)S(1)}, bf16[256,384]{1,0:T(8,128)(2,1)S(1)}, u32[]{:S(2)}, u32[]{:S(2)}) collective-permute-start(bf16[256,384]{1,0:T(8,128)(2,1)S(1)} %get-tuple-element.29), channel_id=1, source_target_pairs={{0,64},{32,96},{64,0},{96,32},{1,65},{33,97},{65,1},{97,33},{2,66}... | collective-permute-start | bytes 589832 | tf_op jit(solution)/shard_map/ppermute | solution.py:19
  98.7 3.2 %collective-permute-start.16 = (bf16[256,384]{1,0:T(8,128)(2,1)S(1)}, bf16[256,384]{1,0:T(8,128)(2,1)S(1)}, u32[]{:S(2)}, u32[]{:S(2)}) collective-permute-start(bf16[256,384]{1,0:T(8,128)(2,1)S(1)} %get-tuple-element.31), channel_id=1, source_target_pairs={{0,96},{32,0},{64,32},{96,64},{1,97},{33,1},{65,33},{97,65},{2,98}... | collective-permute-start | bytes 589832 | tf_op jit(solution)/shard_map/ppermute | solution.py:19
  103.4 4.1 %collective-permute-done.14 = bf16[256,384]{1,0:T(8,128)(2,1)S(1)} collective-permute-done((bf16[256,384]{1,0:T(8,128)(2,1)S(1)}, bf16[256,384]{1,0:T(8,128)(2,1)S(1)}, u32[]{:S(2)}, u32[]{:S(2)}) %collective-permute-start.14) | collective-permute-done | bytes 196640 | tf_op jit(solution)/shard_map/ppermute | solution.py:19
  107.6 4.8 %collective-permute-done.15 = bf16[256,384]{1,0:T(8,128)(2,1)S(1)} collective-permute-done((bf16[256,384]{1,0:T(8,128)(2,1)S(1)}, bf16[256,384]{1,0:T(8,128)(2,1)S(1)}, u32[]{:S(2)}, u32[]{:S(2)}) %collective-permute-start.15) | collective-permute-done | bytes 196640 | tf_op jit(solution)/shard_map/ppermute | solution.py:19
  114.5 2.0 %collective-permute-start.18 = (f32[5,256]{1,0:T(8,128)S(1)}, f32[5,256]{1,0:T(8,128)S(1)}, u32[]{:S(2)}, u32[]{:S(2)}) collective-permute-start(f32[5,256]{1,0:T(8,128)S(1)} %stack.60), channel_id=1, source_target_pairs={{0,32},{32,64},{64,96},{96,0},{1,33},{33,65},{65,97},{97,1},{2,34}... | collective-permute-start | bytes 15368 | tf_op jit(solution)/shard_map/ppermute | solution.py:19
  120.5 4.5 %collective-permute-start.20 = (bf16[384,384]{1,0:T(8,128)(2,1)S(1)}, bf16[384,384]{1,0:T(8,128)(2,1)S(1)}, u32[]{:S(2)}, u32[]{:S(2)}) collective-permute-start(bf16[384,384]{1,0:T(8,128)(2,1)S(1)} %fusion.9), channel_id=1, source_target_pairs={{0,128},{128,0},{1,129},{129,1},{2,130},{130,2},{3,131},{131,3},{4... | collective-permute-start | bytes 884744 | tf_op jit(solution)/shard_map/ppermute | solution.py:19
  126.6 16.0 %all_to_all.16 = bf16[32,14,384]{2,1,0:T(8,128)(2,1)S(1)} all-to-all(bf16[32,14,384]{2,1,0:T(8,128)(2,1)S(1)} %pad_maximum_fusion), channel_id=1, replica_groups=mesh['group'=2,'row'=4,'zl'=2,'y'=4,'x'=4] {'zl','y','x'}, dimensions={0} | all-to-all | bytes 688128 | tf_op jit(solution)/shard_map/all_to_all | solution.py:392
  142.8 12.7 %all_to_all.17 = bf16[32,12,384]{2,1,0:T(8,128)(2,1)S(1)} all-to-all(bf16[32,12,384]{2,1,0:T(8,128)(2,1)S(1)} %broadcast_in_dim.22), channel_id=1, replica_groups=mesh['group'=2,'row'=4,'zl'=2,'y'=4,'x'=4] {'zl','y','x'}, dimensions={0} | all-to-all | bytes 589824 | tf_op jit(solution)/shard_map/all_to_all | solution.py:396
  155.5 2.8 %collective-permute-start.21 = (bf16[384,384]{1,0:T(8,128)(2,1)S(1)}, bf16[384,384]{1,0:T(8,128)(2,1)S(1)}, u32[]{:S(2)}, u32[]{:S(2)}) collective-permute-start(bf16[384,384]{1,0:T(8,128)(2,1)S(1)} %reshape.119), channel_id=1, source_target_pairs={{0,128},{128,0},{1,129},{129,1},{2,130},{130,2},{3,131},{131,3},{4... | collective-permute-start | bytes 884744 | tf_op jit(solution)/shard_map/ppermute | solution.py:19
  (104 shorter events, 28.3 us)
Async XLA Ops:
  2.4 8.2 %collective-permute-start = (bf16[48,3072]{1,0:T(8,128)(2,1)}, bf16[48,3072]{1,0:T(8,128)(2,1)}, u32[]{:S(2)}, u32[]{:S(2)}) collective-permute-start(bf16[48,3072]{1,0:T(8,128)(2,1)} %shard_map.122), channel_id=1, source_target_pairs={{0,16},{144,128},{1,17},{145,129},{2,18},{146,130},{3,19},{147,131... | collective-permute-start | bytes 884744 | tf_op jit(solution)/shard_map/ppermute | solution.py:295
  10.6 49.6 %collective-permute-start.2 = (bf16[2,576,384]{2,1,0:T(8,128)(2,1)S(1)}, bf16[2,576,384]{2,1,0:T(8,128)(2,1)S(1)}, u32[]{:S(2)}, u32[]{:S(2)}) collective-permute-start(bf16[2,576,384]{2,1,0:T(8,128)(2,1)S(1)} %maximum_maximum_fusion.own), channel_id=1, source_target_pairs={{0,32},{32,64},{64,96},{96,0},{1,33},{33,65},{65,97},{97,1},{2,34}... | collective-permute-start | bytes 2654216 | tf_op jit(solution)/shard_map/ppermute | solution.py:19
  14.0 50.1 %collective-permute-start.1 = (bf16[2,576,384]{2,1,0:T(8,128)(2,1)S(1)}, bf16[2,576,384]{2,1,0:T(8,128)(2,1)}, u32[]{:S(2)}, u32[]{:S(2)}) collective-permute-start(bf16[2,576,384]{2,1,0:T(8,128)(2,1)S(1)} %maximum_maximum_fusion.own), channel_id=1, source_target_pairs={{0,96},{32,0},{64,32},{96,64},{1,97},{33,1},{65,33},{97,65},{2,98}... | collective-permute-start | bytes 2654216 | tf_op jit(solution)/shard_map/ppermute | solution.py:19
  18.1 9.6 %collective-permute-start.5 = (bf16[48,3072]{1,0:T(8,128)(2,1)S(1)}, bf16[48,3072]{1,0:T(8,128)(2,1)S(1)}, u32[]{:S(2)}, u32[]{:S(2)}) collective-permute-start(bf16[48,3072]{1,0:T(8,128)(2,1)S(1)} %broadcast_select_fusion.refs_0_), channel_id=1, source_target_pairs={{0,3},{128,140},{1,0},{129,141},{2,1},{130,142},{3,2},{131,143},{4... | collective-permute-start | bytes 884744 | tf_op jit(solution)/shard_map/ppermute | solution.py:309
  20.9 7.5 %collective-permute-start.6 = (bf16[48,3072]{1,0:T(8,128)(2,1)S(1)}, bf16[48,3072]{1,0:T(8,128)(2,1)S(1)}, u32[]{:S(2)}, u32[]{:S(2)}) collective-permute-start(bf16[48,3072]{1,0:T(8,128)(2,1)S(1)} %broadcast_select_fusion.refs_0_), channel_id=1, source_target_pairs={{0,2},{128,136},{1,3},{129,137},{2,0},{130,138},{3,1},{131,139},{4... | collective-permute-start | bytes 884744 | tf_op jit(solution)/shard_map/ppermute | solution.py:309
  21.2 10.2 %collective-permute-start.7 = (bf16[48,3072]{1,0:T(8,128)(2,1)S(1)}, bf16[48,3072]{1,0:T(8,128)(2,1)S(1)}, u32[]{:S(2)}, u32[]{:S(2)}) collective-permute-start(bf16[48,3072]{1,0:T(8,128)(2,1)S(1)} %broadcast_select_fusion.refs_0_), channel_id=1, source_target_pairs={{0,1},{128,132},{1,2},{129,133},{2,3},{130,134},{3,0},{131,135},{4... | collective-permute-start | bytes 884744 | tf_op jit(solution)/shard_map/ppermute | solution.py:309
  35.7 30.7 %copy-start.12 = (bf16[1536]{0:T(1024)(128)(2,1)S(1)}, bf16[1536]{0:T(1024)(128)(2,1)}, u32[]{:S(2)}) copy-start(bf16[1536]{0:T(1024)(128)(2,1)} %param.14) | copy-start | bytes 9220
  35.7 37.8 %collective-permute-start.8 = (bf16[4,48,3072]{2,1,0:T(8,128)(2,1)S(1)}, bf16[4,48,3072]{2,1,0:T(8,128)(2,1)}, u32[]{:S(2)}, u32[]{:S(2)}) collective-permute-start(bf16[4,48,3072]{2,1,0:T(8,128)(2,1)S(1)} %shard_map.124.refs_0_), channel_id=1, source_target_pairs={{0,12},{128,131},{1,13},{129,128},{2,14},{130,129},{3,15},{131,130... | collective-permute-start | bytes 3538952 | tf_op jit(solution)/shard_map/ppermute | solution.py:309
  38.3 35.7 %collective-permute-start.9 = (bf16[4,48,3072]{2,1,0:T(8,128)(2,1)S(1)}, bf16[4,48,3072]{2,1,0:T(8,128)(2,1)}, u32[]{:S(2)}, u32[]{:S(2)}) collective-permute-start(bf16[4,48,3072]{2,1,0:T(8,128)(2,1)S(1)} %shard_map.124.refs_0_), channel_id=1, source_target_pairs={{0,8},{128,130},{1,9},{129,131},{2,10},{130,128},{3,11},{131,129},... | collective-permute-start | bytes 3538952 | tf_op jit(solution)/shard_map/ppermute | solution.py:309
  38.8 35.3 %collective-permute-start.10 = (bf16[4,48,3072]{2,1,0:T(8,128)(2,1)S(1)}, bf16[4,48,3072]{2,1,0:T(8,128)(2,1)}, u32[]{:S(2)}, u32[]{:S(2)}) collective-permute-start(bf16[4,48,3072]{2,1,0:T(8,128)(2,1)S(1)} %shard_map.124.refs_0_), channel_id=1, source_target_pairs={{0,4},{128,129},{1,5},{129,130},{2,6},{130,131},{3,7},{131,128},{4... | collective-permute-start | bytes 3538952 | tf_op jit(solution)/shard_map/ppermute | solution.py:309
  61.0 14.5 %collective-permute-start.3 = (bf16[576,384]{1,0:T(8,128)(2,1)}, bf16[576,384]{1,0:T(8,128)(2,1)S(1)}, u32[]{:S(2)}, u32[]{:S(2)}) collective-permute-start(bf16[576,384]{1,0:T(8,128)(2,1)} %slice_bitcast_fusion.1), channel_id=1, source_target_pairs={{0,32},{32,64},{64,96},{96,0},{1,33},{33,65},{65,97},{97,1},{2,34}... | collective-permute-start | bytes 1327112 | tf_op jit(solution)/shard_map/ppermute | solution.py:19
  66.0 14.5 %collective-permute-start.4 = (bf16[576,384]{1,0:T(8,128)(2,1)}, bf16[576,384]{1,0:T(8,128)(2,1)}, u32[]{:S(2)}, u32[]{:S(2)}) collective-permute-start(bf16[576,384]{1,0:T(8,128)(2,1)} %slice_bitcast_fusion), channel_id=1, source_target_pairs={{0,96},{32,0},{64,32},{96,64},{1,97},{33,1},{65,33},{97,65},{2,98}... | collective-permute-start | bytes 1327112 | tf_op jit(solution)/shard_map/ppermute | solution.py:19
  73.5 11.3 %collective-permute-start.11 = (bf16[4,48,3072]{2,1,0:T(8,128)(2,1)}, bf16[4,48,3072]{2,1,0:T(8,128)(2,1)S(1)}, u32[]{:S(2)}, u32[]{:S(2)}) collective-permute-start(bf16[4,48,3072]{2,1,0:T(8,128)(2,1)} %collective-permute-done.8.refs_1_), channel_id=1, source_target_pairs={{0,128},{128,0},{1,129},{129,1},{2,130},{130,2},{3,131},{131,3},{4... | collective-permute-start | bytes 3538952 | tf_op jit(solution)/shard_map/ppermute | solution.py:19
  74.0 10.8 %collective-permute-start.12 = (bf16[4,48,3072]{2,1,0:T(8,128)(2,1)}, bf16[4,48,3072]{2,1,0:T(8,128)(2,1)S(1)}, u32[]{:S(2)}, u32[]{:S(2)}) collective-permute-start(bf16[4,48,3072]{2,1,0:T(8,128)(2,1)} %collective-permute-done.9.refs_2_), channel_id=1, source_target_pairs={{0,128},{128,0},{1,129},{129,1},{2,130},{130,2},{3,131},{131,3},{4... | collective-permute-start | bytes 3538952 | tf_op jit(solution)/shard_map/ppermute | solution.py:19
  74.1 10.7 %collective-permute-start.13 = (bf16[4,48,3072]{2,1,0:T(8,128)(2,1)}, bf16[4,48,3072]{2,1,0:T(8,128)(2,1)S(1)}, u32[]{:S(2)}, u32[]{:S(2)}) collective-permute-start(bf16[4,48,3072]{2,1,0:T(8,128)(2,1)} %collective-permute-done.10.refs_3_), channel_id=1, source_target_pairs={{0,128},{128,0},{1,129},{129,1},{2,130},{130,2},{3,131},{131,3},{4... | collective-permute-start | bytes 3538952 | tf_op jit(solution)/shard_map/ppermute | solution.py:19
  84.8 17.2 %copy-start.13 = (bf16[384]{0:T(512)(128)(2,1)S(1)}, bf16[384]{0:T(512)(128)(2,1)}, u32[]{:S(2)}) copy-start(bf16[384]{0:T(512)(128)(2,1)} %param.15) | copy-start | bytes 2308
  95.3 12.3 %collective-permute-start.14 = (bf16[256,384]{1,0:T(8,128)(2,1)S(1)}, bf16[256,384]{1,0:T(8,128)(2,1)S(1)}, u32[]{:S(2)}, u32[]{:S(2)}) collective-permute-start(bf16[256,384]{1,0:T(8,128)(2,1)S(1)} %get-tuple-element.29), channel_id=1, source_target_pairs={{0,64},{32,96},{64,0},{96,32},{1,65},{33,97},{65,1},{97,33},{2,66}... | collective-permute-start | bytes 589832 | tf_op jit(solution)/shard_map/ppermute | solution.py:19
  97.6 14.7 %collective-permute-start.15 = (bf16[256,384]{1,0:T(8,128)(2,1)S(1)}, bf16[256,384]{1,0:T(8,128)(2,1)S(1)}, u32[]{:S(2)}, u32[]{:S(2)}) collective-permute-start(bf16[256,384]{1,0:T(8,128)(2,1)S(1)} %get-tuple-element.30), channel_id=1, source_target_pairs={{0,32},{32,64},{64,96},{96,0},{1,33},{33,65},{65,97},{97,1},{2,34}... | collective-permute-start | bytes 589832 | tf_op jit(solution)/shard_map/ppermute | solution.py:19
  98.7 13.6 %collective-permute-start.16 = (bf16[256,384]{1,0:T(8,128)(2,1)S(1)}, bf16[256,384]{1,0:T(8,128)(2,1)S(1)}, u32[]{:S(2)}, u32[]{:S(2)}) collective-permute-start(bf16[256,384]{1,0:T(8,128)(2,1)S(1)} %get-tuple-element.31), channel_id=1, source_target_pairs={{0,96},{32,0},{64,32},{96,64},{1,97},{33,1},{65,33},{97,65},{2,98}... | collective-permute-start | bytes 589832 | tf_op jit(solution)/shard_map/ppermute | solution.py:19
  112.8 6.5 %collective-permute-start.17 = (f32[5,256]{1,0:T(8,128)S(1)}, f32[5,256]{1,0:T(8,128)S(1)}, u32[]{:S(2)}, u32[]{:S(2)}) collective-permute-start(f32[5,256]{1,0:T(8,128)S(1)} %stack.60), channel_id=1, source_target_pairs={{0,64},{32,96},{64,0},{96,32},{1,65},{33,97},{65,1},{97,33},{2,66}... | collective-permute-start | bytes 15368 | tf_op jit(solution)/shard_map/ppermute | solution.py:19
  114.5 4.8 %collective-permute-start.18 = (f32[5,256]{1,0:T(8,128)S(1)}, f32[5,256]{1,0:T(8,128)S(1)}, u32[]{:S(2)}, u32[]{:S(2)}) collective-permute-start(f32[5,256]{1,0:T(8,128)S(1)} %stack.60), channel_id=1, source_target_pairs={{0,32},{32,64},{64,96},{96,0},{1,33},{33,65},{65,97},{97,1},{2,34}... | collective-permute-start | bytes 15368 | tf_op jit(solution)/shard_map/ppermute | solution.py:19
  116.5 3.4 %collective-permute-start.19 = (f32[5,256]{1,0:T(8,128)S(1)}, f32[5,256]{1,0:T(8,128)S(1)}, u32[]{:S(2)}, u32[]{:S(2)}) collective-permute-start(f32[5,256]{1,0:T(8,128)S(1)} %stack.60), channel_id=1, source_target_pairs={{0,96},{32,0},{64,32},{96,64},{1,97},{33,1},{65,33},{97,65},{2,98}... | collective-permute-start | bytes 15368 | tf_op jit(solution)/shard_map/ppermute | solution.py:19
  120.5 5.7 %collective-permute-start.20 = (bf16[384,384]{1,0:T(8,128)(2,1)S(1)}, bf16[384,384]{1,0:T(8,128)(2,1)S(1)}, u32[]{:S(2)}, u32[]{:S(2)}) collective-permute-start(bf16[384,384]{1,0:T(8,128)(2,1)S(1)} %fusion.9), channel_id=1, source_target_pairs={{0,128},{128,0},{1,129},{129,1},{2,130},{130,2},{3,131},{131,3},{4... | collective-permute-start | bytes 884744 | tf_op jit(solution)/shard_map/ppermute | solution.py:19
  155.5 4.6 %collective-permute-start.21 = (bf16[384,384]{1,0:T(8,128)(2,1)S(1)}, bf16[384,384]{1,0:T(8,128)(2,1)S(1)}, u32[]{:S(2)}, u32[]{:S(2)}) collective-permute-start(bf16[384,384]{1,0:T(8,128)(2,1)S(1)} %reshape.119), channel_id=1, source_target_pairs={{0,128},{128,0},{1,129},{129,1},{2,130},{130,2},{3,131},{131,3},{4... | collective-permute-start | bytes 884744 | tf_op jit(solution)/shard_map/ppermute | solution.py:19
  (13 other events, 58.7 us)

commit v7 on v6

--- a/solution.py
+++ b/solution.py
@@ -345,7 +345,7 @@
     part, *away = branch(place, normed, weights_own, weights_other)
     held = (own, after, before, far_top, far_bottom)
     away, held = lax.optimization_barrier((away, held))
-    got = [shift(away[j - 1], "row", 4, j) for j in (2, 1, 3)]
+    got = [shift(away[j - 1], "row", 4, j) for j in (1, 3, 2)]
     pupils, head = student(place, *held, head_weight)
 
     averaged = part + sum(piece.astype(jnp.float32) for piece in got)

time: 163 us -> 163 us (level)
  waiting for transfers between devices: 50.4 us -> 48 us
  starting transfers between devices: 39.1 us -> 40.9 us
    ppermute x15, waiting for transfers between devices: 37.9 us -> 35.5 us  [shift(): lax.ppermute(value, axis, [(i, (i + by) % size) for i in range(size)])]
    ppermute x15, starting transfers between devices: 30.2 us -> 32 us  [shift(): lax.ppermute(value, axis, [(i, (i + by) % size) for i in range(size)])]
  transfers between devices with their start and end apart: 22 -> 22, of which waited for: 11 -> 10; matrix products, arithmetic and copies ran while one was open for 5% -> 5% of each run, Pallas kernels for 4% -> 4%
where the time goes in v7:
time: 163 us; the launch traced here: 162 us
  waiting for transfers between devices  48 us (29%)
  starting transfers between devices  40.9 us (25%)
  blocking collectives  35.6 us (22%)
  Pallas kernels  18.6 us (11%)
  local copies, waits for them, and re-layouts  10.5 us (6%)
  other arithmetic  4.29 us (3%)
  between operations  3.43 us (2%)
    ppermute x15, waiting for transfers between devices, shift(): lax.ppermute(value, axis, [(i, (i + by) % size) for i in range(size)])  35.5 us
    ppermute x15, starting transfers between devices, shift(): lax.ppermute(value, axis, [(i, (i + by) % size) for i in range(size)])  32 us
    all_to_all x1, blocking collectives, shards(): packet = lax.all_to_all(packet, COL, 0, 0, tiled=True).astype(jnp.float32)  16.2 us
    all_to_all x1, blocking collectives, shards(): lax.all_to_all(jnp.broadcast_to(piece[None], (32, 12, PART)), COL, 0, 0,...  12.7 us
    pallas_call x1, Pallas kernels, branch(): pl.pallas_call(branch_kernel, in_specs=[pl.BlockSpec(memory_space=pltpu.S...  10.5 us
    ppermute x6, waiting for transfers between devices, collect(): pieces.append(lax.ppermute(value, ('group', 'y', 'x'), pairs))  7.97 us
    ppermute x6, starting transfers between devices, collect(): pieces.append(lax.ppermute(value, ('group', 'y', 'x'), pairs))  7.53 us
    all_to_all x1, blocking collectives, shards(): lax.all_to_all(jnp.broadcast_to(line[None], (2,) + line.shape), 'group',...  6.69 us
  transfers between devices with their start and end apart: 22, of which 10 were waited for; matrix products, arithmetic and copies ran while one was open for 5% of the time, Pallas kernels for 4%

profile of v7, /device:TPU:1, one launch (start us, length us, event | category | flops | bytes accessed | tf_op | source)
XLA Modules:
  0.0 162.0 jit_solution(2590405620468015876)
XLA Ops:
  6.1 4.5 %collective-permute-done = bf16[48,3072]{1,0:T(8,128)(2,1)} collective-permute-done((bf16[48,3072]{1,0:T(8,128)(2,1)}, bf16[48,3072]{1,0:T(8,128)(2,1)}, u32[]{:S(2)}, u32[]{:S(2)}) %collective-permute-start) | collective-permute-done | bytes 294944 | tf_op jit(solution)/shard_map/ppermute | solution.py:295
  10.6 3.4 %collective-permute-start.2 = (bf16[2,576,384]{2,1,0:T(8,128)(2,1)S(1)}, bf16[2,576,384]{2,1,0:T(8,128)(2,1)S(1)}, u32[]{:S(2)}, u32[]{:S(2)}) collective-permute-start(bf16[2,576,384]{2,1,0:T(8,128)(2,1)S(1)} %maximum_maximum_fusion.own), channel_id=1, source_target_pairs={{0,32},{32,64},{64,96},{96,0},{1,33},{33,65},{65,97},{97,1},{2,34}... | collective-permute-start | bytes 2654216 | tf_op jit(solution)/shard_map/ppermute | solution.py:19
  14.0 3.0 %collective-permute-start.1 = (bf16[2,576,384]{2,1,0:T(8,128)(2,1)S(1)}, bf16[2,576,384]{2,1,0:T(8,128)(2,1)}, u32[]{:S(2)}, u32[]{:S(2)}) collective-permute-start(bf16[2,576,384]{2,1,0:T(8,128)(2,1)S(1)} %maximum_maximum_fusion.own), channel_id=1, source_target_pairs={{0,96},{32,0},{64,32},{96,64},{1,97},{33,1},{65,33},{97,65},{2,98}... | collective-permute-start | bytes 2654216 | tf_op jit(solution)/shard_map/ppermute | solution.py:19
  18.1 2.8 %collective-permute-start.5 = (bf16[48,3072]{1,0:T(8,128)(2,1)S(1)}, bf16[48,3072]{1,0:T(8,128)(2,1)S(1)}, u32[]{:S(2)}, u32[]{:S(2)}) collective-permute-start(bf16[48,3072]{1,0:T(8,128)(2,1)S(1)} %broadcast_select_fusion.refs_0_), channel_id=1, source_target_pairs={{0,3},{128,140},{1,0},{129,141},{2,1},{130,142},{3,2},{131,143},{4... | collective-permute-start | bytes 884744 | tf_op jit(solution)/shard_map/ppermute | solution.py:309
  22.0 5.7 %collective-permute-done.5.refs_1_ = bf16[48,3072]{1,0:T(8,128)(2,1)S(1)} collective-permute-done((bf16[48,3072]{1,0:T(8,128)(2,1)S(1)}, bf16[48,3072]{1,0:T(8,128)(2,1)S(1)}, u32[]{:S(2)}, u32[]{:S(2)}) %collective-permute-start.5) | collective-permute-done | bytes 294944 | tf_op jit(solution)/shard_map/ppermute | solution.py:309
  29.2 2.3 %collective-permute-done.7.refs_3_ = bf16[48,3072]{1,0:T(8,128)(2,1)S(1)} collective-permute-done((bf16[48,3072]{1,0:T(8,128)(2,1)S(1)}, bf16[48,3072]{1,0:T(8,128)(2,1)S(1)}, u32[]{:S(2)}, u32[]{:S(2)}) %collective-permute-start.7) | collective-permute-done | bytes 294944 | tf_op jit(solution)/shard_map/ppermute | solution.py:309
  35.7 2.6 %collective-permute-start.8 = (bf16[4,48,3072]{2,1,0:T(8,128)(2,1)S(1)}, bf16[4,48,3072]{2,1,0:T(8,128)(2,1)}, u32[]{:S(2)}, u32[]{:S(2)}) collective-permute-start(bf16[4,48,3072]{2,1,0:T(8,128)(2,1)S(1)} %shard_map.124.refs_0_), channel_id=1, source_target_pairs={{0,12},{128,131},{1,13},{129,128},{2,14},{130,129},{3,15},{131,130... | collective-permute-start | bytes 3538952 | tf_op jit(solution)/shard_map/ppermute | solution.py:309
  39.4 20.8 %collective-permute-done.2.before = bf16[2,576,384]{2,1,0:T(8,128)(2,1)S(1)} collective-permute-done((bf16[2,576,384]{2,1,0:T(8,128)(2,1)S(1)}, bf16[2,576,384]{2,1,0:T(8,128)(2,1)S(1)}, u32[]{:S(2)}, u32[]{:S(2)}) %collective-permute-start.2) | collective-permute-done | bytes 884768 | tf_op jit(solution)/shard_map/ppermute | solution.py:19
  61.0 3.1 %collective-permute-start.3 = (bf16[576,384]{1,0:T(8,128)(2,1)}, bf16[576,384]{1,0:T(8,128)(2,1)S(1)}, u32[]{:S(2)}, u32[]{:S(2)}) collective-permute-start(bf16[576,384]{1,0:T(8,128)(2,1)} %slice_bitcast_fusion.1), channel_id=1, source_target_pairs={{0,32},{32,64},{64,96},{96,0},{1,33},{33,65},{65,97},{97,1},{2,34}... | collective-permute-start | bytes 1327112 | tf_op jit(solution)/shard_map/ppermute | solution.py:19
  64.2 1.8 %slice_bitcast_fusion = bf16[576,384]{1,0:T(8,128)(2,1)} fusion(bf16[2,576,384]{2,1,0:T(8,128)(2,1)} %collective-permute-done.1.after), kind=kLoop, calls=%fused_computation.13 | loop fusion | bytes 884736 | tf_op jit(solution)/shard_map/squeeze | solution.py:341
  66.7 6.7 %all_to_all.15 = bf16[2,4,48,3072]{3,2,1,0:T(8,128)(2,1)S(1)} all-to-all(bf16[2,4,48,3072]{3,2,1,0:T(8,128)(2,1)S(1)} %broadcast_in_dim.14), channel_id=1, replica_groups=mesh['group'=2,'row'=4,'zl'=2,'y'=4,'x'=4] {'group'}, dimensions={0} | all-to-all | bytes 4718592 | tf_op jit(solution)/shard_map/all_to_all | solution.py:314
  75.5 4.9 %collective-permute-done.4.far_bottom = bf16[576,384]{1,0:T(8,128)(2,1)} collective-permute-done((bf16[576,384]{1,0:T(8,128)(2,1)}, bf16[576,384]{1,0:T(8,128)(2,1)}, u32[]{:S(2)}, u32[]{:S(2)}) %collective-permute-start.4) | collective-permute-done | bytes 442400 | tf_op jit(solution)/shard_map/ppermute | solution.py:19
  80.5 4.3 %shard_map.123.normed = bf16[1024,1536]{1,0:T(8,128)(2,1)S(1)} custom-call(s32[4]{0:T(128)S(1)} %pad_add_fusion.place, bf16[2,576,384]{2,1,0:T(8,128)(2,1)S(1)} %maximum_maximum_fusion.own, bf16[2,576,384]{2,1,0:T(8,128)(2,1)} %collective-permute-done.1.after, bf16[2,576,384]{2,1,0:T(8,128)(2,1)S(1)} %collective-permute-done.2.before, ...), custom_call_target="tpu_custom_call" | custom-call | flops 30000001024 | bytes 6291456 | tf_op jit(solution)/shard_map/pallas_call | solution.py:42
  84.8 10.5 %shard_map.125 = (f32[256,384]{1,0:T(8,128)S(1)}, bf16[256,384]{1,0:T(8,128)(2,1)S(1)}, bf16[256,384]{1,0:T(8,128)(2,1)S(1)}, bf16[256,384]{1,0:T(8,128)(2,1)S(1)}) custom-call(s32[4]{0:T(128)S(1)} %pad_add_fusion.place, bf16[1024,1536]{1,0:T(8,128)(2,1)S(1)} %shard_map.123.normed, bf16[4,48,3072]{2,1,0:T(8,128)(2,1)S(1)} %shard_map.124.refs_0_, ...), custom_call_target="tpu_custom_call" | custom-call | flops 6442450944 | bytes 10485760 | tf_op jit(solution)/shard_map/pallas_call | solution.py:154
  95.3 3.3 %collective-permute-start.14 = (bf16[256,384]{1,0:T(8,128)(2,1)S(1)}, bf16[256,384]{1,0:T(8,128)(2,1)S(1)}, u32[]{:S(2)}, u32[]{:S(2)}) collective-permute-start(bf16[256,384]{1,0:T(8,128)(2,1)S(1)} %get-tuple-element.29), channel_id=1, source_target_pairs={{0,32},{32,64},{64,96},{96,0},{1,33},{33,65},{65,97},{97,1},{2,34}... | collective-permute-start | bytes 589832 | tf_op jit(solution)/shard_map/ppermute | solution.py:19
  99.0 3.1 %collective-permute-start.16 = (bf16[256,384]{1,0:T(8,128)(2,1)S(1)}, bf16[256,384]{1,0:T(8,128)(2,1)S(1)}, u32[]{:S(2)}, u32[]{:S(2)}) collective-permute-start(bf16[256,384]{1,0:T(8,128)(2,1)S(1)} %get-tuple-element.31), channel_id=1, source_target_pairs={{0,64},{32,96},{64,0},{96,32},{1,65},{33,97},{65,1},{97,33},{2,66}... | collective-permute-start | bytes 589832 | tf_op jit(solution)/shard_map/ppermute | solution.py:19
  103.5 1.9 %collective-permute-done.15 = bf16[256,384]{1,0:T(8,128)(2,1)S(1)} collective-permute-done((bf16[256,384]{1,0:T(8,128)(2,1)S(1)}, bf16[256,384]{1,0:T(8,128)(2,1)S(1)}, u32[]{:S(2)}, u32[]{:S(2)}) %collective-permute-start.15) | collective-permute-done | bytes 196640 | tf_op jit(solution)/shard_map/ppermute | solution.py:19
  105.5 5.3 %collective-permute-done.16 = bf16[256,384]{1,0:T(8,128)(2,1)S(1)} collective-permute-done((bf16[256,384]{1,0:T(8,128)(2,1)S(1)}, bf16[256,384]{1,0:T(8,128)(2,1)S(1)}, u32[]{:S(2)}, u32[]{:S(2)}) %collective-permute-start.16) | collective-permute-done | bytes 196640 | tf_op jit(solution)/shard_map/ppermute | solution.py:19
  111.1 3.3 %collective-permute-start.17 = (f32[5,256]{1,0:T(8,128)S(1)}, f32[5,256]{1,0:T(8,128)S(1)}, u32[]{:S(2)}, u32[]{:S(2)}) collective-permute-start(f32[5,256]{1,0:T(8,128)S(1)} %stack.60), channel_id=1, source_target_pairs={{0,64},{32,96},{64,0},{96,32},{1,65},{33,97},{65,1},{97,33},{2,66}... | collective-permute-start | bytes 15368 | tf_op jit(solution)/shard_map/ppermute | solution.py:19
  114.5 3.6 %collective-permute-start.19 = (f32[5,256]{1,0:T(8,128)S(1)}, f32[5,256]{1,0:T(8,128)S(1)}, u32[]{:S(2)}, u32[]{:S(2)}) collective-permute-start(f32[5,256]{1,0:T(8,128)S(1)} %stack.60), channel_id=1, source_target_pairs={{0,96},{32,0},{64,32},{96,64},{1,97},{33,1},{65,33},{97,65},{2,98}... | collective-permute-start | bytes 15368 | tf_op jit(solution)/shard_map/ppermute | solution.py:19
  119.8 4.6 %collective-permute-start.20 = (bf16[384,384]{1,0:T(8,128)(2,1)S(1)}, bf16[384,384]{1,0:T(8,128)(2,1)S(1)}, u32[]{:S(2)}, u32[]{:S(2)}) collective-permute-start(bf16[384,384]{1,0:T(8,128)(2,1)S(1)} %fusion.9), channel_id=1, source_target_pairs={{0,128},{128,0},{1,129},{129,1},{2,130},{130,2},{3,131},{131,3},{4... | collective-permute-start | bytes 884744 | tf_op jit(solution)/shard_map/ppermute | solution.py:19
  125.9 16.2 %all_to_all.16 = bf16[32,14,384]{2,1,0:T(8,128)(2,1)S(1)} all-to-all(bf16[32,14,384]{2,1,0:T(8,128)(2,1)S(1)} %pad_maximum_fusion), channel_id=1, replica_groups=mesh['group'=2,'row'=4,'zl'=2,'y'=4,'x'=4] {'zl','y','x'}, dimensions={0} | all-to-all | bytes 688128 | tf_op jit(solution)/shard_map/all_to_all | solution.py:392
  142.3 12.7 %all_to_all.17 = bf16[32,12,384]{2,1,0:T(8,128)(2,1)S(1)} all-to-all(bf16[32,12,384]{2,1,0:T(8,128)(2,1)S(1)} %broadcast_in_dim.22), channel_id=1, replica_groups=mesh['group'=2,'row'=4,'zl'=2,'y'=4,'x'=4] {'zl','y','x'}, dimensions={0} | all-to-all | bytes 589824 | tf_op jit(solution)/shard_map/all_to_all | solution.py:396
  155.1 2.8 %collective-permute-start.21 = (bf16[384,384]{1,0:T(8,128)(2,1)S(1)}, bf16[384,384]{1,0:T(8,128)(2,1)S(1)}, u32[]{:S(2)}, u32[]{:S(2)}) collective-permute-start(bf16[384,384]{1,0:T(8,128)(2,1)S(1)} %reshape.119), channel_id=1, source_target_pairs={{0,128},{128,0},{1,129},{129,1},{2,130},{130,2},{3,131},{131,3},{4... | collective-permute-start | bytes 884744 | tf_op jit(solution)/shard_map/ppermute | solution.py:19
  (104 shorter events, 25.2 us)
Async XLA Ops:
  2.4 8.2 %collective-permute-start = (bf16[48,3072]{1,0:T(8,128)(2,1)}, bf16[48,3072]{1,0:T(8,128)(2,1)}, u32[]{:S(2)}, u32[]{:S(2)}) collective-permute-start(bf16[48,3072]{1,0:T(8,128)(2,1)} %shard_map.122), channel_id=1, source_target_pairs={{0,16},{144,128},{1,17},{145,129},{2,18},{146,130},{3,19},{147,131... | collective-permute-start | bytes 884744 | tf_op jit(solution)/shard_map/ppermute | solution.py:295
  10.6 49.6 %collective-permute-start.2 = (bf16[2,576,384]{2,1,0:T(8,128)(2,1)S(1)}, bf16[2,576,384]{2,1,0:T(8,128)(2,1)S(1)}, u32[]{:S(2)}, u32[]{:S(2)}) collective-permute-start(bf16[2,576,384]{2,1,0:T(8,128)(2,1)S(1)} %maximum_maximum_fusion.own), channel_id=1, source_target_pairs={{0,32},{32,64},{64,96},{96,0},{1,33},{33,65},{65,97},{97,1},{2,34}... | collective-permute-start | bytes 2654216 | tf_op jit(solution)/shard_map/ppermute | solution.py:19
  14.0 50.1 %collective-permute-start.1 = (bf16[2,576,384]{2,1,0:T(8,128)(2,1)S(1)}, bf16[2,576,384]{2,1,0:T(8,128)(2,1)}, u32[]{:S(2)}, u32[]{:S(2)}) collective-permute-start(bf16[2,576,384]{2,1,0:T(8,128)(2,1)S(1)} %maximum_maximum_fusion.own), channel_id=1, source_target_pairs={{0,96},{32,0},{64,32},{96,64},{1,97},{33,1},{65,33},{97,65},{2,98}... | collective-permute-start | bytes 2654216 | tf_op jit(solution)/shard_map/ppermute | solution.py:19
  18.1 9.6 %collective-permute-start.5 = (bf16[48,3072]{1,0:T(8,128)(2,1)S(1)}, bf16[48,3072]{1,0:T(8,128)(2,1)S(1)}, u32[]{:S(2)}, u32[]{:S(2)}) collective-permute-start(bf16[48,3072]{1,0:T(8,128)(2,1)S(1)} %broadcast_select_fusion.refs_0_), channel_id=1, source_target_pairs={{0,3},{128,140},{1,0},{129,141},{2,1},{130,142},{3,2},{131,143},{4... | collective-permute-start | bytes 884744 | tf_op jit(solution)/shard_map/ppermute | solution.py:309
  20.9 7.5 %collective-permute-start.6 = (bf16[48,3072]{1,0:T(8,128)(2,1)S(1)}, bf16[48,3072]{1,0:T(8,128)(2,1)S(1)}, u32[]{:S(2)}, u32[]{:S(2)}) collective-permute-start(bf16[48,3072]{1,0:T(8,128)(2,1)S(1)} %broadcast_select_fusion.refs_0_), channel_id=1, source_target_pairs={{0,2},{128,136},{1,3},{129,137},{2,0},{130,138},{3,1},{131,139},{4... | collective-permute-start | bytes 884744 | tf_op jit(solution)/shard_map/ppermute | solution.py:309
  21.2 10.2 %collective-permute-start.7 = (bf16[48,3072]{1,0:T(8,128)(2,1)S(1)}, bf16[48,3072]{1,0:T(8,128)(2,1)S(1)}, u32[]{:S(2)}, u32[]{:S(2)}) collective-permute-start(bf16[48,3072]{1,0:T(8,128)(2,1)S(1)} %broadcast_select_fusion.refs_0_), channel_id=1, source_target_pairs={{0,1},{128,132},{1,2},{129,133},{2,3},{130,134},{3,0},{131,135},{4... | collective-permute-start | bytes 884744 | tf_op jit(solution)/shard_map/ppermute | solution.py:309
  35.7 30.7 %copy-start.12 = (bf16[1536]{0:T(1024)(128)(2,1)S(1)}, bf16[1536]{0:T(1024)(128)(2,1)}, u32[]{:S(2)}) copy-start(bf16[1536]{0:T(1024)(128)(2,1)} %param.14) | copy-start | bytes 9220
  35.7 37.8 %collective-permute-start.8 = (bf16[4,48,3072]{2,1,0:T(8,128)(2,1)S(1)}, bf16[4,48,3072]{2,1,0:T(8,128)(2,1)}, u32[]{:S(2)}, u32[]{:S(2)}) collective-permute-start(bf16[4,48,3072]{2,1,0:T(8,128)(2,1)S(1)} %shard_map.124.refs_0_), channel_id=1, source_target_pairs={{0,12},{128,131},{1,13},{129,128},{2,14},{130,129},{3,15},{131,130... | collective-permute-start | bytes 3538952 | tf_op jit(solution)/shard_map/ppermute | solution.py:309
  38.3 35.7 %collective-permute-start.9 = (bf16[4,48,3072]{2,1,0:T(8,128)(2,1)S(1)}, bf16[4,48,3072]{2,1,0:T(8,128)(2,1)}, u32[]{:S(2)}, u32[]{:S(2)}) collective-permute-start(bf16[4,48,3072]{2,1,0:T(8,128)(2,1)S(1)} %shard_map.124.refs_0_), channel_id=1, source_target_pairs={{0,8},{128,130},{1,9},{129,131},{2,10},{130,128},{3,11},{131,129},... | collective-permute-start | bytes 3538952 | tf_op jit(solution)/shard_map/ppermute | solution.py:309
  38.8 35.3 %collective-permute-start.10 = (bf16[4,48,3072]{2,1,0:T(8,128)(2,1)S(1)}, bf16[4,48,3072]{2,1,0:T(8,128)(2,1)}, u32[]{:S(2)}, u32[]{:S(2)}) collective-permute-start(bf16[4,48,3072]{2,1,0:T(8,128)(2,1)S(1)} %shard_map.124.refs_0_), channel_id=1, source_target_pairs={{0,4},{128,129},{1,5},{129,130},{2,6},{130,131},{3,7},{131,128},{4... | collective-permute-start | bytes 3538952 | tf_op jit(solution)/shard_map/ppermute | solution.py:309
  61.0 14.5 %collective-permute-start.3 = (bf16[576,384]{1,0:T(8,128)(2,1)}, bf16[576,384]{1,0:T(8,128)(2,1)S(1)}, u32[]{:S(2)}, u32[]{:S(2)}) collective-permute-start(bf16[576,384]{1,0:T(8,128)(2,1)} %slice_bitcast_fusion.1), channel_id=1, source_target_pairs={{0,32},{32,64},{64,96},{96,0},{1,33},{33,65},{65,97},{97,1},{2,34}... | collective-permute-start | bytes 1327112 | tf_op jit(solution)/shard_map/ppermute | solution.py:19
  66.0 14.5 %collective-permute-start.4 = (bf16[576,384]{1,0:T(8,128)(2,1)}, bf16[576,384]{1,0:T(8,128)(2,1)}, u32[]{:S(2)}, u32[]{:S(2)}) collective-permute-start(bf16[576,384]{1,0:T(8,128)(2,1)} %slice_bitcast_fusion), channel_id=1, source_target_pairs={{0,96},{32,0},{64,32},{96,64},{1,97},{33,1},{65,33},{97,65},{2,98}... | collective-permute-start | bytes 1327112 | tf_op jit(solution)/shard_map/ppermute | solution.py:19
  73.5 11.3 %collective-permute-start.11 = (bf16[4,48,3072]{2,1,0:T(8,128)(2,1)}, bf16[4,48,3072]{2,1,0:T(8,128)(2,1)S(1)}, u32[]{:S(2)}, u32[]{:S(2)}) collective-permute-start(bf16[4,48,3072]{2,1,0:T(8,128)(2,1)} %collective-permute-done.8.refs_1_), channel_id=1, source_target_pairs={{0,128},{128,0},{1,129},{129,1},{2,130},{130,2},{3,131},{131,3},{4... | collective-permute-start | bytes 3538952 | tf_op jit(solution)/shard_map/ppermute | solution.py:19
  74.0 10.8 %collective-permute-start.12 = (bf16[4,48,3072]{2,1,0:T(8,128)(2,1)}, bf16[4,48,3072]{2,1,0:T(8,128)(2,1)S(1)}, u32[]{:S(2)}, u32[]{:S(2)}) collective-permute-start(bf16[4,48,3072]{2,1,0:T(8,128)(2,1)} %collective-permute-done.9.refs_2_), channel_id=1, source_target_pairs={{0,128},{128,0},{1,129},{129,1},{2,130},{130,2},{3,131},{131,3},{4... | collective-permute-start | bytes 3538952 | tf_op jit(solution)/shard_map/ppermute | solution.py:19
  74.1 10.7 %collective-permute-start.13 = (bf16[4,48,3072]{2,1,0:T(8,128)(2,1)}, bf16[4,48,3072]{2,1,0:T(8,128)(2,1)S(1)}, u32[]{:S(2)}, u32[]{:S(2)}) collective-permute-start(bf16[4,48,3072]{2,1,0:T(8,128)(2,1)} %collective-permute-done.10.refs_3_), channel_id=1, source_target_pairs={{0,128},{128,0},{1,129},{129,1},{2,130},{130,2},{3,131},{131,3},{4... | collective-permute-start | bytes 3538952 | tf_op jit(solution)/shard_map/ppermute | solution.py:19
  84.8 17.3 %copy-start.13 = (bf16[384]{0:T(512)(128)(2,1)S(1)}, bf16[384]{0:T(512)(128)(2,1)}, u32[]{:S(2)}) copy-start(bf16[384]{0:T(512)(128)(2,1)} %param.15) | copy-start | bytes 2308
  95.3 8.2 %collective-permute-start.14 = (bf16[256,384]{1,0:T(8,128)(2,1)S(1)}, bf16[256,384]{1,0:T(8,128)(2,1)S(1)}, u32[]{:S(2)}, u32[]{:S(2)}) collective-permute-start(bf16[256,384]{1,0:T(8,128)(2,1)S(1)} %get-tuple-element.29), channel_id=1, source_target_pairs={{0,32},{32,64},{64,96},{96,0},{1,33},{33,65},{65,97},{97,1},{2,34}... | collective-permute-start | bytes 589832 | tf_op jit(solution)/shard_map/ppermute | solution.py:19
  98.6 6.8 %collective-permute-start.15 = (bf16[256,384]{1,0:T(8,128)(2,1)S(1)}, bf16[256,384]{1,0:T(8,128)(2,1)S(1)}, u32[]{:S(2)}, u32[]{:S(2)}) collective-permute-start(bf16[256,384]{1,0:T(8,128)(2,1)S(1)} %get-tuple-element.30), channel_id=1, source_target_pairs={{0,96},{32,0},{64,32},{96,64},{1,97},{33,1},{65,33},{97,65},{2,98}... | collective-permute-start | bytes 589832 | tf_op jit(solution)/shard_map/ppermute | solution.py:19
  99.0 11.8 %collective-permute-start.16 = (bf16[256,384]{1,0:T(8,128)(2,1)S(1)}, bf16[256,384]{1,0:T(8,128)(2,1)S(1)}, u32[]{:S(2)}, u32[]{:S(2)}) collective-permute-start(bf16[256,384]{1,0:T(8,128)(2,1)S(1)} %get-tuple-element.31), channel_id=1, source_target_pairs={{0,64},{32,96},{64,0},{96,32},{1,65},{33,97},{65,1},{97,33},{2,66}... | collective-permute-start | bytes 589832 | tf_op jit(solution)/shard_map/ppermute | solution.py:19
  111.1 6.9 %collective-permute-start.17 = (f32[5,256]{1,0:T(8,128)S(1)}, f32[5,256]{1,0:T(8,128)S(1)}, u32[]{:S(2)}, u32[]{:S(2)}) collective-permute-start(f32[5,256]{1,0:T(8,128)S(1)} %stack.60), channel_id=1, source_target_pairs={{0,64},{32,96},{64,0},{96,32},{1,65},{33,97},{65,1},{97,33},{2,66}... | collective-permute-start | bytes 15368 | tf_op jit(solution)/shard_map/ppermute | solution.py:19
  114.5 4.6 %collective-permute-start.18 = (f32[5,256]{1,0:T(8,128)S(1)}, f32[5,256]{1,0:T(8,128)S(1)}, u32[]{:S(2)}, u32[]{:S(2)}) collective-permute-start(f32[5,256]{1,0:T(8,128)S(1)} %stack.60), channel_id=1, source_target_pairs={{0,32},{32,64},{64,96},{96,0},{1,33},{33,65},{65,97},{97,1},{2,34}... | collective-permute-start | bytes 15368 | tf_op jit(solution)/shard_map/ppermute | solution.py:19
  114.5 4.6 %collective-permute-start.19 = (f32[5,256]{1,0:T(8,128)S(1)}, f32[5,256]{1,0:T(8,128)S(1)}, u32[]{:S(2)}, u32[]{:S(2)}) collective-permute-start(f32[5,256]{1,0:T(8,128)S(1)} %stack.60), channel_id=1, source_target_pairs={{0,96},{32,0},{64,32},{96,64},{1,97},{33,1},{65,33},{97,65},{2,98}... | collective-permute-start | bytes 15368 | tf_op jit(solution)/shard_map/ppermute | solution.py:19
  119.8 5.8 %collective-permute-start.20 = (bf16[384,384]{1,0:T(8,128)(2,1)S(1)}, bf16[384,384]{1,0:T(8,128)(2,1)S(1)}, u32[]{:S(2)}, u32[]{:S(2)}) collective-permute-start(bf16[384,384]{1,0:T(8,128)(2,1)S(1)} %fusion.9), channel_id=1, source_target_pairs={{0,128},{128,0},{1,129},{129,1},{2,130},{130,2},{3,131},{131,3},{4... | collective-permute-start | bytes 884744 | tf_op jit(solution)/shard_map/ppermute | solution.py:19
  155.1 4.6 %collective-permute-start.21 = (bf16[384,384]{1,0:T(8,128)(2,1)S(1)}, bf16[384,384]{1,0:T(8,128)(2,1)S(1)}, u32[]{:S(2)}, u32[]{:S(2)}) collective-permute-start(bf16[384,384]{1,0:T(8,128)(2,1)S(1)} %reshape.119), channel_id=1, source_target_pairs={{0,128},{128,0},{1,129},{129,1},{2,130},{130,2},{3,131},{131,3},{4... | collective-permute-start | bytes 884744 | tf_op jit(solution)/shard_map/ppermute | solution.py:19
  (13 other events, 57.2 us)
